TPU v7x, 32 devices: a whole 2x2x4 slice. The times are simulated.
32 devices in a mesh: dp: 16 (over z, y, x), mp: 2 (over core).
Axes of the slice: x: 2, y: 2, z: 4, core: 2. Of those that a mesh axis runs over, the one named last changes fastest.
Arguments:
- context: bfloat16 [1536, 1024], P('dp'), may hold values from -6 to 6
- codes: int32 [1536, 3, 2], P('dp'), may hold values from 0 to 2047
- delays: int32 [1536], P('dp'), may hold values from 1 to 2
- counts: int32 [1536], P('dp'), may hold values from 0 to 2, as said below
- w_attn_in: float32 [2, 1024, 3, 1024], P(None, 'dp', None, 'mp'), may hold values from -0.1875 to 0.1875
- w_attn_out: float32 [2, 1024, 1024], P(None, 'mp', 'dp'), may hold values from -0.25 to 0.25
- w_gate_up: float32 [2, 1024, 2, 2816], P(None, 'dp', None, 'mp'), may hold values from -0.1875 to 0.1875
- w_down: float32 [2, 2816, 1024], P(None, 'mp', 'dp'), may hold values from -0.109375 to 0.109375
- w_head: float32 [2, 1024, 2048], P(None, 'dp', 'mp'), may hold values from -0.375 to 0.375
- embed_table: float32 [1, 2048, 1024], P(None, 'mp', 'dp'), may hold values from -6 to 6
- norm_gains: float32 [2, 3, 1024], P(None, None, 'dp'), may hold values from 0.5 to 1.5
- first_attn_in: float32 [2, 1024, 3, 1024], P(None, 'dp', None, 'mp'), may hold values from -2.3841858e-06 to 2.3841858e-06
- first_attn_out: float32 [2, 1024, 1024], P(None, 'mp', 'dp'), may hold values from -2.3841858e-06 to 2.3841858e-06
- first_gate_up: float32 [2, 1024, 2, 2816], P(None, 'dp', None, 'mp'), may hold values from -2.3841858e-06 to 2.3841858e-06
- first_down: float32 [2, 2816, 1024], P(None, 'mp', 'dp'), may hold values from -2.3841858e-06 to 2.3841858e-06
- first_head: float32 [2, 1024, 2048], P(None, 'dp', 'mp'), may hold values from -2.3841858e-06 to 2.3841858e-06
- first_embed: float32 [1, 2048, 1024], P(None, 'mp', 'dp'), may hold values from -2.3841858e-07 to 2.3841858e-07
- first_gains: float32 [2, 3, 1024], P(None, None, 'dp'), may hold values from -7.6293945e-06 to 7.6293945e-06
- second_attn_in: float32 [2, 1024, 3, 1024], P(None, 'dp', None, 'mp'), may hold values from 6.252401e-13 to 2.5009604e-12
- second_attn_out: float32 [2, 1024, 1024], P(None, 'mp', 'dp'), may hold values from 6.252401e-13 to 2.5009604e-12
- second_gate_up: float32 [2, 1024, 2, 2816], P(None, 'dp', None, 'mp'), may hold values from 6.252401e-13 to 2.5009604e-12
- second_down: float32 [2, 2816, 1024], P(None, 'mp', 'dp'), may hold values from 6.252401e-13 to 2.5009604e-12
- second_head: float32 [2, 1024, 2048], P(None, 'dp', 'mp'), may hold values from 6.252401e-13 to 2.5009604e-12
- second_embed: float32 [1, 2048, 1024], P(None, 'mp', 'dp'), may hold values from 6.252401e-15 to 2.5009603e-14
- second_gains: float32 [2, 3, 1024], P(None, None, 'dp'), may hold values from 6.252401e-12 to 2.5009604e-11
Outputs:
- next_attn_in: float32 [2, 1024, 3, 1024], P(None, 'dp', None, 'mp')
- next_attn_out: float32 [2, 1024, 1024], P(None, 'mp', 'dp')
- next_gate_up: float32 [2, 1024, 2, 2816], P(None, 'dp', None, 'mp')
- next_down: float32 [2, 2816, 1024], P(None, 'mp', 'dp')
- next_head: float32 [2, 1024, 2048], P(None, 'dp', 'mp')
- next_embed: float32 [1, 2048, 1024], P(None, 'mp', 'dp')
- next_gains: float32 [2, 3, 1024], P(None, None, 'dp')
- next_first_attn_in: float32 [2, 1024, 3, 1024], P(None, 'dp', None, 'mp')
- next_first_attn_out: float32 [2, 1024, 1024], P(None, 'mp', 'dp')
- next_first_gate_up: float32 [2, 1024, 2, 2816], P(None, 'dp', None, 'mp')
- next_first_down: float32 [2, 2816, 1024], P(None, 'mp', 'dp')
- next_first_head: float32 [2, 1024, 2048], P(None, 'dp', 'mp')
- next_first_embed: float32 [1, 2048, 1024], P(None, 'mp', 'dp')
- next_first_gains: float32 [2, 3, 1024], P(None, None, 'dp')
- next_second_attn_in: float32 [2, 1024, 3, 1024], P(None, 'dp', None, 'mp')
- next_second_attn_out: float32 [2, 1024, 1024], P(None, 'mp', 'dp')
- next_second_gate_up: float32 [2, 1024, 2, 2816], P(None, 'dp', None, 'mp')
- next_second_down: float32 [2, 2816, 1024], P(None, 'mp', 'dp')
- next_second_head: float32 [2, 1024, 2048], P(None, 'dp', 'mp')
- next_second_embed: float32 [1, 2048, 1024], P(None, 'mp', 'dp')
- next_second_gains: float32 [2, 3, 1024], P(None, None, 'dp')
- loss: float32 [], replicated
- grad_norm: float32 [], replicated
Inputs may be any that keep to these rules, and one draw needn't show every extreme that they name: Positions 0 to counts - 1 of a frame count in the loss.
All inputs are finite; a program needn't handle non-finite values.
Results may differ from a plain program's by a relative error of at most 0.012.
Values may be sent and summed in bfloat16 or wider, within the bound.
No kernel may reach another device: no remote copies, remote signals or barrier semaphores. Data moves between devices by JAX's collectives and lax.ppermute only.
A program may use at most 256 MiB of HBM per device.

v0:
```python
import jax
import jax.numpy as jnp
from jax import lax
from jax.sharding import PartitionSpec as P

HEAD_DIM = 64
MICRO = 2


NORM_EPS = 1e-05
CLIP_NORM = 0.02
BETA_ONE = 0.9
BETA_TWO = 0.95
BIAS_ONE = 1.0 - 0.9**10
BIAS_TWO = 1.0 - 0.95**10
ADAM_EPS = 1e-08
DECAY = 0.1
RATE_MATRIX = 0.03
RATE_TABLE = 0.5


def rms_norm(inputs, gain_vec):
    return (
        inputs * lax.rsqrt(jnp.mean(inputs * inputs, axis=-1, keepdims=True) + NORM_EPS) * gain_vec
    )


def norm_back(inputs, gain_vec, upstream):
    _, pullback = jax.vjp(rms_norm, inputs, gain_vec)
    grad_in, grad_gain = pullback(upstream)
    return (grad_in, grad_gain[:, 0, :])


def attend(queries, key_vecs, values):
    scores = (
        jnp.einsum("kfhd,jfhd->fhkj", queries, key_vecs, precision=lax.Precision.HIGHEST) * 0.125
    )
    num_pos = queries.shape[0]
    causal = lax.broadcasted_iota(jnp.int32, (num_pos, num_pos), 0) >= lax.broadcasted_iota(
        jnp.int32, (num_pos, num_pos), 1
    )
    scores = jnp.where(causal, scores, -1e30)
    probs = jax.nn.softmax(scores, axis=-1)
    mixture = jnp.einsum("fhkj,jfhd->kfhd", probs, values, precision=lax.Precision.HIGHEST)
    return mixture.reshape(mixture.shape[0], mixture.shape[1], -1)


def pick_targets(codes, delays):
    window = lax.broadcasted_iota(jnp.int32, (1, codes.shape[1], 1), 1)
    delayed = jnp.sum(jnp.where(window == delays[:, None, None], codes, 0), axis=1)
    position = lax.broadcasted_iota(jnp.int32, delayed.shape, 1)
    return jnp.where(position == 0, codes[:, 0, :], delayed)


def model_sum(pieces):
    return lax.psum(pieces, "mp")


def fetch(low_params):
    return (
        lax.all_gather(low_params[0], "dp", axis=1, tiled=True),
        lax.all_gather(low_params[1], "dp", axis=2, tiled=True),
        lax.all_gather(low_params[2], "dp", axis=1, tiled=True),
        lax.all_gather(low_params[3], "dp", axis=2, tiled=True),
        lax.all_gather(low_params[4], "dp", axis=1, tiled=True),
        lax.all_gather(low_params[5], "dp", axis=2, tiled=True),
        lax.all_gather(low_params[6], "dp", axis=2, tiled=True),
    )


def reduce_grads(grads):
    return (
        lax.psum_scatter(grads[0], "dp", scatter_dimension=1, tiled=True),
        lax.psum_scatter(grads[1], "dp", scatter_dimension=2, tiled=True),
        lax.psum_scatter(grads[2], "dp", scatter_dimension=1, tiled=True),
        lax.psum_scatter(grads[3], "dp", scatter_dimension=2, tiled=True),
        lax.psum_scatter(grads[4], "dp", scatter_dimension=1, tiled=True),
        lax.psum_scatter(grads[5], "dp", scatter_dimension=2, tiled=True),
        lax.psum_scatter(grads[6], "dp", scatter_dimension=2, tiled=True),
    )


def forward(weights, context, targets, loss_mask, vocab_start):
    w_attn_in, w_attn_out, w_gate_up, w_down, w_head, embed_table, norm_gains = weights
    gain_all = norm_gains.astype(jnp.float32)
    vocab_local = w_head.shape[2]
    local_ids = targets.T - vocab_start
    vocab_iota = lax.broadcasted_iota(jnp.int32, (1, 1, vocab_local), 2)
    picks = local_ids[:, :, None] == vocab_iota
    table_hot = picks[:-1].astype(jnp.bfloat16)
    looked = model_sum(
        jnp.einsum("kfv,kvd->kfd", table_hot, embed_table, preferred_element_type=jnp.float32)
    )
    stream = jnp.concatenate([context.astype(jnp.float32)[None], looked], axis=0)
    attn_low = rms_norm(stream, gain_all[:, 0:1, :]).astype(jnp.bfloat16)
    qkv = jnp.einsum(
        "kfd,kdce->kfce", attn_low, w_attn_in, preferred_element_type=jnp.float32
    ).astype(jnp.bfloat16)
    head_shape = qkv.shape[:2] + (qkv.shape[3] // HEAD_DIM, HEAD_DIM)
    queries = qkv[:, :, 0].astype(jnp.float32).reshape(head_shape)
    key_vecs = qkv[:, :, 1].astype(jnp.float32).reshape(head_shape)
    values = qkv[:, :, 2].astype(jnp.float32).reshape(head_shape)
    attended = attend(queries, key_vecs, values).astype(jnp.bfloat16)
    residual = stream + model_sum(
        jnp.einsum("kfi,kio->kfo", attended, w_attn_out, preferred_element_type=jnp.float32)
    )
    ffn_low = rms_norm(residual, gain_all[:, 1:2, :]).astype(jnp.bfloat16)
    gate_up = jnp.einsum("kfd,kdch->kfch", ffn_low, w_gate_up, preferred_element_type=jnp.float32)
    hidden = (jax.nn.silu(gate_up[:, :, 0]) * gate_up[:, :, 1]).astype(jnp.bfloat16)
    output = residual + model_sum(
        jnp.einsum("kfh,khd->kfd", hidden, w_down, preferred_element_type=jnp.float32)
    )
    head_low = rms_norm(output, gain_all[:, 2:3, :]).astype(jnp.bfloat16)
    logits = jnp.einsum("kfd,kdv->kfv", head_low, w_head, preferred_element_type=jnp.float32)
    local_max = jnp.max(logits, axis=-1)
    target_part = jnp.sum(jnp.where(picks, logits, 0.0), axis=-1)
    row_max = lax.pmax(local_max, "mp")
    sum_exp, target_logit = lax.psum(
        (jnp.sum(jnp.exp(logits - row_max[..., None]), axis=-1), target_part), "mp"
    )
    log_total = row_max + jnp.log(sum_exp)
    loss_sum = jnp.sum((log_total - target_logit) * loss_mask)
    kept = (
        picks,
        stream,
        attn_low,
        queries,
        key_vecs,
        values,
        attended,
        residual,
        ffn_low,
        gate_up,
        hidden,
        output,
        head_low,
        logits,
        log_total,
    )
    return (kept, loss_sum)


def swiglu(gate_up):
    return jax.nn.silu(gate_up[:, :, 0]) * gate_up[:, :, 1]


def backward(weights, kept, loss_mask, inverse_count):
    w_attn_in, w_attn_out, w_gate_up, w_down, w_head, embed_table, norm_gains = weights
    gain_all = norm_gains.astype(jnp.float32)
    (
        picks,
        stream,
        attn_low,
        queries,
        key_vecs,
        values,
        attended,
        residual,
        ffn_low,
        gate_up,
        hidden,
        output,
        head_low,
        logits,
        log_total,
    ) = kept
    probs = jnp.exp(logits - log_total[..., None])
    d_logits = (
        (probs - picks.astype(jnp.float32)) * (loss_mask * inverse_count)[..., None]
    ).astype(jnp.bfloat16)
    grad_head = jnp.einsum("kfd,kfv->kdv", head_low, d_logits, preferred_element_type=jnp.float32)
    d_head_in = model_sum(
        jnp.einsum("kfv,kdv->kfd", d_logits, w_head, preferred_element_type=jnp.float32)
    )
    d_output, gain_head = norm_back(output, gain_all[:, 2:3, :], d_head_in)
    d_output_low = d_output.astype(jnp.bfloat16)
    grad_down = jnp.einsum("kfh,kfd->khd", hidden, d_output_low, preferred_element_type=jnp.float32)
    d_hidden = jnp.einsum("kfd,khd->kfh", d_output_low, w_down, preferred_element_type=jnp.float32)
    _, swiglu_back = jax.vjp(swiglu, gate_up)
    d_gate_up = swiglu_back(d_hidden)[0].astype(jnp.bfloat16)
    grad_gate_up = jnp.einsum(
        "kfd,kfch->kdch", ffn_low, d_gate_up, preferred_element_type=jnp.float32
    )
    d_ffn_in = model_sum(
        jnp.einsum("kfch,kdch->kfd", d_gate_up, w_gate_up, preferred_element_type=jnp.float32)
    )
    d_norm_ffn, gain_ffn = norm_back(residual, gain_all[:, 1:2, :], d_ffn_in)
    d_residual = d_output + d_norm_ffn
    d_res_low = d_residual.astype(jnp.bfloat16)
    grad_out = jnp.einsum("kfi,kfo->kio", attended, d_res_low, preferred_element_type=jnp.float32)
    d_attended = jnp.einsum(
        "kfo,kio->kfi", d_res_low, w_attn_out, preferred_element_type=jnp.float32
    )
    _, attend_back = jax.vjp(attend, queries, key_vecs, values)
    d_heads = attend_back(d_attended)
    d_qkv = jnp.stack([piece.reshape(piece.shape[:2] + (-1,)) for piece in d_heads], axis=2).astype(
        jnp.bfloat16
    )
    grad_attn_in = jnp.einsum("kfd,kfce->kdce", attn_low, d_qkv, preferred_element_type=jnp.float32)
    d_attn_in = model_sum(
        jnp.einsum("kfce,kdce->kfd", d_qkv, w_attn_in, preferred_element_type=jnp.float32)
    )
    d_norm_attn, gain_attn = norm_back(stream, gain_all[:, 0:1, :], d_attn_in)
    d_stream = (d_residual + d_norm_attn)[1:].astype(jnp.bfloat16)
    grad_embed = jnp.einsum(
        "kfv,kfd->kvd",
        picks[:-1].astype(jnp.bfloat16),
        d_stream,
        preferred_element_type=jnp.float32,
    )
    grad_gains = jnp.stack([gain_attn, gain_ffn, gain_head], axis=1)
    return (grad_attn_in, grad_out, grad_gate_up, grad_down, grad_head, grad_embed, grad_gains)


def shards(
    context,
    codes,
    delays,
    counts,
    w_attn_in,
    w_attn_out,
    w_gate_up,
    w_down,
    w_head,
    embed_table,
    norm_gains,
    first_attn_in,
    first_attn_out,
    first_gate_up,
    first_down,
    first_head,
    first_embed,
    first_gains,
    second_attn_in,
    second_attn_out,
    second_gate_up,
    second_down,
    second_head,
    second_embed,
    second_gains,
):
    params = (w_attn_in, w_attn_out, w_gate_up, w_down, w_head, embed_table, norm_gains)
    firsts = (
        first_attn_in,
        first_attn_out,
        first_gate_up,
        first_down,
        first_head,
        first_embed,
        first_gains,
    )
    seconds = (
        second_attn_in,
        second_attn_out,
        second_gate_up,
        second_down,
        second_head,
        second_embed,
        second_gains,
    )
    low_params = tuple((weight.astype(jnp.bfloat16) for weight in params))
    model_ways = lax.axis_size("mp")
    vocab_start = lax.axis_index("mp") * w_head.shape[2]
    total_count = lax.psum(jnp.sum(counts).astype(jnp.float32), "dp")
    inverse_count = 1.0 / total_count
    targets = pick_targets(codes, delays)
    position = lax.broadcasted_iota(jnp.int32, (codes.shape[2], codes.shape[0]), 0)
    loss_mask = (position < counts[None, :]).astype(jnp.float32)
    batch_rows = context.shape[0] // MICRO
    shared = None
    shared = fetch(low_params)
    accum = None
    loss_local = jnp.float32(0.0)
    for micro_step in range(MICRO):
        frame_range = slice(micro_step * batch_rows, (micro_step + 1) * batch_rows)
        kept, loss_part = forward(
            shared,
            context[frame_range],
            targets[frame_range],
            loss_mask[:, frame_range],
            vocab_start,
        )
        grads = backward(shared, kept, loss_mask[:, frame_range], inverse_count)
        accum = (
            grads if accum is None else tuple((left + right for left, right in zip(accum, grads)))
        )
        loss_local = loss_local + loss_part
    accum = reduce_grads(accum)
    squares = (
        sum((jnp.sum(grad * grad) for grad in accum[:6]))
        + jnp.sum(accum[6] * accum[6]) / model_ways
    )
    square_total, loss_total = lax.psum((squares, loss_local / model_ways), ("dp", "mp"))
    grad_norm = jnp.sqrt(square_total)
    clip_scale = jnp.minimum(1.0, CLIP_NORM / (grad_norm + 1e-06))
    rates = (RATE_MATRIX,) * 5 + (RATE_TABLE, RATE_TABLE)
    new_weights, new_firsts, new_seconds = ([], [], [])
    for weight, first, second, grad, rate in zip(params, firsts, seconds, accum, rates):
        clipped = grad * clip_scale
        first_new = BETA_ONE * first + (1.0 - BETA_ONE) * clipped
        second_new = BETA_TWO * second + (1.0 - BETA_TWO) * clipped * clipped
        adam_step = first_new / BIAS_ONE / (jnp.sqrt(second_new / BIAS_TWO) + ADAM_EPS)
        new_weights.append(weight * (1.0 - rate * DECAY) - rate * adam_step)
        new_firsts.append(first_new)
        new_seconds.append(second_new)
    loss = loss_total / total_count
    return (
        new_weights[0],
        new_weights[1],
        new_weights[2],
        new_weights[3],
        new_weights[4],
        new_weights[5],
        new_weights[6],
        new_firsts[0],
        new_firsts[1],
        new_firsts[2],
        new_firsts[3],
        new_firsts[4],
        new_firsts[5],
        new_firsts[6],
        new_seconds[0],
        new_seconds[1],
        new_seconds[2],
        new_seconds[3],
        new_seconds[4],
        new_seconds[5],
        new_seconds[6],
        loss,
        grad_norm,
    )


def solution(mesh):
    in_specs = (
        P("dp", None),
        P("dp", None, None),
        P("dp"),
        P("dp"),
        P(None, "dp", None, "mp"),
        P(None, "mp", "dp"),
        P(None, "dp", None, "mp"),
        P(None, "mp", "dp"),
        P(None, "dp", "mp"),
        P(None, "mp", "dp"),
        P(None, None, "dp"),
        P(None, "dp", None, "mp"),
        P(None, "mp", "dp"),
        P(None, "dp", None, "mp"),
        P(None, "mp", "dp"),
        P(None, "dp", "mp"),
        P(None, "mp", "dp"),
        P(None, None, "dp"),
        P(None, "dp", None, "mp"),
        P(None, "mp", "dp"),
        P(None, "dp", None, "mp"),
        P(None, "mp", "dp"),
        P(None, "dp", "mp"),
        P(None, "mp", "dp"),
        P(None, None, "dp"),
    )
    out_specs = (
        P(None, "dp", None, "mp"),
        P(None, "mp", "dp"),
        P(None, "dp", None, "mp"),
        P(None, "mp", "dp"),
        P(None, "dp", "mp"),
        P(None, "mp", "dp"),
        P(None, None, "dp"),
        P(None, "dp", None, "mp"),
        P(None, "mp", "dp"),
        P(None, "dp", None, "mp"),
        P(None, "mp", "dp"),
        P(None, "dp", "mp"),
        P(None, "mp", "dp"),
        P(None, None, "dp"),
        P(None, "dp", None, "mp"),
        P(None, "mp", "dp"),
        P(None, "dp", None, "mp"),
        P(None, "mp", "dp"),
        P(None, "dp", "mp"),
        P(None, "mp", "dp"),
        P(None, None, "dp"),
        P(),
        P(),
    )
    return jax.shard_map(shards, mesh=mesh, in_specs=in_specs, out_specs=out_specs, check_vma=False)
```

profile of v0, /device:TPU:1, one launch (start us, length us, event | category | flops | bytes accessed | tf_op | source)
XLA Modules:
  0.0 2321.2 jit_solution(17882000480023827224)
XLA Ops:
  11.5 62.2 %all-gather.7.cloned.1.call-done = bf16[1,1024,1024]{1,2,0:T(8,128)(2,1)} async-done(((bf16[1,1024,64]{1,2,0:T(8,128)(2,1)}), bf16[1,1024,1024]{1,2,0:T(8,128)(2,1)}) %all-gather.7.cloned.1.call-update) | async-done | bytes 2097168 | tf_op jit(solution)/shard_map/all_gather | solution.py:66
  73.8 3.0 fusion.28
  76.8 3.0 fusion.31
  81.6 34.5 %all_gather.22 = bf16[2,3,1024]{1,0,2:T(2,128)(2,1)S(1)} all-gather(bf16[2,3,64]{1,0,2:T(2,128)(2,1)S(1)} %copy.258), channel_id=1, replica_groups=mesh['dp'=16,'mp'=2] {'dp'}, dimensions={2}, use_global_device_ids=true | all-gather | bytes 13056 | tf_op jit(solution)/shard_map/all_gather | solution.py:67
  116.1 2.4 fusion.138
  121.4 74.6 %all-gather.9.cloned.1.call-done = bf16[2,1024,3,512]{3,1,2,0:T(8,128)(2,1)} async-done(((bf16[2,64,3,512]{3,1,2,0:T(8,128)(2,1)}), bf16[2,1024,3,512]{3,1,2,0:T(8,128)(2,1)}) %all-gather.9.cloned.1.call-update) | async-done | bytes 6291472 | tf_op jit(solution)/shard_map/all_gather | solution.py:61
  196.0 4.2 convolution_convert_fusion
  205.6 4.2 convolution_convert_fusion.1
  217.2 42.1 %all-gather.11.cloned.1.call-done = bf16[2,512,1024]{1,2,0:T(8,128)(2,1)} async-done(((bf16[2,512,64]{1,2,0:T(8,128)(2,1)}), bf16[2,512,1024]{1,2,0:T(8,128)(2,1)}) %all-gather.11.cloned.1.call-update) | async-done | bytes 2097168 | tf_op jit(solution)/shard_map/all_gather | solution.py:62
  259.3 3.1 fusion.151
  262.4 3.1 fusion.149
  269.4 14.9 all-reduce.32.cloned.1.call-done
  286.8 143.3 %all-gather.13.cloned.1.call-done = bf16[2,1024,2,1408]{3,1,2,0:T(8,128)(2,1)} async-done(((bf16[2,64,2,1408]{3,1,2,0:T(8,128)(2,1)}), bf16[2,1024,2,1408]{3,1,2,0:T(8,128)(2,1)}) %all-gather.13.cloned.1.call-update) | async-done | bytes 11534352 | tf_op jit(solution)/shard_map/all_gather | solution.py:63
  430.1 6.2 fusion.2
  438.1 2.2 fusion.108
  440.4 80.3 %all-gather.15.cloned.1.call-done = bf16[2,1408,1024]{1,2,0:T(8,128)(2,1)} async-done(((bf16[2,1408,64]{1,2,0:T(8,128)(2,1)}), bf16[2,1408,1024]{1,2,0:T(8,128)(2,1)}) %all-gather.15.cloned.1.call-update) | async-done | bytes 5767184 | tf_op jit(solution)/shard_map/all_gather | solution.py:64
  520.7 5.3 fusion.152
  526.0 2.6 fusion.150
  531.8 33.8 %psum.137 = f32[]{:T(128)} all-reduce(f32[]{:T(128)S(6)} %convert_element_type.145), channel_id=1, replica_groups=mesh['dp'=16,'mp'=2] {'dp'}, use_global_device_ids=true, to_apply=%region_14.15 | all-reduce | flops 1 | bytes 8 | tf_op jit(solution)/shard_map/psum | solution.py:264
  570.1 57.6 %all-gather.17.cloned.1.call-done = bf16[2,1024,1024]{2,1,0:T(8,128)(2,1)} async-done(((bf16[2,64,1024]{2,1,0:T(8,128)(2,1)}), bf16[2,1024,1024]{2,1,0:T(8,128)(2,1)}) %all-gather.17.cloned.1.call-update) | async-done | bytes 4194320 | tf_op jit(solution)/shard_map/all_gather | solution.py:65
  627.6 3.3 fusion.144
  632.1 4.0 all-reduce.13
  636.4 2.5 all-reduce.6
  639.5 4.7 fusion.123
  644.2 2.2 fusion.122
  646.5 18.0 all-reduce.28.cloned.1.call-done
  667.3 4.3 multiply_bitcast_fusion
  672.9 8.2 fusion.17
  681.1 4.2 fusion.14
  689.0 17.0 all-reduce.26.cloned.1.call-done
  705.9 2.0 multiply_reduce_fusion.5
  709.3 2.4 fusion.49
  715.4 4.6 fusion.27
  720.0 2.1 fusion.95
  723.4 3.1 multiply_reduce_fusion.18
  726.5 3.3 multiply_reduce_fusion.12
  737.3 2.8 fusion.23
  741.6 5.5 convolution_bitcast_fusion
  747.1 5.5 convolution_bitcast_fusion.1
  752.8 20.5 all-reduce.24.cloned.1.call-done
  777.1 3.4 reshape.304
  781.9 3.7 add_bitcast_fusion
  785.6 11.0 copy.302
  798.2 2.7 convolution_add_fusion.4
  803.3 4.6 convolution_add_fusion.3
  810.7 6.0 convolution_add_fusion.1
  819.7 6.5 convolution_add_fusion.2
  827.3 9.4 fusion.43
  836.8 14.9 convolution_add_fusion
  857.1 172.0 %all-reduce.22.cloned.1.call-done = f32[1,1024,1024]{1,0,2:T(1,128)} async-done(((f32[1,1024,1024]{1,0,2:T(1,128)}), f32[1,1024,1024]{1,0,2:T(1,128)}) %all-reduce.22.cloned.1.call-update) | async-done | bytes 4194320
  1029.0 2.1 multiply_reduce_fusion.24
  1031.1 93.3 %reduce-scatter.11.cloned.1.call-done = f32[2,512,64]{1,2,0:T(8,128)} async-done(((f32[2,512,1024]{1,2,0:T(8,128)}), f32[2,512,64]{1,2,0:T(8,128)}) %reduce-scatter.11.cloned.1.call-update) | async-done | bytes 262160 | tf_op jit(solution)/shard_map/reduce_scatter | solution.py:74
  1126.1 178.6 %reduce-scatter.17.cloned.1.call-done = f32[2,64,1024]{2,1,0:T(8,128)} async-done(((f32[2,1024,1024]{2,1,0:T(8,128)}), f32[2,64,1024]{2,1,0:T(8,128)}) %reduce-scatter.17.cloned.1.call-update) | async-done | bytes 524304 | tf_op jit(solution)/shard_map/reduce_scatter | solution.py:77
  1306.5 243.8 %reduce-scatter.15.cloned.1.call-done = f32[2,1408,64]{1,2,0:T(8,128)} async-done(((f32[2,1408,1024]{1,2,0:T(8,128)}), f32[2,1408,64]{1,2,0:T(8,128)}) %reduce-scatter.15.cloned.1.call-update) | async-done | bytes 720912 | tf_op jit(solution)/shard_map/reduce_scatter | solution.py:76
  1552.1 213.0 %reduce-scatter.9.cloned.1.call-done = f32[2,64,3,512]{3,1,2,0:T(8,128)} async-done(((f32[2,1024,3,512]{3,1,2,0:T(8,128)}), f32[2,64,3,512]{3,1,2,0:T(8,128)}) %reduce-scatter.9.cloned.1.call-update) | async-done | bytes 786448 | tf_op jit(solution)/shard_map/reduce_scatter | solution.py:73
  1768.3 472.0 %reduce-scatter.13.cloned.1.call-done = f32[2,64,2,1408]{3,1,2,0:T(8,128)} async-done(((f32[2,1024,2,1408]{3,1,2,0:T(8,128)}), f32[2,64,2,1408]{3,1,2,0:T(8,128)}) %reduce-scatter.13.cloned.1.call-update) | async-done | bytes 1441808 | tf_op jit(solution)/shard_map/reduce_scatter | solution.py:75
  2240.3 2.3 multiply_reduce_fusion
  2245.3 45.2 %all-reduce.5 = (f32[]{:T(128)}, f32[]{:T(128)}) all-reduce(f32[]{:T(128)S(6)} %add.329, f32[]{:T(128)S(6)} %div.326), channel_id=1, replica_groups=mesh['dp'=16,'mp'=2] {'dp','mp'}, use_global_device_ids=true, to_apply=%region_61.62 | all-reduce | flops 2 | bytes 16 | tf_op jit(solution)/shard_map/psum | solution.py:293
  2291.2 2.9 multiply_subtract_fusion
  2294.2 2.2 copy.307
  2296.4 2.2 copy.308
  2298.6 2.2 copy.309
  2302.9 2.0 multiply_subtract_fusion.4
  2304.9 2.7 multiply_subtract_fusion.3
  (417 shorter events, 91.7 us)
Async XLA Ops:
  7.2 72.7 %copy-start.26 = (f32[2,64,3,512]{3,1,2,0:T(8,128)S(1)}, f32[2,64,3,512]{3,1,2,0:T(8,128)}, u32[]{:S(2)}) copy-start(f32[2,64,3,512]{3,1,2,0:T(8,128)} %param.29) | copy-start | bytes 2359300
  7.2 73.5 %copy-start.48 = (f32[2,512,64]{1,2,0:T(8,128)S(1)}, f32[2,512,64]{1,2,0:T(8,128)}, u32[]{:S(2)}) copy-start(f32[2,512,64]{1,2,0:T(8,128)} %param.30) | copy-start | bytes 786436
  7.2 74.3 %copy-start.110 = (f32[2,3,64]{2,0,1:T(2,128)S(1)}, f32[2,3,64]{2,0,1:T(2,128)}, u32[]{:S(2)}) copy-start(f32[2,3,64]{2,0,1:T(2,128)} %param.35) | copy-start | bytes 4612
  7.2 66.5 %all-gather.7.cloned.1.call-start = ((), (), s32[]{:S(2)}) async-start(), calls=%async_computation.6 | async-start | bytes 2228224 | tf_op jit(solution)/shard_map/all_gather | solution.py:66
  9.0 110.3 %all-reduce.34.cloned.1.call-start = ((), (), s32[]{:S(2)}) async-start(), calls=%async_computation.24 | async-start | bytes 786432 | tf_op jit(solution)/shard_map/psum | solution.py:56
  11.4 107.2 %copy-start.81 = (pred[2,48,1024]{2,1,0:T(8,128)(4,1)}, pred[2,48,1024]{2,1,0:T(8,128)(4,1)S(1)}, u32[]{:S(2)}) copy-start(pred[2,48,1024]{2,1,0:T(8,128)(4,1)S(1)} %iota_compare_fusion.1) | copy-start | bytes 294916
  11.5 107.0 %copy-start.79 = (pred[2,48,1024]{2,1,0:T(8,128)(4,1)}, pred[2,48,1024]{2,1,0:T(8,128)(4,1)S(1)}, u32[]{:S(2)}) copy-start(pred[2,48,1024]{2,1,0:T(8,128)(4,1)S(1)} %iota_compare_fusion) | copy-start | bytes 294916
  79.8 116.2 %all-gather.9.cloned.1.call-start = ((), (), s32[]{:S(2)}) async-start(), calls=%async_computation.7 | async-start | bytes 6684672 | tf_op jit(solution)/shard_map/all_gather | solution.py:61
  80.7 37.9 %copy-start.100 = (bf16[96,1024]{1,0:T(8,128)(2,1)S(1)}, bf16[96,1024]{1,0:T(8,128)(2,1)}, u32[]{:S(2)}) copy-start(bf16[96,1024]{1,0:T(8,128)(2,1)} %param.25) | copy-start | bytes 589828
  80.7 178.6 %all-gather.11.cloned.1.call-start = ((), (), s32[]{:S(2)}) async-start(), calls=%async_computation.8 | async-start | bytes 2228224 | tf_op jit(solution)/shard_map/all_gather | solution.py:62
  81.4 202.9 %all-reduce.32.cloned.1.call-start = ((), (), s32[]{:S(2)}) async-start(), calls=%async_computation.23 | async-start | bytes 1572864 | tf_op jit(solution)/shard_map/psum | solution.py:56
  118.6 166.9 %copy-start.11 = (f32[1,48,1024]{2,1,0:T(8,128)}, f32[1,48,1024]{2,1,0:T(8,128)S(1)}, u32[]{:S(2)}) copy-start(f32[1,48,1024]{2,1,0:T(8,128)S(1)} %get-tuple-element.225) | copy-start | bytes 589828
  119.3 91.8 %copy-start.120 = (pred[2,2]{0,1:T(4,128)(4,1)}, pred[2,2]{0,1:T(4,128)(4,1)S(1)}, u32[]{:S(2)}) copy-start(pred[2,2]{0,1:T(4,128)(4,1)S(1)} %iota_compare_fusion.3) | copy-start | bytes 16
  121.4 79.3 %copy-start.114 = (f32[2,48]{1,0:T(2,128)}, f32[2,48]{1,0:T(2,128)S(1)}, u32[]{:S(2)}) copy-start(f32[2,48]{1,0:T(2,128)S(1)} %multiply_reduce_fusion.23) | copy-start | bytes 1156
  205.6 53.7 %copy-start.51 = (bf16[2,48,512]{2,1,0:T(8,128)(2,1)}, bf16[2,48,512]{2,1,0:T(8,128)(2,1)S(1)}, u32[]{:S(2)}) copy-start(bf16[2,48,512]{2,1,0:T(8,128)(2,1)S(1)} %convert_element_type.154) | copy-start | bytes 294916
  212.7 46.6 %copy-start.39 = (f32[48,8,2]{2,1,0:T(8,128)}, f32[48,8,2]{2,1,0:T(8,128)S(1)}, u32[]{:S(2)}) copy-start(f32[48,8,2]{2,1,0:T(8,128)S(1)} %get-tuple-element.243) | copy-start | bytes 9220
  213.7 51.9 %copy-start.17 = (f32[2,64,2,1408]{3,2,1,0:T(2,128)S(1)}, f32[2,64,2,1408]{3,2,1,0:T(2,128)}, u32[]{:S(2)}) copy-start(f32[2,64,2,1408]{3,2,1,0:T(2,128)} %param.31) | copy-start | bytes 4325380
  217.2 49.3 %copy-start.65 = (bf16[2,48,512]{2,1,0:T(8,128)(2,1)}, bf16[2,48,512]{2,1,0:T(8,128)(2,1)S(1)}, u32[]{:S(2)}) copy-start(bf16[2,48,512]{2,1,0:T(8,128)(2,1)S(1)} %convert_element_type.135) | copy-start | bytes 294916
  262.4 21.9 copy-start.13
  265.5 164.6 %all-gather.13.cloned.1.call-start = ((), (), s32[]{:S(2)}) async-start(), calls=%async_computation.9 | async-start | bytes 12255232 | tf_op jit(solution)/shard_map/all_gather | solution.py:63
  266.6 254.1 %all-gather.15.cloned.1.call-start = ((), (), s32[]{:S(2)}) async-start(), calls=%async_computation.10 | async-start | bytes 6127616 | tf_op jit(solution)/shard_map/all_gather | solution.py:64
  268.5 299.2 %all-reduce.30.cloned.1.call-start = ((), (), s32[]{:S(2)}) async-start(), calls=%async_computation.22 | async-start | bytes 1572864 | tf_op jit(solution)/shard_map/psum | solution.py:56
  285.4 150.9 %copy-start.116 = (f32[2,48]{1,0:T(2,128)}, f32[2,48]{1,0:T(2,128)S(1)}, u32[]{:S(2)}) copy-start(f32[2,48]{1,0:T(2,128)S(1)} %get-tuple-element.207) | copy-start | bytes 1156
  285.5 282.3 %copy-start.5 = (f32[2,48,1024]{2,1,0:T(8,128)}, f32[2,48,1024]{2,1,0:T(8,128)S(1)}, u32[]{:S(2)}) copy-start(f32[2,48,1024]{2,1,0:T(8,128)S(1)} %get-tuple-element.208) | copy-start | bytes 1179652
  286.7 149.6 %copy-start.117 = (f32[2,48]{1,0:T(2,128)}, f32[2,48]{1,0:T(2,128)S(1)}, u32[]{:S(2)}) copy-start(f32[2,48]{1,0:T(2,128)S(1)} %get-tuple-element.209) | copy-start | bytes 1156
  437.3 83.4 %copy-start.31 = (bf16[2,48,1408]{2,1,0:T(8,128)(2,1)}, bf16[2,48,1408]{2,1,0:T(8,128)(2,1)S(1)}, u32[]{:S(2)}) copy-start(bf16[2,48,1408]{2,1,0:T(8,128)(2,1)S(1)} %multiply_convert_fusion) | copy-start | bytes 811012
  440.4 88.2 %copy-start.33 = (bf16[2,48,1408]{2,1,0:T(8,128)(2,1)}, bf16[2,48,1408]{2,1,0:T(8,128)(2,1)S(1)}, u32[]{:S(2)}) copy-start(bf16[2,48,1408]{2,1,0:T(8,128)(2,1)S(1)} %multiply_convert_fusion.1) | copy-start | bytes 811012
  528.6 99.0 %all-gather.17.cloned.1.call-start = ((), (), s32[]{:S(2)}) async-start(), calls=%async_computation.11 | async-start | bytes 4456448 | tf_op jit(solution)/shard_map/all_gather | solution.py:65
  530.5 134.0 %all-reduce.28.cloned.1.call-start = ((), (), s32[]{:S(2)}) async-start(), calls=%async_computation.21 | async-start | bytes 1572864 | tf_op jit(solution)/shard_map/psum | solution.py:56
  630.9 13.3 copy-start.7
  632.1 14.3 copy-start.9
  646.4 59.5 %all-reduce.26.cloned.1.call-start = ((), (), s32[]{:S(2)}) async-start(), calls=%async_computation.20 | async-start | bytes 1572864 | tf_op jit(solution)/shard_map/psum | solution.py:56
  671.7 9.4 slice-start.2
  671.7 9.4 slice-start.3
  685.3 27.2 %copy-start.2 = (bf16[2,512,1024]{1,2,0:T(8,128)(2,1)S(1)}, bf16[2,512,1024]{1,2,0:T(8,128)(2,1)}, u32[]{:S(2)}) copy-start(bf16[2,512,1024]{1,2,0:T(8,128)(2,1)} %all-gather.11.cloned.1.call-done) | copy-start | bytes 6291460
  685.3 88.0 %all-reduce.24.cloned.1.call-start = ((), (), s32[]{:S(2)}) async-start(), calls=%async_computation.19 | async-start | bytes 1572864 | tf_op jit(solution)/shard_map/psum | solution.py:56
  730.8 9.4 copy-start.99
  741.1 11.6 copy-start.59
  741.3 11.3 copy-start.61
  741.6 11.1 copy-start.63
  747.1 26.2 %copy-start.12 = (f32[1,48,1024]{2,1,0:T(8,128)S(1)}, f32[1,48,1024]{2,1,0:T(8,128)}, u32[]{:S(2)}) copy-start(f32[1,48,1024]{2,1,0:T(8,128)} %copy-done.11) | copy-start | bytes 589828
  747.1 26.2 %copy-start.14 = (f32[1,48,1024]{2,1,0:T(8,128)S(1)}, f32[1,48,1024]{2,1,0:T(8,128)}, u32[]{:S(2)}) copy-start(f32[1,48,1024]{2,1,0:T(8,128)} %get-tuple-element.173) | copy-start | bytes 589828
  747.1 26.2 %copy-start.16 = (f32[1,48,1024]{2,1,0:T(8,128)S(1)}, f32[1,48,1024]{2,1,0:T(8,128)}, u32[]{:S(2)}) copy-start(f32[1,48,1024]{2,1,0:T(8,128)} %get-tuple-element.172) | copy-start | bytes 589828
  747.1 28.2 %copy-start.101 = (f32[2,1024]{1,0:T(2,128)S(1)}, f32[2,1024]{1,0:T(2,128)}, u32[]{:S(2)}) copy-start(f32[2,1024]{1,0:T(2,128)} %get-tuple-element.232) | copy-start | bytes 24580
  752.7 28.3 %copy-start.115 = (f32[2,48]{1,0:T(2,128)S(1)}, f32[2,48]{1,0:T(2,128)}, u32[]{:S(2)}) copy-start(f32[2,48]{1,0:T(2,128)} %copy-done.114) | copy-start | bytes 1156
  752.7 28.3 %copy-start.113 = (f32[2,48]{1,0:T(2,128)S(1)}, f32[2,48]{1,0:T(2,128)}, u32[]{:S(2)}) copy-start(f32[2,48]{1,0:T(2,128)} %copy-done.112) | copy-start | bytes 1156
  752.7 28.4 %copy-start.21 = (f32[2,48,1024]{2,1,0:T(8,128)S(1)}, f32[2,48,1024]{2,1,0:T(8,128)}, u32[]{:S(2)}) copy-start(f32[2,48,1024]{2,1,0:T(8,128)} %get-tuple-element.230) | copy-start | bytes 1179652
  752.7 28.4 %copy-start.82 = (pred[2,48,1024]{2,1,0:T(8,128)(4,1)S(1)}, pred[2,48,1024]{2,1,0:T(8,128)(4,1)}, u32[]{:S(2)}) copy-start(pred[2,48,1024]{2,1,0:T(8,128)(4,1)} %copy-done.81) | copy-start | bytes 294916
  752.7 102.1 %reduce-scatter.19.cloned.1.call-start = ((), (), s32[]{:S(2)}) async-start(), calls=%async_computation.17 | async-start | bytes 557056
  780.5 248.5 %all-reduce.22.cloned.1.call-start = ((), (), s32[]{:S(2)}) async-start(), calls=%async_computation.18 | async-start | bytes 8388608
  796.6 327.9 %reduce-scatter.11.cloned.1.call-start = ((), (), s32[]{:S(2)}) async-start(), calls=%async_computation.13 | async-start | bytes 4456448 | tf_op jit(solution)/shard_map/reduce_scatter | solution.py:74
  801.0 503.7 %reduce-scatter.17.cloned.1.call-start = ((), (), s32[]{:S(2)}) async-start(), calls=%async_computation.16 | async-start | bytes 8912896 | tf_op jit(solution)/shard_map/reduce_scatter | solution.py:77
  808.0 742.2 %reduce-scatter.15.cloned.1.call-start = ((), (), s32[]{:S(2)}) async-start(), calls=%async_computation.15 | async-start | bytes 12255232 | tf_op jit(solution)/shard_map/reduce_scatter | solution.py:76
  816.8 948.3 %reduce-scatter.9.cloned.1.call-start = ((), (), s32[]{:S(2)}) async-start(), calls=%async_computation.12 | async-start | bytes 13369344 | tf_op jit(solution)/shard_map/reduce_scatter | solution.py:73
  826.2 10.6 copy-start.6
  826.2 10.6 copy-start.76
  826.2 10.6 copy-start.78
  826.2 1414.1 %reduce-scatter.13.cloned.1.call-start = ((), (), s32[]{:S(2)}) async-start(), calls=%async_computation.14 | async-start | bytes 24510464 | tf_op jit(solution)/shard_map/reduce_scatter | solution.py:75
  851.7 1439.5 %copy-start.18 = (f32[2,64,2,1408]{3,2,1,0:T(2,128)S(1)}, f32[2,64,2,1408]{3,2,1,0:T(2,128)}, u32[]{:S(2)}) copy-start(f32[2,64,2,1408]{3,2,1,0:T(2,128)} %param.31) | copy-start | bytes 4325380
  851.7 1439.5 %copy-start.45 = (f32[2,64,2,1408]{3,2,1,0:T(2,128)S(1)}, f32[2,64,2,1408]{3,2,1,0:T(2,128)}, u32[]{:S(2)}) copy-start(f32[2,64,2,1408]{3,2,1,0:T(2,128)} %param.38) | copy-start | bytes 4325380
  2294.2 8.7 copy-start.47
  2294.2 8.7 copy-start.86
  2298.6 8.9 copy-start.29
  2298.6 8.9 copy-start.30
  (84 other events, 350.8 us)
Sparse Core Ops, SparseCore 0:
  11.4 62.3 all-gather.6
  79.9 18.0 all-reduce.33
  101.7 94.2 all-gather.8
  199.6 59.6 all-gather.10
  265.6 18.6 all-reduce.31
  287.5 142.5 all-gather.12
  433.4 87.2 all-gather.14
  528.7 19.0 all-reduce.29
  551.6 75.9 all-gather.16
  646.5 17.8 all-reduce.27
  685.5 20.4 all-reduce.25
  752.9 20.4 all-reduce.23
  780.7 66.3 reduce-scatter.18
  853.5 175.5 all-reduce.21
  1031.2 93.2 reduce-scatter.10
  1126.6 178.0 reduce-scatter.16
  1306.8 243.3 reduce-scatter.14
  1555.7 209.3 reduce-scatter.8
  1767.5 472.7 reduce-scatter.12
where the time goes:
time: 2330 us; the launch traced here: 2320 us
  waiting for transfers between devices  1900 us (82%)
  matrix products  159 us (7%)
  blocking collectives  120 us (5%)
  other arithmetic  60.5 us (3%)
  local copies, waits for them, and re-layouts  48.5 us (2%)
  between operations  28.1 us (1%)
    reduce_scatter x1, waiting for transfers between devices, reduce_grads(): lax.psum_scatter(grads[2], 'dp', scatter_dimension=1, tiled=True)  472 us
    reduce_scatter x1, waiting for transfers between devices, reduce_grads(): lax.psum_scatter(grads[3], 'dp', scatter_dimension=2, tiled=True)  244 us
    reduce_scatter x1, waiting for transfers between devices, reduce_grads(): lax.psum_scatter(grads[0], 'dp', scatter_dimension=1, tiled=True)  213 us
    reduce_scatter x1, waiting for transfers between devices, reduce_grads(): lax.psum_scatter(grads[4], 'dp', scatter_dimension=1, tiled=True)  179 us
    unnamed x21, waiting for transfers between devices  172 us
    all_gather x1, waiting for transfers between devices, fetch(): lax.all_gather(low_params[2], 'dp', axis=1, tiled=True)  143 us
    reduce_scatter x1, waiting for transfers between devices, reduce_grads(): lax.psum_scatter(grads[1], 'dp', scatter_dimension=2, tiled=True)  93.3 us
    all_gather x1, waiting for transfers between devices, fetch(): lax.all_gather(low_params[3], 'dp', axis=2, tiled=True)  80.3 us
  transfers between devices with their start and end apart: 19, of which 16 were waited for; matrix products, arithmetic and copies ran while one was open for 6% of the time, Pallas kernels for 0%

commit v1 on v0

v1 whole, which is shorter than its diff:
```python
import jax
import jax.numpy as jnp
from jax import lax
from jax.sharding import PartitionSpec as P

HEAD_DIM = 64
TP = 4
LANE = 128

NORM_EPS = 1e-05
CLIP_NORM = 0.02
BETA_ONE = 0.9
BETA_TWO = 0.95
BIAS_ONE = 1.0 - 0.9**10
BIAS_TWO = 1.0 - 0.95**10
ADAM_EPS = 1e-08
DECAY = 0.1
RATE_MATRIX = 0.03
RATE_TABLE = 0.5

BF = jnp.bfloat16
F32 = jnp.float32


def core_swap(piece):
    return lax.ppermute(piece, "mp", [(0, 1), (1, 0)])


def flip(piece, mask):
    ways = lax.axis_size("dp")
    return lax.ppermute(piece, "dp", [(chip, chip ^ mask) for chip in range(ways)])


def peer(piece, step):
    return flip(piece, (step >> 1) * 4 + (step & 1))


def other_y(piece):
    return flip(piece, 2)


def from_h(piece, step):
    ways = lax.axis_size("dp")
    return lax.ppermute(piece, "dp", [(chip, (chip - 8 * step) % ways) for chip in range(ways)])


def to_h(piece, step):
    ways = lax.axis_size("dp")
    return lax.ppermute(piece, "dp", [(chip, (chip + 8 * step) % ways) for chip in range(ways)])


def group_gather(block):
    return jnp.concatenate([block] + [peer(block, step) for step in range(1, TP)], axis=0)


def group_scatter(partial):
    rows = partial.shape[0] // TP
    total = partial[:rows]
    for step in range(1, TP):
        total = total + peer(partial[step * rows : (step + 1) * rows].astype(BF), step).astype(F32)
    return total


def peer_slots(stats, step):
    parts = jnp.split(stats, TP, axis=1)
    return jnp.concatenate([parts[k ^ step] for k in range(TP)], axis=1)


def by_core(core, zero, one):
    return jnp.where(core == 0, zero, one)


def by_slot(rel, low, side):
    rel = [jnp.where(side == 0, rel[k], rel[k ^ 1]) for k in range(TP)]
    return [jnp.where(low == 0, rel[k], rel[k ^ 2]) for k in range(TP)]


def gather_weight(packed, core, low, side):
    mine = by_core(core, packed[0], packed[1])
    theirs = core_swap(by_core(core, packed[1], packed[0]))
    first = by_core(core, mine, theirs)
    second = by_core(core, theirs, mine)
    pieces = [first[0], first[1], second[0], second[1]]
    rel = by_slot(pieces, low, side)
    rel = [rel[0]] + [peer(rel[step], step) for step in range(1, TP)]
    held = jnp.concatenate(by_slot(rel, low, side), axis=0)
    groups = lax.axis_size("dp") // 8
    held = jnp.concatenate([held] + [from_h(held, step) for step in range(1, groups)], axis=0)
    return jnp.concatenate([held, other_y(held)], axis=0)


def scatter_grad(grad, core, low, side):
    half = grad.shape[0] // 2
    kept = grad[:half] + other_y(grad[half:].astype(BF)).astype(F32)
    groups = lax.axis_size("dp") // 8
    rows = half // groups
    total = kept[:rows]
    for step in range(1, groups):
        total = total + to_h(kept[step * rows : (step + 1) * rows].astype(BF), step).astype(F32)
    squares = jnp.sum(total * total)
    low_total = total.astype(BF).reshape(TP, rows // TP, -1)
    rel = by_slot([low_total[k] for k in range(TP)], low, side)
    rel = [rel[0]] + [peer(rel[step], step) for step in range(1, TP)]
    first, second = [jnp.stack(pair) for pair in zip(*[iter(by_slot(rel, low, side))] * 2)]
    mine = by_core(core, first, second)
    theirs = core_swap(by_core(core, second, first))
    return by_core(core, mine, theirs), by_core(core, theirs, mine), squares


def norm_parts(inputs):
    scale = lax.rsqrt(jnp.mean(inputs * inputs, axis=-1, keepdims=True) + NORM_EPS)
    return inputs * scale, scale


def norm_back(normed, scale, gain, upstream):
    scaled = upstream * gain
    inner = jnp.mean(scaled * normed, axis=-1, keepdims=True)
    return scale * (scaled - normed * inner), jnp.sum(upstream * normed, axis=0)


def dot(left, right):
    return jnp.dot(left, right, preferred_element_type=F32)


def dot_t(left, right):
    return lax.dot_general(left, right, (((1,), (1,)), ((), ())), preferred_element_type=F32)


def t_dot(left, right):
    return lax.dot_general(left, right, (((0,), (0,)), ((), ())), preferred_element_type=F32)


def wide_dot(left, right):
    return jnp.dot(left, right, preferred_element_type=F32, precision=lax.Precision.HIGHEST)


def split_hidden(array, wide):
    rest = array[..., wide:]
    pad = [(0, 0)] * (array.ndim - 1) + [(0, wide - rest.shape[-1])]
    return array[..., :wide], jnp.pad(rest, pad)


def halves(array):
    size = array.shape[-1] // 2
    return array[..., :size], array[..., size:]


def adam(weight, first, second, clipped, rate):
    first_new = BETA_ONE * first + (1.0 - BETA_ONE) * clipped
    second_new = BETA_TWO * second + (1.0 - BETA_TWO) * clipped * clipped
    adam_step = first_new / BIAS_ONE / (jnp.sqrt(second_new / BIAS_TWO) + ADAM_EPS)
    return weight * (1.0 - rate * DECAY) - rate * adam_step, first_new, second_new


def pick_targets(codes, delays):
    window = lax.broadcasted_iota(jnp.int32, (1, codes.shape[1], 1), 1)
    delayed = jnp.sum(jnp.where(window == delays[:, None, None], codes, 0), axis=1)
    position = lax.broadcasted_iota(jnp.int32, delayed.shape, 1)
    return jnp.where(position == 0, codes[:, 0, :], delayed)


def shards(*args):
    context, codes, delays, counts = args[:4]
    params, firsts, seconds = args[4:11], args[11:18], args[18:25]
    w_attn_in, w_attn_out, w_gate_up, w_down, w_head, embed_table, norm_gains = params
    chips = lax.axis_size("dp")
    groups = chips // 8
    chip = lax.axis_index("dp")
    core = lax.axis_index("mp")
    side = chip & 1
    level = (chip >> 1) & 1
    low = (chip >> 2) & 1
    high = chip >> 3
    slot = low * 2 + side
    frames, width = context.shape
    rows = width // chips
    ffn_half = w_down.shape[1]
    ffn_wide = -(-ffn_half // (2 * LANE)) * LANE
    vocab_half = embed_table.shape[1]

    out_t = jnp.swapaxes(w_attn_out, 1, 2)
    down_t = jnp.swapaxes(w_down, 1, 2)

    def pack(parts):
        zero = jnp.concatenate([part[0].astype(BF) for part in parts], axis=-1)
        one = jnp.concatenate([part[1].astype(BF) for part in parts], axis=-1)
        return jnp.stack([zero, one], axis=1)

    attn_parts = [halves(w_attn_in[:, :, k]) for k in range(3)] + [halves(out_t)]
    full_attn = gather_weight(pack(attn_parts), core, low, side)
    gate_parts = [split_hidden(w_gate_up[:, :, k], ffn_wide) for k in range(2)]
    full_gate = gather_weight(pack(gate_parts), core, low, side)
    full_down = gather_weight(pack([split_hidden(down_t, ffn_wide)]), core, low, side)
    full_head = gather_weight(pack([halves(w_head)]), core, low, side)
    heads_wide = w_attn_out.shape[1] // 2
    full_in, full_out = full_attn[:, : 3 * heads_wide], full_attn[:, 3 * heads_wide :]

    targets = pick_targets(codes, delays)
    facts = jnp.concatenate([targets.T, counts[None]], axis=0)
    facts = lax.all_to_all(jnp.broadcast_to(facts[None], (chips,) + facts.shape), "dp", 0, 0)
    gain_send = jnp.broadcast_to(
        norm_gains.astype(BF).reshape(1, 6, rows), (chips, 6, rows)
    )
    gain_all = lax.all_to_all(gain_send, "dp", 0, 0)
    total_count = jnp.sum(facts[:, 2]).astype(F32)
    inverse_count = 1.0 / total_count
    chip_ids = lax.broadcasted_iota(jnp.int32, (TP, chips), 1)
    steps = lax.broadcasted_iota(jnp.int32, (TP, chips), 0)
    slots = slot ^ steps
    members = high * 8 + (slots >> 1) * 4 + level * 2 + (slots & 1)
    chosen = (members == chip_ids)[:, :, None, None]
    group_facts = jnp.sum(jnp.where(chosen, facts[None], 0), axis=1)
    group_frames = TP * frames
    group_targets = by_core(core, group_facts[:, 0], group_facts[:, 1]).reshape(group_frames)
    group_mask = (group_facts[:, 2].reshape(group_frames) > core).astype(F32)

    feature = lax.broadcasted_iota(jnp.int32, (1, width), 1)
    member = feature // rows
    place_y = member // (groups * TP)
    place_h = (member // TP) % groups
    place_t = member % TP
    source_chip = (
        ((high + place_h) % groups) * 8
        + (place_t >> 1) * 4
        + (level ^ place_y) * 2
        + (place_t & 1)
    )
    source = source_chip * rows + feature % rows
    order = (lax.broadcasted_iota(jnp.int32, (width, width), 0) == source).astype(BF)

    vocab_ids = core * vocab_half + lax.broadcasted_iota(jnp.int32, (1, vocab_half), 1)
    all_hot = (facts[:, 0].reshape(-1, 1) == vocab_ids).astype(BF)
    looked = dot(all_hot, embed_table[0].astype(BF)).astype(BF)
    looked = looked + core_swap(looked)
    looked = lax.all_to_all(looked.reshape(chips, frames, rows), "dp", 0, 0)
    looked = jnp.swapaxes(looked, 0, 1).reshape(frames, width)
    gain_abs = jnp.swapaxes(gain_all, 0, 1).reshape(2, 3, width)
    gain_abs = by_core(core, gain_abs[0], gain_abs[1])
    base = by_core(core, context, looked)
    moved = dot(jnp.concatenate([base, gain_abs, jnp.zeros((13, width), BF)], axis=0), order)
    stream = moved[:frames]
    gains = moved[frames : frames + 3]

    attn_norm, attn_scale = norm_parts(stream)
    attn_low = group_gather((attn_norm * gains[0]).astype(BF))
    qkv = dot(attn_low, full_in).astype(BF)
    kv_other = core_swap(qkv[:, heads_wide:]).astype(F32)
    query = qkv[:, :heads_wide].astype(F32)
    key_self = qkv[:, heads_wide : 2 * heads_wide].astype(F32)
    val_self = qkv[:, 2 * heads_wide :].astype(F32)
    key_gap = kv_other[:, :heads_wide] - key_self
    val_gap = kv_other[:, heads_wide:] - val_self
    lane_row = lax.broadcasted_iota(jnp.int32, (heads_wide, heads_wide), 0) // HEAD_DIM
    lane_col = lax.broadcasted_iota(jnp.int32, (heads_wide, heads_wide), 1) // HEAD_DIM
    head_sum = (lane_row == lane_col).astype(F32)
    gap = wide_dot(query * key_gap, head_sum) * 0.125
    prob_other = by_core(core, 0.0, jax.nn.sigmoid(gap))
    prob_self = by_core(core, 1.0, jax.nn.sigmoid(-gap))
    attended = (val_self + prob_other * val_gap).astype(BF)
    residual = stream + group_scatter(dot_t(attended, full_out))
    ffn_norm, ffn_scale = norm_parts(residual)
    ffn_low = group_gather((ffn_norm * gains[1]).astype(BF))
    gate_up = dot(ffn_low, full_gate)
    gate, up = gate_up[:, :ffn_wide], gate_up[:, ffn_wide:]
    sig = jax.nn.sigmoid(gate)
    hidden = (gate * sig * up).astype(BF)
    output = residual + group_scatter(dot_t(hidden, full_down))
    head_norm, head_scale = norm_parts(output)
    head_low = group_gather((head_norm * gains[2]).astype(BF))
    logits = dot(head_low, full_head)
    vocab_part = logits.shape[1]
    part_ids = slot * vocab_part + lax.broadcasted_iota(jnp.int32, (1, vocab_part), 1)
    picks = group_targets[:, None] == part_ids
    part_max = jnp.max(logits, axis=-1)
    part_exp = jnp.exp(logits - part_max[:, None])
    part_sum = jnp.sum(part_exp, axis=-1)
    part_target = jnp.sum(jnp.where(picks, logits, 0.0), axis=-1)
    stats = jnp.stack([part_max, part_sum, part_target], axis=0)
    stats = [stats] + [peer_slots(peer(stats, step), step) for step in range(1, TP)]
    row_max = stats[0][0]
    for piece in stats[1:]:
        row_max = jnp.maximum(row_max, piece[0])
    sum_exp = sum(piece[1] * jnp.exp(piece[0] - row_max) for piece in stats)
    target_logit = sum(piece[2] for piece in stats)
    losses = (row_max + jnp.log(sum_exp) - target_logit) * group_mask
    loss_local = jnp.sum(losses[:frames])

    weight_row = group_mask * inverse_count
    factor = jnp.exp(part_max - row_max) / sum_exp
    d_logits = (
        (part_exp * factor[:, None] - picks.astype(F32)) * weight_row[:, None]
    ).astype(BF)
    d_head_in = group_scatter(dot_t(d_logits, full_head))
    grad_head = t_dot(head_low, d_logits)
    d_output, gain_head = norm_back(head_norm, head_scale, gains[2], d_head_in)
    d_output_low = group_gather(d_output.astype(BF))
    d_hidden = dot(d_output_low, full_down)
    d_gate = d_hidden * up * (sig * (1.0 + gate * (1.0 - sig)))
    d_up = d_hidden * (gate * sig)
    d_gate_up = jnp.concatenate([d_gate, d_up], axis=1).astype(BF)
    d_ffn_in = group_scatter(dot_t(d_gate_up, full_gate))
    grad_down = t_dot(d_output_low, hidden)
    grad_gate = t_dot(ffn_low, d_gate_up)
    d_norm_ffn, gain_ffn = norm_back(ffn_norm, ffn_scale, gains[1], d_ffn_in)
    d_residual = d_output + d_norm_ffn
    d_res_low = group_gather(d_residual.astype(BF))
    d_attended = dot(d_res_low, full_out)
    pull = wide_dot(d_attended * val_gap, head_sum)
    d_score = prob_other * prob_self * pull * 0.125
    d_query = d_score * key_gap
    d_key_other = d_score * query
    d_val_other = prob_other * d_attended
    d_kv = core_swap(jnp.concatenate([d_key_other, d_val_other], axis=1).astype(BF)).astype(F32)
    d_key = d_kv[:, :heads_wide] - d_key_other
    d_val = d_kv[:, heads_wide:] + prob_self * d_attended
    d_qkv = jnp.concatenate([d_query, d_key, d_val], axis=1).astype(BF)
    d_attn_in = group_scatter(dot_t(d_qkv, full_in))
    grad_attn = jnp.concatenate([t_dot(attn_low, d_qkv), t_dot(d_res_low, attended)], axis=1)
    d_norm_attn, gain_attn = norm_back(attn_norm, attn_scale, gains[0], d_attn_in)
    d_stream = (d_residual + d_norm_attn).astype(BF)

    gain_rows = jnp.stack([gain_attn, gain_ffn, gain_head]).astype(BF)
    back = jnp.concatenate([d_stream, gain_rows, jnp.zeros((13, width), BF)], axis=0)
    back = dot_t(back, order).astype(BF)
    back = jnp.swapaxes(back.reshape(frames + 16, chips, rows), 0, 1)
    back = lax.all_to_all(back, "dp", 0, 0)
    gain_mine = jnp.sum(back[:, frames : frames + 3].astype(F32), axis=0)
    back_other = core_swap(back)
    gain_theirs = jnp.sum(back_other[:, frames : frames + 3].astype(F32), axis=0)
    grad_gains = jnp.stack(
        [by_core(core, gain_mine, gain_theirs), by_core(core, gain_theirs, gain_mine)]
    )
    d_rows = by_core(core, back_other[:, :frames], back[:, :frames]).reshape(-1, rows)
    grad_embed = t_dot(all_hot, d_rows)

    head_zero, head_one, sq_head = scatter_grad(grad_head, core, low, side)
    down_zero, down_one, sq_down = scatter_grad(grad_down, core, low, side)
    gate_zero, gate_one, sq_gate = scatter_grad(grad_gate, core, low, side)
    attn_zero, attn_one, sq_attn = scatter_grad(grad_attn, core, low, side)
    squares = (
        sq_head
        + sq_down
        + sq_gate
        + sq_attn
        + jnp.sum(grad_embed * grad_embed)
        + jnp.sum(gain_mine * gain_mine)
    )
    tally_lane = lax.broadcasted_iota(jnp.int32, (8, LANE), 1)
    tally = jnp.where(tally_lane == 0, squares, jnp.where(tally_lane == 1, loss_local, 0.0))
    ways = chips * lax.axis_size("mp")
    tally = lax.all_to_all(jnp.broadcast_to(tally[None], (ways, 8, LANE)), ("dp", "mp"), 0, 0)
    tally = jnp.sum(tally[:, 0], axis=0)
    grad_norm = jnp.sqrt(tally[0])
    loss = tally[1] / total_count
    clip_scale = jnp.minimum(1.0, CLIP_NORM / (grad_norm + 1e-06))

    def unpack(zero, one, start, size):
        both = jnp.stack([zero[:, :, start : start + size], one[:, :, start : start + size]])
        return both[:, 0], both[:, 1]

    def join(parts):
        return jnp.concatenate(parts, axis=-1)

    def join_hidden(parts):
        return jnp.concatenate([parts[0], parts[1][..., : ffn_half - ffn_wide]], axis=-1)

    g_in = jnp.stack(
        [join(unpack(attn_zero, attn_one, k * heads_wide, heads_wide)) for k in range(3)], axis=2
    )
    g_out = jnp.swapaxes(join(unpack(attn_zero, attn_one, 3 * heads_wide, heads_wide)), 1, 2)
    g_gate = jnp.stack(
        [join_hidden(unpack(gate_zero, gate_one, k * ffn_wide, ffn_wide)) for k in range(2)], axis=2
    )
    g_down = jnp.swapaxes(join_hidden(unpack(down_zero, down_one, 0, ffn_wide)), 1, 2)
    g_head = join(unpack(head_zero, head_one, 0, vocab_part))
    grads = (g_in, g_out, g_gate, g_down, g_head, grad_embed[None], grad_gains)
    rates = (RATE_MATRIX,) * 5 + (RATE_TABLE, RATE_TABLE)
    updates = [
        adam(weight, first, second, grad.astype(F32) * clip_scale, rate)
        for weight, first, second, grad, rate in zip(params, firsts, seconds, grads, rates)
    ]
    new_weights, new_firsts, new_seconds = zip(*updates)
    return new_weights + new_firsts + new_seconds + (loss, grad_norm)


def solution(mesh):
    weight_specs = (
        P(None, "dp", None, "mp"),
        P(None, "mp", "dp"),
        P(None, "dp", None, "mp"),
        P(None, "mp", "dp"),
        P(None, "dp", "mp"),
        P(None, "mp", "dp"),
        P(None, None, "dp"),
    )
    in_specs = (P("dp", None), P("dp", None, None), P("dp"), P("dp")) + weight_specs * 3
    out_specs = weight_specs * 3 + (P(), P())
    return jax.shard_map(shards, mesh=mesh, in_specs=in_specs, out_specs=out_specs, check_vma=False)
```

time: 2330 us -> 480 us (0.21)
  waiting for transfers between devices: 1900 us -> 179 us
  starting transfers between devices: 1.54 us -> 135 us
  matrix products: 159 us -> 31.8 us
  blocking collectives: 120 us -> 0 us
    reduce_scatter x5 -> x0, waiting for transfers between devices: 1200 us -> none  [the longest x1 472 us: reduce_grads(): lax.psum_scatter(grads[2], 'dp', scatter_dimension=1, tiled=True)]
    all_gather x6 -> x0, waiting for transfers between devices: 460 us -> none  [the longest x1 143 us: fetch(): lax.all_gather(low_params[2], 'dp', axis=1, tiled=True)]
    ppermute x0 -> x85, waiting for transfers between devices: none -> 173 us  [the longest x65 109 us: flip(): lax.ppermute(piece, 'dp', [(chip, chip ^ mask) for chip in range(ways)])]
    unnamed x21 -> x0, waiting for transfers between devices: 172 us -> none
    dot_general x46 -> x21, matrix products: 159 us -> 31.8 us  [the longest x6 11.3 us: t_dot(): lax.dot_general(left, right, (((0,), (0,)), ((), ())), preferred_element_...]
    ppermute x0 -> x85, starting transfers between devices: none -> 108 us  [the longest x65 57.7 us: flip(): lax.ppermute(piece, 'dp', [(chip, chip ^ mask) for chip in range(ways)])]
    psum x3 -> x0, blocking collectives: 81.5 us -> none  [the longest x1 45.2 us: shards(): lax.psum((squares, loss_local / model_ways), ('dp', 'mp'))]
    psum x6 -> x0, waiting for transfers between devices: 70.4 us -> none  [model_sum(): return lax.psum(pieces, 'mp')]
  transfers between devices with their start and end apart: 19 -> 90, of which waited for: 16 -> 34; matrix products, arithmetic and copies ran while one was open for 6% -> 25% of each run, Pallas kernels for 0% -> 0%
where the time goes in v1:
time: 480 us; the launch traced here: 474 us
  waiting for transfers between devices  179 us (37%)
  starting transfers between devices  135 us (28%)
  other arithmetic  59.3 us (12%)
  local copies, waits for them, and re-layouts  57.2 us (12%)
  matrix products  31.8 us (7%)
  between operations  11.3 us (2%)
    ppermute x65, waiting for transfers between devices, flip(): lax.ppermute(piece, 'dp', [(chip, chip ^ mask) for chip in range(ways)])  109 us
    ppermute x65, starting transfers between devices, flip(): lax.ppermute(piece, 'dp', [(chip, chip ^ mask) for chip in range(ways)])  57.7 us
    ppermute x4, waiting for transfers between devices, to_h(): lax.ppermute(piece, 'dp', [(chip, (chip + 8 * step) % ways) for chip in r...  44.1 us
    ppermute x12, starting transfers between devices, core_swap(): return lax.ppermute(piece, 'mp', [(0, 1), (1, 0)])  42.9 us
    unnamed x255, local copies, waits for them, and re-layouts  32.5 us
    ppermute x4, waiting for transfers between devices, from_h(): lax.ppermute(piece, 'dp', [(chip, (chip - 8 * step) % ways) for chip in r...  19.9 us
    dot_general x6, matrix products, t_dot(): lax.dot_general(left, right, (((0,), (0,)), ((), ())), preferred_element_...  11.3 us
    select_n x19, other arithmetic, by_core(): return jnp.where(core == 0, zero, one)  11.1 us
  transfers between devices with their start and end apart: 90, of which 34 were waited for; matrix products, arithmetic and copies ran while one was open for 25% of the time, Pallas kernels for 0%

profile of v1, /device:TPU:1, one launch (start us, length us, event | category | flops | bytes accessed | tf_op | source)
XLA Modules:
  0.0 473.5 jit_solution(454414308082844159)
XLA Ops:
  5.0 7.6 %all-to-all-start.2 = ((bf16[16,2,192]{2,1,0:T(2,128)(2,1)}), bf16[16,2,192]{2,1,0:T(2,128)(2,1)S(1)}, u32[]{:S(2)}, u32[]{:S(2)}) async-start(bf16[16,2,192]{2,1,0:T(2,128)(2,1)} %reshape.631), calls=%async_computation.2 | async-start | bytes 32768 | tf_op jit(solution)/shard_map/all_to_all | solution.py:204
  19.4 6.3 %all-to-all-start = ((s32[16,3,96]{2,1,0:T(4,128)}), s32[16,3,96]{2,1,0:T(4,128)S(1)}, u32[]{:S(2)}, u32[]{:S(2)}) async-start(s32[16,3,96]{2,1,0:T(4,128)} %broadcast_in_dim.91), calls=%async_computation | async-start | bytes 65536 | tf_op jit(solution)/shard_map/all_to_all | solution.py:200
  26.7 5.2 %all-to-all-done = s32[16,3,96]{2,1,0:T(4,128)S(1)} async-done(((s32[16,3,96]{2,1,0:T(4,128)}), s32[16,3,96]{2,1,0:T(4,128)S(1)}, u32[]{:S(2)}, u32[]{:S(2)}) %all-to-all-start) | async-done | bytes 18464 | tf_op jit(solution)/shard_map/all_to_all | solution.py:200
  35.8 1.9 collective-permute-start.38
  38.4 3.0 collective-permute-start.17
  50.9 3.7 all-to-all-start.1
  60.7 2.5 collective-permute-done.6
  63.3 3.8 collective-permute-done.7
  75.5 5.3 %collective-permute-done.19 = bf16[64,1536]{1,0:T(8,128)(2,1)S(1)} collective-permute-done((bf16[64,1536]{1,0:T(8,128)(2,1)S(1)}, bf16[64,1536]{1,0:T(8,128)(2,1)S(1)}, u32[]{:S(2)}, u32[]{:S(2)}) %collective-permute-start.19) | collective-permute-done | bytes 196640 | tf_op jit(solution)/shard_map/ppermute | solution.py:31
  80.7 4.2 collective-permute-done.20
  89.0 3.2 collective-permute-start.21
  94.0 2.1 constant_dynamic-update-slice_fusion
  99.3 1.8 collective-permute-start.3
  101.8 12.5 %collective-permute-done.9 = bf16[512,1024]{1,0:T(8,128)(2,1)S(1)} collective-permute-done((bf16[512,1024]{1,0:T(8,128)(2,1)}, bf16[512,1024]{1,0:T(8,128)(2,1)S(1)}, u32[]{:S(2)}, u32[]{:S(2)}) %collective-permute-start.9) | collective-permute-done | bytes 1048608 | tf_op jit(solution)/shard_map/ppermute | solution.py:31
  116.0 7.7 %collective-permute-start.10 = (bf16[384,512]{1,0:T(8,128)(2,1)S(1)}, bf16[384,512]{1,0:T(8,128)(2,1)S(1)}, u32[]{:S(2)}, u32[]{:S(2)}) collective-permute-start(bf16[384,512]{1,0:T(8,128)(2,1)S(1)} %slice.774), channel_id=1, source_target_pairs={{0,1},{1,0},{2,3},{3,2},{4,5},{5,4},{6,7},{7,6},{8,9},{9,8},{10,11... | collective-permute-start | bytes 1179656 | tf_op jit(solution)/shard_map/ppermute | solution.py:26
  123.7 18.8 %collective-permute-done.27 = bf16[256,768]{1,0:T(8,128)(2,1)S(1)} collective-permute-done((bf16[256,768]{1,0:T(8,128)(2,1)S(1)}, bf16[256,768]{1,0:T(8,128)(2,1)S(1)}, u32[]{:S(2)}, u32[]{:S(2)}) %collective-permute-start.27) | collective-permute-done | bytes 393248 | tf_op jit(solution)/shard_map/ppermute | solution.py:44
  143.5 2.1 constant_dynamic-update-slice_fusion.11
  151.7 7.6 %collective-permute-done.28 = bf16[512,768]{1,0:T(8,128)(2,1)S(1)} collective-permute-done((bf16[512,768]{1,0:T(8,128)(2,1)S(1)}, bf16[512,768]{1,0:T(8,128)(2,1)S(1)}, u32[]{:S(2)}, u32[]{:S(2)}) %collective-permute-start.28) | collective-permute-done | bytes 786464 | tf_op jit(solution)/shard_map/ppermute | solution.py:31
  159.8 1.7 collective-permute-start.14
  162.9 30.1 %collective-permute-done.22 = bf16[512,1536]{1,0:T(8,128)(2,1)S(1)} collective-permute-done((bf16[512,1536]{1,0:T(8,128)(2,1)S(1)}, bf16[512,1536]{1,0:T(8,128)(2,1)S(1)}, u32[]{:S(2)}, u32[]{:S(2)}) %collective-permute-start.22) | collective-permute-done | bytes 1572896 | tf_op jit(solution)/shard_map/ppermute | solution.py:31
  195.7 3.3 fusion.100
  202.8 1.7 collective-permute-start.29
  208.9 2.2 collective-permute-done.31
  211.5 1.5 collective-permute-start.32
  214.4 2.4 collective-permute-done.40
  219.6 2.2 fusion.219
  229.2 2.2 fusion.220
  232.7 1.5 collective-permute-start.46
  234.2 2.0 fusion.98
  237.1 2.3 collective-permute-done.46
  244.3 2.0 collective-permute-done.47
  247.8 4.1 collective-permute-done.49
  253.0 3.4 fusion.221
  259.1 1.8 fusion.38
  268.3 6.1 %collective-permute-done.64 = bf16[256,512]{1,0:T(8,128)(2,1)S(1)} collective-permute-done((bf16[256,512]{1,0:T(8,128)(2,1)S(1)}, bf16[256,512]{1,0:T(8,128)(2,1)S(1)}, u32[]{:S(2)}, u32[]{:S(2)}) %collective-permute-start.64) | collective-permute-done | bytes 262176 | tf_op jit(solution)/shard_map/ppermute | solution.py:49
  275.9 2.0 collective-permute-start.82
  277.9 3.5 collective-permute-done.55
  283.2 13.6 %collective-permute-start.56 = (bf16[384,512]{1,0:T(8,128)(2,1)S(1)}, bf16[384,512]{1,0:T(8,128)(2,1)S(1)}, u32[]{:S(2)}, u32[]{:S(2)}) collective-permute-start(bf16[384,512]{1,0:T(8,128)(2,1)S(1)} %pad_maximum_fusion.15), channel_id=1, source_target_pairs={{0,1},{1,0},{2,3},{3,2},{4,5},{5,4},{6,7},{7,6},{8,9},{9,8},{10,11... | collective-permute-start | bytes 1179656 | tf_op jit(solution)/shard_map/ppermute | solution.py:26
  296.8 3.4 collective-permute-start.84
  304.8 1.6 collective-permute-start.71
  311.0 7.2 %collective-permute-done.71 = bf16[96,1024]{1,0:T(8,128)(2,1)S(1)} collective-permute-done((bf16[96,1024]{1,0:T(8,128)(2,1)S(1)}, bf16[96,1024]{1,0:T(8,128)(2,1)S(1)}, u32[]{:S(2)}, u32[]{:S(2)}) %collective-permute-start.71) | collective-permute-done | bytes 196640 | tf_op jit(solution)/shard_map/ppermute | solution.py:31
  318.7 2.7 concatenate.163
  321.4 2.1 fusion.45
  328.8 4.3 all-to-all-start.3
  336.2 10.9 %collective-permute-start.80 = (bf16[2,64,768]{2,1,0:T(8,128)(2,1)}, bf16[2,64,768]{2,1,0:T(8,128)(2,1)}, u32[]{:S(2)}, u32[]{:S(2)}) collective-permute-start(bf16[2,64,768]{2,1,0:T(8,128)(2,1)} %broadcast_select_fusion.11), channel_id=1, source_target_pairs={{0,1},{1,0},{2,3},{3,2},{4,5},{5,4},{6,7},{7,6},{8,9},{9,8},{10,11... | collective-permute-start | bytes 589832 | tf_op jit(solution)/shard_map/ppermute | solution.py:26
  348.3 1.6 collective-permute-start.57
  355.3 2.8 slice_add_fusion
  358.2 1.7 copy-done.1
  365.0 3.5 multiply_reduce_fusion.13
  368.5 5.5 %collective-permute-done.57 = bf16[512,1024]{1,0:T(8,128)(2,1)} collective-permute-done((bf16[512,1024]{1,0:T(8,128)(2,1)}, bf16[512,1024]{1,0:T(8,128)(2,1)}, u32[]{:S(2)}, u32[]{:S(2)}) %collective-permute-start.57) | collective-permute-done | bytes 1048608 | tf_op jit(solution)/shard_map/ppermute | solution.py:31
  374.0 1.7 fusion.14
  375.8 2.0 collective-permute-start.58
  377.8 31.7 %collective-permute-done.68 = bf16[256,1536]{1,0:T(8,128)(2,1)} collective-permute-done((bf16[256,1536]{1,0:T(8,128)(2,1)}, bf16[256,1536]{1,0:T(8,128)(2,1)}, u32[]{:S(2)}, u32[]{:S(2)}) %collective-permute-start.68) | collective-permute-done | bytes 786464 | tf_op jit(solution)/shard_map/ppermute | solution.py:49
  409.5 2.2 fusion.30
  414.4 6.3 %collective-permute-done.58 = bf16[256,1024]{1,0:T(8,128)(2,1)S(1)} collective-permute-done((bf16[256,1024]{1,0:T(8,128)(2,1)S(1)}, bf16[256,1024]{1,0:T(8,128)(2,1)S(1)}, u32[]{:S(2)}, u32[]{:S(2)}) %collective-permute-start.58) | collective-permute-done | bytes 524320 | tf_op jit(solution)/shard_map/ppermute | solution.py:49
  420.7 2.1 fusion.43
  428.2 5.1 %all-to-all-start.4 = ((f32[32,8,128]{2,1,0:T(8,128)}), f32[32,8,128]{2,1,0:T(8,128)}, u32[]{:S(2)}, u32[]{:S(2)}) async-start(f32[32,8,128]{2,1,0:T(8,128)} %broadcast_in_dim.102), calls=%async_computation.4 | async-start | bytes 262144 | tf_op jit(solution)/shard_map/all_to_all | solution.py:351
  433.3 2.4 collective-permute-start.75
  437.2 5.6 %collective-permute-done.75 = bf16[64,1536]{1,0:T(8,128)(2,1)S(1)} collective-permute-done((bf16[64,1536]{1,0:T(8,128)(2,1)}, bf16[64,1536]{1,0:T(8,128)(2,1)S(1)}, u32[]{:S(2)}, u32[]{:S(2)}) %collective-permute-start.75) | collective-permute-done | bytes 196640 | tf_op jit(solution)/shard_map/ppermute | solution.py:31
  453.2 1.7 multiply_subtract_fusion.2
  459.1 1.8 multiply_subtract_fusion.1
  464.5 2.2 copy.369
  466.7 2.2 copy.370
  468.9 2.2 copy.371
  (607 shorter events, 156.6 us)
Async XLA Ops:
  2.7 43.4 %collective-permute-start.23 = (bf16[2,64,768]{2,1,0:T(8,128)(2,1)}, bf16[2,64,768]{2,1,0:T(8,128)(2,1)}, u32[]{:S(2)}, u32[]{:S(2)}) collective-permute-start(bf16[2,64,768]{2,1,0:T(8,128)(2,1)} %select_bitcast_fusion.8), channel_id=1, source_target_pairs={{0,1},{1,0},{2,3},{3,2},{4,5},{5,4},{6,7},{7,6},{8,9},{9,8},{10,11... | collective-permute-start | bytes 589832 | tf_op jit(solution)/shard_map/ppermute | solution.py:26
  3.8 50.9 %collective-permute-start.4 = (bf16[2,64,1024]{2,1,0:T(8,128)(2,1)}, bf16[2,64,1024]{2,1,0:T(8,128)(2,1)}, u32[]{:S(2)}, u32[]{:S(2)}) collective-permute-start(bf16[2,64,1024]{2,1,0:T(8,128)(2,1)} %select_bitcast_fusion.1), channel_id=1, source_target_pairs={{0,1},{1,0},{2,3},{3,2},{4,5},{5,4},{6,7},{7,6},{8,9},{9,8},{10,11... | collective-permute-start | bytes 786440 | tf_op jit(solution)/shard_map/ppermute | solution.py:26
  5.0 13.8 %all-to-all-start.2 = ((bf16[16,2,192]{2,1,0:T(2,128)(2,1)}), bf16[16,2,192]{2,1,0:T(2,128)(2,1)S(1)}, u32[]{:S(2)}, u32[]{:S(2)}) async-start(bf16[16,2,192]{2,1,0:T(2,128)(2,1)} %reshape.631), calls=%async_computation.2 | async-start | bytes 32768 | tf_op jit(solution)/shard_map/all_to_all | solution.py:204
  13.3 20.6 %collective-permute-start.35 = (bf16[2,64,512]{2,1,0:T(8,128)(2,1)}, bf16[2,64,512]{2,1,0:T(8,128)(2,1)}, u32[]{:S(2)}, u32[]{:S(2)}) collective-permute-start(bf16[2,64,512]{2,1,0:T(8,128)(2,1)} %select_bitcast_fusion.18), channel_id=1, source_target_pairs={{0,1},{1,0},{2,3},{3,2},{4,5},{5,4},{6,7},{7,6},{8,9},{9,8},{10,11... | collective-permute-start | bytes 393224 | tf_op jit(solution)/shard_map/ppermute | solution.py:26
  19.4 12.6 %all-to-all-start = ((s32[16,3,96]{2,1,0:T(4,128)}), s32[16,3,96]{2,1,0:T(4,128)S(1)}, u32[]{:S(2)}, u32[]{:S(2)}) async-start(s32[16,3,96]{2,1,0:T(4,128)} %broadcast_in_dim.91), calls=%async_computation | async-start | bytes 65536 | tf_op jit(solution)/shard_map/all_to_all | solution.py:200
  38.4 31.4 %collective-permute-start.17 = (bf16[2,64,1536]{2,1,0:T(8,128)(2,1)}, bf16[2,64,1536]{2,1,0:T(8,128)(2,1)}, u32[]{:S(2)}, u32[]{:S(2)}) collective-permute-start(bf16[2,64,1536]{2,1,0:T(8,128)(2,1)} %select_bitcast_fusion), channel_id=1, source_target_pairs={{0,1},{1,0},{2,3},{3,2},{4,5},{5,4},{6,7},{7,6},{8,9},{9,8},{10,11... | collective-permute-start | bytes 1179656 | tf_op jit(solution)/shard_map/ppermute | solution.py:26
  47.1 9.9 %collective-permute-start.24 = (bf16[64,768]{1,0:T(8,128)(2,1)S(1)}, bf16[64,768]{1,0:T(8,128)(2,1)S(1)}, u32[]{:S(2)}, u32[]{:S(2)}) collective-permute-start(bf16[64,768]{1,0:T(8,128)(2,1)S(1)} %get-tuple-element.375), channel_id=1, source_target_pairs={{0,2},{2,0},{4,6},{6,4},{8,10},{10,8},{12,14},{14,12},{16,18},{18,... | collective-permute-start | bytes 294920 | tf_op jit(solution)/shard_map/ppermute | solution.py:31
  48.2 10.0 %collective-permute-start.25 = (bf16[64,768]{1,0:T(8,128)(2,1)S(1)}, bf16[64,768]{1,0:T(8,128)(2,1)S(1)}, u32[]{:S(2)}, u32[]{:S(2)}) collective-permute-start(bf16[64,768]{1,0:T(8,128)(2,1)S(1)} %get-tuple-element.249), channel_id=1, source_target_pairs={{0,8},{2,10},{4,12},{6,14},{8,0},{10,2},{12,4},{14,6},{16,24},{18,... | collective-permute-start | bytes 294920 | tf_op jit(solution)/shard_map/ppermute | solution.py:31
  48.6 9.9 %collective-permute-start.26 = (bf16[64,768]{1,0:T(8,128)(2,1)S(1)}, bf16[64,768]{1,0:T(8,128)(2,1)S(1)}, u32[]{:S(2)}, u32[]{:S(2)}) collective-permute-start(bf16[64,768]{1,0:T(8,128)(2,1)S(1)} %get-tuple-element.376), channel_id=1, source_target_pairs={{0,10},{2,8},{4,14},{6,12},{8,2},{10,0},{12,6},{14,4},{16,26},{18,... | collective-permute-start | bytes 294920 | tf_op jit(solution)/shard_map/ppermute | solution.py:31
  50.9 41.9 %all-to-all-start.1 = ((bf16[16,96,64]{1,2,0:T(8,128)(2,1)}), bf16[16,96,64]{1,2,0:T(8,128)(2,1)S(1)}, u32[]{:S(2)}, u32[]{:S(2)}) async-start(bf16[16,96,64]{1,2,0:T(8,128)(2,1)} %copy.330), calls=%async_computation.1 | async-start | bytes 524288 | tf_op jit(solution)/shard_map/all_to_all | solution.py:235
  58.2 8.8 %collective-permute-start.7 = (bf16[64,1024]{1,0:T(8,128)(2,1)S(1)}, bf16[64,1024]{1,0:T(8,128)(2,1)S(1)}, u32[]{:S(2)}, u32[]{:S(2)}) collective-permute-start(bf16[64,1024]{1,0:T(8,128)(2,1)S(1)} %get-tuple-element.351), channel_id=1, source_target_pairs={{0,10},{2,8},{4,14},{6,12},{8,2},{10,0},{12,6},{14,4},{16,26},{18,... | collective-permute-start | bytes 393224 | tf_op jit(solution)/shard_map/ppermute | solution.py:31
  68.4 25.6 %collective-permute-start.8 = (bf16[256,1024]{1,0:T(8,128)(2,1)}, bf16[256,1024]{1,0:T(8,128)(2,1)}, u32[]{:S(2)}, u32[]{:S(2)}) collective-permute-start(bf16[256,1024]{1,0:T(8,128)(2,1)} %pad_maximum_fusion.12), channel_id=1, source_target_pairs={{0,16},{2,18},{4,20},{6,22},{8,24},{10,26},{12,28},{14,30},{16,0},... | collective-permute-start | bytes 1572872 | tf_op jit(solution)/shard_map/ppermute | solution.py:44
  71.9 8.9 %collective-permute-start.19 = (bf16[64,1536]{1,0:T(8,128)(2,1)S(1)}, bf16[64,1536]{1,0:T(8,128)(2,1)S(1)}, u32[]{:S(2)}, u32[]{:S(2)}) collective-permute-start(bf16[64,1536]{1,0:T(8,128)(2,1)S(1)} %get-tuple-element.262), channel_id=1, source_target_pairs={{0,8},{2,10},{4,12},{6,14},{8,0},{10,2},{12,4},{14,6},{16,24},{18,... | collective-permute-start | bytes 589832 | tf_op jit(solution)/shard_map/ppermute | solution.py:31
  73.1 11.9 %collective-permute-start.20 = (bf16[64,1536]{1,0:T(8,128)(2,1)S(1)}, bf16[64,1536]{1,0:T(8,128)(2,1)S(1)}, u32[]{:S(2)}, u32[]{:S(2)}) collective-permute-start(bf16[64,1536]{1,0:T(8,128)(2,1)S(1)} %get-tuple-element.327), channel_id=1, source_target_pairs={{0,10},{2,8},{4,14},{6,12},{8,2},{10,0},{12,6},{14,4},{16,26},{18,... | collective-permute-start | bytes 589832 | tf_op jit(solution)/shard_map/ppermute | solution.py:31
  89.0 54.4 %collective-permute-start.21 = (bf16[256,1536]{1,0:T(8,128)(2,1)}, bf16[256,1536]{1,0:T(8,128)(2,1)}, u32[]{:S(2)}, u32[]{:S(2)}) collective-permute-start(bf16[256,1536]{1,0:T(8,128)(2,1)} %pad_maximum_fusion.4), channel_id=1, source_target_pairs={{0,16},{2,18},{4,20},{6,22},{8,24},{10,26},{12,28},{14,30},{16,0},... | collective-permute-start | bytes 2359304 | tf_op jit(solution)/shard_map/ppermute | solution.py:44
  96.1 18.1 %collective-permute-start.9 = (bf16[512,1024]{1,0:T(8,128)(2,1)}, bf16[512,1024]{1,0:T(8,128)(2,1)S(1)}, u32[]{:S(2)}, u32[]{:S(2)}) collective-permute-start(bf16[512,1024]{1,0:T(8,128)(2,1)} %get-tuple-element.348), channel_id=1, source_target_pairs={{0,4},{2,6},{4,0},{6,2},{8,12},{10,14},{12,8},{14,10},{16,20},{18,... | collective-permute-start | bytes 3145736 | tf_op jit(solution)/shard_map/ppermute | solution.py:31
  98.4 16.0 %collective-permute-start.1 = (bf16[96,1024]{1,0:T(8,128)(2,1)S(1)}, bf16[96,1024]{1,0:T(8,128)(2,1)S(1)}, u32[]{:S(2)}, u32[]{:S(2)}) collective-permute-start(bf16[96,1024]{1,0:T(8,128)(2,1)S(1)} %multiply_convert_fusion.7), channel_id=1, source_target_pairs={{0,2},{2,0},{4,6},{6,4},{8,10},{10,8},{12,14},{14,12},{16,18},{18,... | collective-permute-start | bytes 589832 | tf_op jit(solution)/shard_map/ppermute | solution.py:31
  99.3 15.1 %collective-permute-start.2 = (bf16[96,1024]{1,0:T(8,128)(2,1)S(1)}, bf16[96,1024]{1,0:T(8,128)(2,1)S(1)}, u32[]{:S(2)}, u32[]{:S(2)}) collective-permute-start(bf16[96,1024]{1,0:T(8,128)(2,1)S(1)} %multiply_convert_fusion.7), channel_id=1, source_target_pairs={{0,8},{2,10},{4,12},{6,14},{8,0},{10,2},{12,4},{14,6},{16,24},{18,... | collective-permute-start | bytes 589832 | tf_op jit(solution)/shard_map/ppermute | solution.py:31
  99.3 15.2 %collective-permute-start.3 = (bf16[96,1024]{1,0:T(8,128)(2,1)S(1)}, bf16[96,1024]{1,0:T(8,128)(2,1)S(1)}, u32[]{:S(2)}, u32[]{:S(2)}) collective-permute-start(bf16[96,1024]{1,0:T(8,128)(2,1)S(1)} %multiply_convert_fusion.7), channel_id=1, source_target_pairs={{0,10},{2,8},{4,14},{6,12},{8,2},{10,0},{12,6},{14,4},{16,26},{18,... | collective-permute-start | bytes 589832 | tf_op jit(solution)/shard_map/ppermute | solution.py:31
  114.3 28.3 %collective-permute-start.27 = (bf16[256,768]{1,0:T(8,128)(2,1)S(1)}, bf16[256,768]{1,0:T(8,128)(2,1)S(1)}, u32[]{:S(2)}, u32[]{:S(2)}) collective-permute-start(bf16[256,768]{1,0:T(8,128)(2,1)S(1)} %copy-done.44), channel_id=1, source_target_pairs={{0,16},{2,18},{4,20},{6,22},{8,24},{10,26},{12,28},{14,30},{16,0},... | collective-permute-start | bytes 1179656 | tf_op jit(solution)/shard_map/ppermute | solution.py:44
  116.0 30.3 %collective-permute-start.10 = (bf16[384,512]{1,0:T(8,128)(2,1)S(1)}, bf16[384,512]{1,0:T(8,128)(2,1)S(1)}, u32[]{:S(2)}, u32[]{:S(2)}) collective-permute-start(bf16[384,512]{1,0:T(8,128)(2,1)S(1)} %slice.774), channel_id=1, source_target_pairs={{0,1},{1,0},{2,3},{3,2},{4,5},{5,4},{6,7},{7,6},{8,9},{9,8},{10,11... | collective-permute-start | bytes 1179656 | tf_op jit(solution)/shard_map/ppermute | solution.py:26
  142.6 16.7 %collective-permute-start.28 = (bf16[512,768]{1,0:T(8,128)(2,1)S(1)}, bf16[512,768]{1,0:T(8,128)(2,1)S(1)}, u32[]{:S(2)}, u32[]{:S(2)}) collective-permute-start(bf16[512,768]{1,0:T(8,128)(2,1)S(1)} %get-tuple-element.373), channel_id=1, source_target_pairs={{0,4},{2,6},{4,0},{6,2},{8,12},{10,14},{12,8},{14,10},{16,20},{18,... | collective-permute-start | bytes 2359304 | tf_op jit(solution)/shard_map/ppermute | solution.py:31
  145.6 47.4 %collective-permute-start.22 = (bf16[512,1536]{1,0:T(8,128)(2,1)S(1)}, bf16[512,1536]{1,0:T(8,128)(2,1)S(1)}, u32[]{:S(2)}, u32[]{:S(2)}) collective-permute-start(bf16[512,1536]{1,0:T(8,128)(2,1)S(1)} %get-tuple-element.324), channel_id=1, source_target_pairs={{0,4},{2,6},{4,0},{6,2},{8,12},{10,14},{12,8},{14,10},{16,20},{18,... | collective-permute-start | bytes 4718600 | tf_op jit(solution)/shard_map/ppermute | solution.py:31
  148.4 10.9 %collective-permute-start.11 = (bf16[96,1024]{1,0:T(8,128)(2,1)S(1)}, bf16[96,1024]{1,0:T(8,128)(2,1)S(1)}, u32[]{:S(2)}, u32[]{:S(2)}) collective-permute-start(bf16[96,1024]{1,0:T(8,128)(2,1)S(1)} %get-tuple-element.328), channel_id=1, source_target_pairs={{0,2},{2,0},{4,6},{6,4},{8,10},{10,8},{12,14},{14,12},{16,18},{18,... | collective-permute-start | bytes 589832 | tf_op jit(solution)/shard_map/ppermute | solution.py:31
  149.7 9.6 %collective-permute-start.12 = (bf16[96,1024]{1,0:T(8,128)(2,1)S(1)}, bf16[96,1024]{1,0:T(8,128)(2,1)S(1)}, u32[]{:S(2)}, u32[]{:S(2)}) collective-permute-start(bf16[96,1024]{1,0:T(8,128)(2,1)S(1)} %get-tuple-element.330), channel_id=1, source_target_pairs={{0,8},{2,10},{4,12},{6,14},{8,0},{10,2},{12,4},{14,6},{16,24},{18,... | collective-permute-start | bytes 589832 | tf_op jit(solution)/shard_map/ppermute | solution.py:31
  149.7 9.7 %collective-permute-start.13 = (bf16[96,1024]{1,0:T(8,128)(2,1)S(1)}, bf16[96,1024]{1,0:T(8,128)(2,1)S(1)}, u32[]{:S(2)}, u32[]{:S(2)}) collective-permute-start(bf16[96,1024]{1,0:T(8,128)(2,1)S(1)} %get-tuple-element.329), channel_id=1, source_target_pairs={{0,10},{2,8},{4,14},{6,12},{8,2},{10,0},{12,6},{14,4},{16,26},{18,... | collective-permute-start | bytes 589832 | tf_op jit(solution)/shard_map/ppermute | solution.py:31
  159.3 47.0 %collective-permute-start.39 = (bf16[256,512]{1,0:T(8,128)(2,1)S(1)}, bf16[256,512]{1,0:T(8,128)(2,1)S(1)}, u32[]{:S(2)}, u32[]{:S(2)}) collective-permute-start(bf16[256,512]{1,0:T(8,128)(2,1)S(1)} %copy-done.48), channel_id=1, source_target_pairs={{0,16},{2,18},{4,20},{6,22},{8,24},{10,26},{12,28},{14,30},{16,0},... | collective-permute-start | bytes 786440 | tf_op jit(solution)/shard_map/ppermute | solution.py:44
  159.8 34.5 %collective-permute-start.14 = (bf16[96,1024]{1,0:T(8,128)(2,1)S(1)}, bf16[96,1024]{1,0:T(8,128)(2,1)S(1)}, u32[]{:S(2)}, u32[]{:S(2)}) collective-permute-start(bf16[96,1024]{1,0:T(8,128)(2,1)S(1)} %multiply_convert_fusion.6), channel_id=1, source_target_pairs={{0,2},{2,0},{4,6},{6,4},{8,10},{10,8},{12,14},{14,12},{16,18},{18,... | collective-permute-start | bytes 589832 | tf_op jit(solution)/shard_map/ppermute | solution.py:31
  161.4 32.9 %collective-permute-start.15 = (bf16[96,1024]{1,0:T(8,128)(2,1)S(1)}, bf16[96,1024]{1,0:T(8,128)(2,1)S(1)}, u32[]{:S(2)}, u32[]{:S(2)}) collective-permute-start(bf16[96,1024]{1,0:T(8,128)(2,1)S(1)} %multiply_convert_fusion.6), channel_id=1, source_target_pairs={{0,8},{2,10},{4,12},{6,14},{8,0},{10,2},{12,4},{14,6},{16,24},{18,... | collective-permute-start | bytes 589832 | tf_op jit(solution)/shard_map/ppermute | solution.py:31
  162.9 31.5 %collective-permute-start.16 = (bf16[96,1024]{1,0:T(8,128)(2,1)S(1)}, bf16[96,1024]{1,0:T(8,128)(2,1)S(1)}, u32[]{:S(2)}, u32[]{:S(2)}) collective-permute-start(bf16[96,1024]{1,0:T(8,128)(2,1)S(1)} %multiply_convert_fusion.6), channel_id=1, source_target_pairs={{0,10},{2,8},{4,14},{6,12},{8,2},{10,0},{12,6},{14,4},{16,26},{18,... | collective-permute-start | bytes 589832 | tf_op jit(solution)/shard_map/ppermute | solution.py:31
  207.2 9.7 %collective-permute-start.40 = (bf16[512,512]{1,0:T(8,128)(2,1)}, bf16[512,512]{1,0:T(8,128)(2,1)S(1)}, u32[]{:S(2)}, u32[]{:S(2)}) collective-permute-start(bf16[512,512]{1,0:T(8,128)(2,1)} %get-tuple-element.395), channel_id=1, source_target_pairs={{0,4},{2,6},{4,0},{6,2},{8,12},{10,14},{12,8},{14,10},{16,20},{18,... | collective-permute-start | bytes 1572872 | tf_op jit(solution)/shard_map/ppermute | solution.py:31
  236.4 27.7 %collective-permute-start.63 = (bf16[512,512]{1,0:T(8,128)(2,1)S(1)}, bf16[512,512]{1,0:T(8,128)(2,1)S(1)}, u32[]{:S(2)}, u32[]{:S(2)}) collective-permute-start(bf16[512,512]{1,0:T(8,128)(2,1)S(1)} %slice.1409), channel_id=1, source_target_pairs={{0,4},{2,6},{4,0},{6,2},{8,12},{10,14},{12,8},{14,10},{16,20},{18,... | collective-permute-start | bytes 1572872 | tf_op jit(solution)/shard_map/ppermute | solution.py:31
  241.1 10.8 %collective-permute-start.49 = (bf16[96,1024]{1,0:T(8,128)(2,1)S(1)}, bf16[96,1024]{1,0:T(8,128)(2,1)S(1)}, u32[]{:S(2)}, u32[]{:S(2)}) collective-permute-start(bf16[96,1024]{1,0:T(8,128)(2,1)S(1)} %fusion.182), channel_id=1, source_target_pairs={{0,10},{2,8},{4,14},{6,12},{8,2},{10,0},{12,6},{14,4},{16,26},{18,... | collective-permute-start | bytes 589832 | tf_op jit(solution)/shard_map/ppermute | solution.py:31
  256.4 8.9 %collective-permute-start.50 = (bf16[96,1024]{1,0:T(8,128)(2,1)S(1)}, bf16[96,1024]{1,0:T(8,128)(2,1)S(1)}, u32[]{:S(2)}, u32[]{:S(2)}) collective-permute-start(bf16[96,1024]{1,0:T(8,128)(2,1)S(1)} %get-tuple-element.315), channel_id=1, source_target_pairs={{0,2},{2,0},{4,6},{6,4},{8,10},{10,8},{12,14},{14,12},{16,18},{18,... | collective-permute-start | bytes 589832 | tf_op jit(solution)/shard_map/ppermute | solution.py:31
  257.1 9.3 %collective-permute-start.51 = (bf16[96,1024]{1,0:T(8,128)(2,1)S(1)}, bf16[96,1024]{1,0:T(8,128)(2,1)S(1)}, u32[]{:S(2)}, u32[]{:S(2)}) collective-permute-start(bf16[96,1024]{1,0:T(8,128)(2,1)S(1)} %get-tuple-element.317), channel_id=1, source_target_pairs={{0,8},{2,10},{4,12},{6,14},{8,0},{10,2},{12,4},{14,6},{16,24},{18,... | collective-permute-start | bytes 589832 | tf_op jit(solution)/shard_map/ppermute | solution.py:31
  257.8 8.6 %collective-permute-start.52 = (bf16[96,1024]{1,0:T(8,128)(2,1)S(1)}, bf16[96,1024]{1,0:T(8,128)(2,1)S(1)}, u32[]{:S(2)}, u32[]{:S(2)}) collective-permute-start(bf16[96,1024]{1,0:T(8,128)(2,1)S(1)} %get-tuple-element.316), channel_id=1, source_target_pairs={{0,10},{2,8},{4,14},{6,12},{8,2},{10,0},{12,6},{14,4},{16,26},{18,... | collective-permute-start | bytes 589832 | tf_op jit(solution)/shard_map/ppermute | solution.py:31
  262.4 92.9 %collective-permute-start.67 = (bf16[512,1536]{1,0:T(8,128)(2,1)}, bf16[512,1536]{1,0:T(8,128)(2,1)}, u32[]{:S(2)}, u32[]{:S(2)}) collective-permute-start(bf16[512,1536]{1,0:T(8,128)(2,1)} %slice.1406), channel_id=1, source_target_pairs={{0,4},{2,6},{4,0},{6,2},{8,12},{10,14},{12,8},{14,10},{16,20},{18,... | collective-permute-start | bytes 4718600 | tf_op jit(solution)/shard_map/ppermute | solution.py:31
  264.1 42.4 %collective-permute-start.65 = (bf16[512,768]{1,0:T(8,128)(2,1)S(1)}, bf16[512,768]{1,0:T(8,128)(2,1)S(1)}, u32[]{:S(2)}, u32[]{:S(2)}) collective-permute-start(bf16[512,768]{1,0:T(8,128)(2,1)S(1)} %slice.1408), channel_id=1, source_target_pairs={{0,4},{2,6},{4,0},{6,2},{8,12},{10,14},{12,8},{14,10},{16,20},{18,... | collective-permute-start | bytes 2359304 | tf_op jit(solution)/shard_map/ppermute | solution.py:31
  265.3 9.1 %collective-permute-start.64 = (bf16[256,512]{1,0:T(8,128)(2,1)S(1)}, bf16[256,512]{1,0:T(8,128)(2,1)S(1)}, u32[]{:S(2)}, u32[]{:S(2)}) collective-permute-start(bf16[256,512]{1,0:T(8,128)(2,1)S(1)} %slice.1412), channel_id=1, source_target_pairs={{0,16},{2,18},{4,20},{6,22},{8,24},{10,26},{12,28},{14,30},{16,0},... | collective-permute-start | bytes 786440 | tf_op jit(solution)/shard_map/ppermute | solution.py:49
  266.9 8.3 %collective-permute-start.53 = (bf16[96,1024]{1,0:T(8,128)(2,1)S(1)}, bf16[96,1024]{1,0:T(8,128)(2,1)S(1)}, u32[]{:S(2)}, u32[]{:S(2)}) collective-permute-start(bf16[96,1024]{1,0:T(8,128)(2,1)S(1)} %get-tuple-element.235), channel_id=1, source_target_pairs={{0,2},{2,0},{4,6},{6,4},{8,10},{10,8},{12,14},{14,12},{16,18},{18,... | collective-permute-start | bytes 589832 | tf_op jit(solution)/shard_map/ppermute | solution.py:31
  267.6 8.3 %collective-permute-start.54 = (bf16[96,1024]{1,0:T(8,128)(2,1)S(1)}, bf16[96,1024]{1,0:T(8,128)(2,1)S(1)}, u32[]{:S(2)}, u32[]{:S(2)}) collective-permute-start(bf16[96,1024]{1,0:T(8,128)(2,1)S(1)} %get-tuple-element.235), channel_id=1, source_target_pairs={{0,8},{2,10},{4,12},{6,14},{8,0},{10,2},{12,4},{14,6},{16,24},{18,... | collective-permute-start | bytes 589832 | tf_op jit(solution)/shard_map/ppermute | solution.py:31
  275.2 8.0 %collective-permute-start.81 = (bf16[64,512]{1,0:T(8,128)(2,1)S(1)}, bf16[64,512]{1,0:T(8,128)(2,1)S(1)}, u32[]{:S(2)}, u32[]{:S(2)}) collective-permute-start(bf16[64,512]{1,0:T(8,128)(2,1)S(1)} %get-tuple-element.385), channel_id=1, source_target_pairs={{0,2},{2,0},{4,6},{6,4},{8,10},{10,8},{12,14},{14,12},{16,18},{18,... | collective-permute-start | bytes 196616 | tf_op jit(solution)/shard_map/ppermute | solution.py:31
  275.9 20.8 %collective-permute-start.82 = (bf16[64,512]{1,0:T(8,128)(2,1)S(1)}, bf16[64,512]{1,0:T(8,128)(2,1)S(1)}, u32[]{:S(2)}, u32[]{:S(2)}) collective-permute-start(bf16[64,512]{1,0:T(8,128)(2,1)S(1)} %get-tuple-element.210), channel_id=1, source_target_pairs={{0,8},{2,10},{4,12},{6,14},{8,0},{10,2},{12,4},{14,6},{16,24},{18,... | collective-permute-start | bytes 196616 | tf_op jit(solution)/shard_map/ppermute | solution.py:31
  281.4 15.3 %collective-permute-start.83 = (bf16[64,512]{1,0:T(8,128)(2,1)S(1)}, bf16[64,512]{1,0:T(8,128)(2,1)S(1)}, u32[]{:S(2)}, u32[]{:S(2)}) collective-permute-start(bf16[64,512]{1,0:T(8,128)(2,1)S(1)} %get-tuple-element.386), channel_id=1, source_target_pairs={{0,10},{2,8},{4,14},{6,12},{8,2},{10,0},{12,6},{14,4},{16,26},{18,... | collective-permute-start | bytes 196616 | tf_op jit(solution)/shard_map/ppermute | solution.py:31
  283.2 19.3 %collective-permute-start.56 = (bf16[384,512]{1,0:T(8,128)(2,1)S(1)}, bf16[384,512]{1,0:T(8,128)(2,1)S(1)}, u32[]{:S(2)}, u32[]{:S(2)}) collective-permute-start(bf16[384,512]{1,0:T(8,128)(2,1)S(1)} %pad_maximum_fusion.15), channel_id=1, source_target_pairs={{0,1},{1,0},{2,3},{3,2},{4,5},{5,4},{6,7},{7,6},{8,9},{9,8},{10,11... | collective-permute-start | bytes 1179656 | tf_op jit(solution)/shard_map/ppermute | solution.py:26
  304.8 13.3 %collective-permute-start.71 = (bf16[96,1024]{1,0:T(8,128)(2,1)S(1)}, bf16[96,1024]{1,0:T(8,128)(2,1)S(1)}, u32[]{:S(2)}, u32[]{:S(2)}) collective-permute-start(bf16[96,1024]{1,0:T(8,128)(2,1)S(1)} %get-tuple-element.313), channel_id=1, source_target_pairs={{0,10},{2,8},{4,14},{6,12},{8,2},{10,0},{12,6},{14,4},{16,26},{18,... | collective-permute-start | bytes 589832 | tf_op jit(solution)/shard_map/ppermute | solution.py:31
  308.6 12.8 %collective-permute-start.66 = (bf16[256,768]{1,0:T(8,128)(2,1)}, bf16[256,768]{1,0:T(8,128)(2,1)}, u32[]{:S(2)}, u32[]{:S(2)}) collective-permute-start(bf16[256,768]{1,0:T(8,128)(2,1)} %slice.1411), channel_id=1, source_target_pairs={{0,16},{2,18},{4,20},{6,22},{8,24},{10,26},{12,28},{14,30},{16,0},... | collective-permute-start | bytes 1179656 | tf_op jit(solution)/shard_map/ppermute | solution.py:49
  324.3 8.9 %collective-permute-start.77 = (bf16[64,768]{1,0:T(8,128)(2,1)}, bf16[64,768]{1,0:T(8,128)(2,1)S(1)}, u32[]{:S(2)}, u32[]{:S(2)}) collective-permute-start(bf16[64,768]{1,0:T(8,128)(2,1)} %get-tuple-element.363), channel_id=1, source_target_pairs={{0,2},{2,0},{4,6},{6,4},{8,10},{10,8},{12,14},{14,12},{16,18},{18,... | collective-permute-start | bytes 294920 | tf_op jit(solution)/shard_map/ppermute | solution.py:31
  325.6 7.8 %collective-permute-start.79 = (bf16[64,768]{1,0:T(8,128)(2,1)}, bf16[64,768]{1,0:T(8,128)(2,1)}, u32[]{:S(2)}, u32[]{:S(2)}) collective-permute-start(bf16[64,768]{1,0:T(8,128)(2,1)} %get-tuple-element.364), channel_id=1, source_target_pairs={{0,10},{2,8},{4,14},{6,12},{8,2},{10,0},{12,6},{14,4},{16,26},{18,... | collective-permute-start | bytes 294920 | tf_op jit(solution)/shard_map/ppermute | solution.py:31
  328.8 22.5 %all-to-all-start.3 = ((bf16[16,112,64]{1,2,0:T(8,128)(2,1)}), bf16[16,112,64]{1,2,0:T(8,128)(2,1)S(1)}, u32[]{:S(2)}, u32[]{:S(2)}) async-start(bf16[16,112,64]{1,2,0:T(8,128)(2,1)} %bitcast.342), calls=%async_computation.3 | async-start | bytes 524288 | tf_op jit(solution)/shard_map/all_to_all | solution.py:326
  336.2 16.6 %collective-permute-start.80 = (bf16[2,64,768]{2,1,0:T(8,128)(2,1)}, bf16[2,64,768]{2,1,0:T(8,128)(2,1)}, u32[]{:S(2)}, u32[]{:S(2)}) collective-permute-start(bf16[2,64,768]{2,1,0:T(8,128)(2,1)} %broadcast_select_fusion.11), channel_id=1, source_target_pairs={{0,1},{1,0},{2,3},{3,2},{4,5},{5,4},{6,7},{7,6},{8,9},{9,8},{10,11... | collective-permute-start | bytes 589832 | tf_op jit(solution)/shard_map/ppermute | solution.py:26
  348.3 25.7 %collective-permute-start.57 = (bf16[512,1024]{1,0:T(8,128)(2,1)}, bf16[512,1024]{1,0:T(8,128)(2,1)}, u32[]{:S(2)}, u32[]{:S(2)}) collective-permute-start(bf16[512,1024]{1,0:T(8,128)(2,1)} %fusion.15), channel_id=1, source_target_pairs={{0,4},{2,6},{4,0},{6,2},{8,12},{10,14},{12,8},{14,10},{16,20},{18,... | collective-permute-start | bytes 3145736 | tf_op jit(solution)/shard_map/ppermute | solution.py:31
  351.2 10.6 %collective-permute-start.72 = (bf16[16,112,64]{1,2,0:T(8,128)(2,1)S(1)}, bf16[16,112,64]{1,2,0:T(8,128)(2,1)S(1)}, u32[]{:S(2)}, u32[]{:S(2)}) collective-permute-start(bf16[16,112,64]{1,2,0:T(8,128)(2,1)S(1)} %all-to-all-done.3), channel_id=1, source_target_pairs={{0,1},{1,0},{2,3},{3,2},{4,5},{5,4},{6,7},{7,6},{8,9},{9,8},{10,11... | collective-permute-start | bytes 688136 | tf_op jit(solution)/shard_map/ppermute | solution.py:26
  360.8 48.7 %collective-permute-start.68 = (bf16[256,1536]{1,0:T(8,128)(2,1)}, bf16[256,1536]{1,0:T(8,128)(2,1)}, u32[]{:S(2)}, u32[]{:S(2)}) collective-permute-start(bf16[256,1536]{1,0:T(8,128)(2,1)} %slice.1407), channel_id=1, source_target_pairs={{0,16},{2,18},{4,20},{6,22},{8,24},{10,26},{12,28},{14,30},{16,0},... | collective-permute-start | bytes 2359304 | tf_op jit(solution)/shard_map/ppermute | solution.py:49
  375.8 44.9 %collective-permute-start.58 = (bf16[256,1024]{1,0:T(8,128)(2,1)S(1)}, bf16[256,1024]{1,0:T(8,128)(2,1)S(1)}, u32[]{:S(2)}, u32[]{:S(2)}) collective-permute-start(bf16[256,1024]{1,0:T(8,128)(2,1)S(1)} %slice.1410), channel_id=1, source_target_pairs={{0,16},{2,18},{4,20},{6,22},{8,24},{10,26},{12,28},{14,30},{16,0},... | collective-permute-start | bytes 1572872 | tf_op jit(solution)/shard_map/ppermute | solution.py:49
  412.6 24.6 %collective-permute-start.73 = (bf16[64,1536]{1,0:T(8,128)(2,1)}, bf16[64,1536]{1,0:T(8,128)(2,1)S(1)}, u32[]{:S(2)}, u32[]{:S(2)}) collective-permute-start(bf16[64,1536]{1,0:T(8,128)(2,1)} %get-tuple-element.308), channel_id=1, source_target_pairs={{0,2},{2,0},{4,6},{6,4},{8,10},{10,8},{12,14},{14,12},{16,18},{18,... | collective-permute-start | bytes 589832 | tf_op jit(solution)/shard_map/ppermute | solution.py:31
  413.7 23.5 %collective-permute-start.74 = (bf16[64,1536]{1,0:T(8,128)(2,1)}, bf16[64,1536]{1,0:T(8,128)(2,1)}, u32[]{:S(2)}, u32[]{:S(2)}) collective-permute-start(bf16[64,1536]{1,0:T(8,128)(2,1)} %get-tuple-element.222), channel_id=1, source_target_pairs={{0,8},{2,10},{4,12},{6,14},{8,0},{10,2},{12,4},{14,6},{16,24},{18,... | collective-permute-start | bytes 589832 | tf_op jit(solution)/shard_map/ppermute | solution.py:31
  422.8 10.5 %collective-permute-start.59 = (bf16[64,1024]{1,0:T(8,128)(2,1)S(1)}, bf16[64,1024]{1,0:T(8,128)(2,1)S(1)}, u32[]{:S(2)}, u32[]{:S(2)}) collective-permute-start(bf16[64,1024]{1,0:T(8,128)(2,1)S(1)} %get-tuple-element.346), channel_id=1, source_target_pairs={{0,2},{2,0},{4,6},{6,4},{8,10},{10,8},{12,14},{14,12},{16,18},{18,... | collective-permute-start | bytes 393224 | tf_op jit(solution)/shard_map/ppermute | solution.py:31
  424.1 11.6 %collective-permute-start.60 = (bf16[64,1024]{1,0:T(8,128)(2,1)S(1)}, bf16[64,1024]{1,0:T(8,128)(2,1)S(1)}, u32[]{:S(2)}, u32[]{:S(2)}) collective-permute-start(bf16[64,1024]{1,0:T(8,128)(2,1)S(1)} %get-tuple-element.231), channel_id=1, source_target_pairs={{0,8},{2,10},{4,12},{6,14},{8,0},{10,2},{12,4},{14,6},{16,24},{18,... | collective-permute-start | bytes 393224 | tf_op jit(solution)/shard_map/ppermute | solution.py:31
  424.1 11.6 %collective-permute-start.61 = (bf16[64,1024]{1,0:T(8,128)(2,1)S(1)}, bf16[64,1024]{1,0:T(8,128)(2,1)S(1)}, u32[]{:S(2)}, u32[]{:S(2)}) collective-permute-start(bf16[64,1024]{1,0:T(8,128)(2,1)S(1)} %get-tuple-element.347), channel_id=1, source_target_pairs={{0,10},{2,8},{4,14},{6,12},{8,2},{10,0},{12,6},{14,4},{16,26},{18,... | collective-permute-start | bytes 393224 | tf_op jit(solution)/shard_map/ppermute | solution.py:31
  428.2 17.3 %all-to-all-start.4 = ((f32[32,8,128]{2,1,0:T(8,128)}), f32[32,8,128]{2,1,0:T(8,128)}, u32[]{:S(2)}, u32[]{:S(2)}) async-start(f32[32,8,128]{2,1,0:T(8,128)} %broadcast_in_dim.102), calls=%async_computation.4 | async-start | bytes 262144 | tf_op jit(solution)/shard_map/all_to_all | solution.py:351
  433.3 9.5 %collective-permute-start.75 = (bf16[64,1536]{1,0:T(8,128)(2,1)}, bf16[64,1536]{1,0:T(8,128)(2,1)S(1)}, u32[]{:S(2)}, u32[]{:S(2)}) collective-permute-start(bf16[64,1536]{1,0:T(8,128)(2,1)} %get-tuple-element.309), channel_id=1, source_target_pairs={{0,10},{2,8},{4,14},{6,12},{8,2},{10,0},{12,6},{14,4},{16,26},{18,... | collective-permute-start | bytes 589832 | tf_op jit(solution)/shard_map/ppermute | solution.py:31
  436.5 19.5 %collective-permute-start.62 = (bf16[2,64,1024]{2,1,0:T(8,128)(2,1)}, bf16[2,64,1024]{2,1,0:T(8,128)(2,1)}, u32[]{:S(2)}, u32[]{:S(2)}) collective-permute-start(bf16[2,64,1024]{2,1,0:T(8,128)(2,1)} %broadcast_select_fusion.8), channel_id=1, source_target_pairs={{0,1},{1,0},{2,3},{3,2},{4,5},{5,4},{6,7},{7,6},{8,9},{9,8},{10,11... | collective-permute-start | bytes 786440 | tf_op jit(solution)/shard_map/ppermute | solution.py:26
  444.7 16.2 %collective-permute-start.76 = (bf16[2,64,1536]{2,1,0:T(8,128)(2,1)}, bf16[2,64,1536]{2,1,0:T(8,128)(2,1)S(1)}, u32[]{:S(2)}, u32[]{:S(2)}) collective-permute-start(bf16[2,64,1536]{2,1,0:T(8,128)(2,1)} %broadcast_select_fusion.3), channel_id=1, source_target_pairs={{0,1},{1,0},{2,3},{3,2},{4,5},{5,4},{6,7},{7,6},{8,9},{9,8},{10,11... | collective-permute-start | bytes 1179656 | tf_op jit(solution)/shard_map/ppermute | solution.py:26
  (142 other events, 1270.6 us)

commit v2 on v1

--- a/solution.py
+++ b/solution.py
@@ -70,41 +70,49 @@
     return jnp.where(core == 0, zero, one)
 
 
-def by_slot(rel, low, side):
-    rel = [jnp.where(side == 0, rel[k], rel[k ^ 1]) for k in range(TP)]
-    return [jnp.where(low == 0, rel[k], rel[k ^ 2]) for k in range(TP)]
-
-
-def gather_weight(packed, core, low, side):
-    mine = by_core(core, packed[0], packed[1])
-    theirs = core_swap(by_core(core, packed[1], packed[0]))
-    first = by_core(core, mine, theirs)
-    second = by_core(core, theirs, mine)
-    pieces = [first[0], first[1], second[0], second[1]]
-    rel = by_slot(pieces, low, side)
-    rel = [rel[0]] + [peer(rel[step], step) for step in range(1, TP)]
-    held = jnp.concatenate(by_slot(rel, low, side), axis=0)
+def pick(array, index):
+    return lax.dynamic_index_in_dim(array, index, 0, keepdims=False)
+
+
+def both_halves(pack, core):
+    mine = pack(core)
+    theirs = core_swap(pack(1 - core))
+    both = by_core(core, jnp.stack([mine, theirs]), jnp.stack([theirs, mine]))
+    _, _, rows, columns = both.shape
+    return both.reshape(TP, rows, columns)
+
+
+def after(value, *earlier):
+    return lax.optimization_barrier((value, earlier))[0]
+
+
+def gather_weight(held):
     groups = lax.axis_size("dp") // 8
-    held = jnp.concatenate([held] + [from_h(held, step) for step in range(1, groups)], axis=0)
-    return jnp.concatenate([held, other_y(held)], axis=0)
-
-
-def scatter_grad(grad, core, low, side):
-    half = grad.shape[0] // 2
-    kept = grad[:half] + other_y(grad[half:].astype(BF)).astype(F32)
-    groups = lax.axis_size("dp") // 8
-    rows = half // groups
-    total = kept[:rows]
+    near = [held] + [from_h(held, step) for step in range(1, groups)]
+    return near + [other_y(block) for block in near]
+
+
+def scatter_grad(blocks):
+    groups = len(blocks) // 2
+    nears = []
     for step in range(1, groups):
-        total = total + to_h(kept[step * rows : (step + 1) * rows].astype(BF), step).astype(F32)
-    squares = jnp.sum(total * total)
-    low_total = total.astype(BF).reshape(TP, rows // TP, -1)
-    rel = by_slot([low_total[k] for k in range(TP)], low, side)
-    rel = [rel[0]] + [peer(rel[step], step) for step in range(1, TP)]
-    first, second = [jnp.stack(pair) for pair in zip(*[iter(by_slot(rel, low, side))] * 2)]
-    mine = by_core(core, first, second)
-    theirs = core_swap(by_core(core, second, first))
-    return by_core(core, mine, theirs), by_core(core, theirs, mine), squares
+        nears.append(blocks[step] + other_y(blocks[groups + step].astype(BF)).astype(F32))
+    total = blocks[0] + other_y(after(blocks[groups].astype(BF), nears)).astype(F32)
+    for step, near in enumerate(nears, 1):
+        total = total + to_h(near.astype(BF), step).astype(F32)
+    return total, nears
+
+
+def split_cores(parts, core):
+    mine = pick(parts, core)
+    theirs = core_swap(pick(parts, 1 - core))
+    return by_core(core, mine, theirs), by_core(core, theirs, mine)
+
+
+def peer_exchange(blocks, slot):
+    rel = [pick(blocks, slot)] + [peer(pick(blocks, slot ^ step), step) for step in range(1, TP)]
+    rel = [jnp.where(slot & 1 == 0, rel[k], rel[k ^ 1]) for k in range(TP)]
+    return jnp.stack([jnp.where(slot & 2 == 0, rel[k], rel[k ^ 2]) for k in range(TP)])
 
 
 def norm_parts(inputs):
@@ -181,27 +189,53 @@
     out_t = jnp.swapaxes(w_attn_out, 1, 2)
     down_t = jnp.swapaxes(w_down, 1, 2)
 
-    def pack(parts):
-        zero = jnp.concatenate([part[0].astype(BF) for part in parts], axis=-1)
-        one = jnp.concatenate([part[1].astype(BF) for part in parts], axis=-1)
-        return jnp.stack([zero, one], axis=1)
-
-    attn_parts = [halves(w_attn_in[:, :, k]) for k in range(3)] + [halves(out_t)]
-    full_attn = gather_weight(pack(attn_parts), core, low, side)
-    gate_parts = [split_hidden(w_gate_up[:, :, k], ffn_wide) for k in range(2)]
-    full_gate = gather_weight(pack(gate_parts), core, low, side)
-    full_down = gather_weight(pack([split_hidden(down_t, ffn_wide)]), core, low, side)
-    full_head = gather_weight(pack([halves(w_head)]), core, low, side)
+    def pack(*parts):
+        def packed(position):
+            parted = [[pick(part, position).astype(BF) for part in pair] for pair in parts]
+            return jnp.stack([jnp.concatenate(side_parts, axis=-1) for side_parts in zip(*parted)])
+
+        return packed
+
+    def concat_pack(*packs):
+        return lambda position: jnp.concatenate([one(position) for one in packs], axis=-1)
+
+    attn_pack = pack(*[halves(w_attn_in[:, :, k]) for k in range(3)], halves(out_t))
+    attn_both = both_halves(attn_pack, core)
+    attn_held = peer_exchange(attn_both, slot)
+
+    targets = pick_targets(codes, delays)
+    facts = jnp.concatenate([targets.T, counts[None]], axis=0).astype(F32)
+    facts = jnp.concatenate([facts.reshape(1, -1), norm_gains.reshape(1, -1)], axis=1)
+    facts = lax.all_to_all(
+        jnp.broadcast_to(facts, (chips, facts.shape[1])), "dp", 0, 0, tiled=True
+    )
+    facts = after(facts, attn_both)
+    gain_all = facts[:, 3 * frames :].reshape(chips, 6, rows).astype(BF)
+    facts = facts[:, : 3 * frames].reshape(chips, 3, frames).astype(jnp.int32)
+
+    gate_pack = pack(*[split_hidden(w_gate_up[:, :, k], ffn_wide) for k in range(2)])
+    gate_both = both_halves(gate_pack, core)
+    last_pack = concat_pack(pack(split_hidden(down_t, ffn_wide)), pack(halves(w_head)))
+    last_both = both_halves(last_pack, core)
     heads_wide = w_attn_out.shape[1] // 2
+
+    vocab_ids = core * vocab_half + lax.broadcasted_iota(jnp.int32, (1, vocab_half), 1)
+    all_hot = (facts[:, 0].reshape(-1, 1) == vocab_ids).astype(BF)
+    looked = dot(all_hot, embed_table[0].astype(BF)).astype(BF)
+    looked = looked + core_swap(looked)
+    looked = lax.all_to_all(after(looked, attn_held).reshape(chips, frames, rows), "dp", 0, 0)
+
+    gate_held = peer_exchange(after(gate_both, attn_held), slot)
+    last_held = peer_exchange(after(last_both, gate_held), slot)
+    attn_blocks = gather_weight(attn_held.reshape(TP * rows, -1))
+    gate_blocks = gather_weight(gate_held.reshape(TP * rows, -1))
+    down_blocks = gather_weight(last_held[..., :ffn_wide].reshape(TP * rows, -1))
+    head_blocks = gather_weight(last_held[..., ffn_wide:].reshape(TP * rows, -1))
+    full_attn, full_gate, full_down, full_head = [
+        jnp.concatenate(blocks) for blocks in (attn_blocks, gate_blocks, down_blocks, head_blocks)
+    ]
     full_in, full_out = full_attn[:, : 3 * heads_wide], full_attn[:, 3 * heads_wide :]
 
-    targets = pick_targets(codes, delays)
-    facts = jnp.concatenate([targets.T, counts[None]], axis=0)
-    facts = lax.all_to_all(jnp.broadcast_to(facts[None], (chips,) + facts.shape), "dp", 0, 0)
-    gain_send = jnp.broadcast_to(
-        norm_gains.astype(BF).reshape(1, 6, rows), (chips, 6, rows)
-    )
-    gain_all = lax.all_to_all(gain_send, "dp", 0, 0)
     total_count = jnp.sum(facts[:, 2]).astype(F32)
     inverse_count = 1.0 / total_count
     chip_ids = lax.broadcasted_iota(jnp.int32, (TP, chips), 1)
@@ -228,11 +262,6 @@
     source = source_chip * rows + feature % rows
     order = (lax.broadcasted_iota(jnp.int32, (width, width), 0) == source).astype(BF)
 
-    vocab_ids = core * vocab_half + lax.broadcasted_iota(jnp.int32, (1, vocab_half), 1)
-    all_hot = (facts[:, 0].reshape(-1, 1) == vocab_ids).astype(BF)
-    looked = dot(all_hot, embed_table[0].astype(BF)).astype(BF)
-    looked = looked + core_swap(looked)
-    looked = lax.all_to_all(looked.reshape(chips, frames, rows), "dp", 0, 0)
     looked = jnp.swapaxes(looked, 0, 1).reshape(frames, width)
     gain_abs = jnp.swapaxes(gain_all, 0, 1).reshape(2, 3, width)
     gain_abs = by_core(core, gain_abs[0], gain_abs[1])
@@ -319,11 +348,23 @@
     d_norm_attn, gain_attn = norm_back(attn_norm, attn_scale, gains[0], d_attn_in)
     d_stream = (d_residual + d_norm_attn).astype(BF)
 
+    returned = [
+        scatter_grad(jnp.split(grad, 2 * groups))
+        for grad in (grad_head, grad_down, grad_gate, grad_attn)
+    ]
+    sum_head, sum_down, sum_gate, sum_attn = [total for total, _ in returned]
+    sq_head, sq_down, sq_gate, sq_attn = [jnp.sum(total * total) for total, _ in returned]
+    sum_ffn = jnp.concatenate([sum_gate.astype(BF), sum_down.astype(BF), sum_head.astype(BF)], axis=1)
+    sum_ffn = peer_exchange(sum_ffn.reshape(TP, rows, -1), slot)
+    ffn_zero, ffn_one = split_cores(sum_ffn.reshape(2, 2, rows, -1), core)
+    sum_attn = peer_exchange(sum_attn.astype(BF).reshape(TP, rows, -1), slot)
+    attn_zero, attn_one = split_cores(sum_attn.reshape(2, 2, rows, -1), core)
+
     gain_rows = jnp.stack([gain_attn, gain_ffn, gain_head]).astype(BF)
     back = jnp.concatenate([d_stream, gain_rows, jnp.zeros((13, width), BF)], axis=0)
     back = dot_t(back, order).astype(BF)
     back = jnp.swapaxes(back.reshape(frames + 16, chips, rows), 0, 1)
-    back = lax.all_to_all(back, "dp", 0, 0)
+    back = after(lax.all_to_all(back, "dp", 0, 0), returned[3][1])
     gain_mine = jnp.sum(back[:, frames : frames + 3].astype(F32), axis=0)
     back_other = core_swap(back)
     gain_theirs = jnp.sum(back_other[:, frames : frames + 3].astype(F32), axis=0)
@@ -332,11 +373,6 @@
     )
     d_rows = by_core(core, back_other[:, :frames], back[:, :frames]).reshape(-1, rows)
     grad_embed = t_dot(all_hot, d_rows)
-
-    head_zero, head_one, sq_head = scatter_grad(grad_head, core, low, side)
-    down_zero, down_one, sq_down = scatter_grad(grad_down, core, low, side)
-    gate_zero, gate_one, sq_gate = scatter_grad(grad_gate, core, low, side)
-    attn_zero, attn_one, sq_attn = scatter_grad(grad_attn, core, low, side)
     squares = (
         sq_head
         + sq_down
@@ -369,10 +405,10 @@
     )
     g_out = jnp.swapaxes(join(unpack(attn_zero, attn_one, 3 * heads_wide, heads_wide)), 1, 2)
     g_gate = jnp.stack(
-        [join_hidden(unpack(gate_zero, gate_one, k * ffn_wide, ffn_wide)) for k in range(2)], axis=2
-    )
-    g_down = jnp.swapaxes(join_hidden(unpack(down_zero, down_one, 0, ffn_wide)), 1, 2)
-    g_head = join(unpack(head_zero, head_one, 0, vocab_part))
+        [join_hidden(unpack(ffn_zero, ffn_one, k * ffn_wide, ffn_wide)) for k in range(2)], axis=2
+    )
+    g_down = jnp.swapaxes(join_hidden(unpack(ffn_zero, ffn_one, 2 * ffn_wide, ffn_wide)), 1, 2)
+    g_head = join(unpack(ffn_zero, ffn_one, 3 * ffn_wide, vocab_part))
     grads = (g_in, g_out, g_gate, g_down, g_head, grad_embed[None], grad_gains)
     rates = (RATE_MATRIX,) * 5 + (RATE_TABLE, RATE_TABLE)
     updates = [

time: 480 us -> 393 us (0.82)
  waiting for transfers between devices: 179 us -> 118 us
  local copies, waits for them, and re-layouts: 57.2 us -> 42.4 us
  other arithmetic: 59.3 us -> 51.3 us
  starting transfers between devices: 135 us -> 129 us
    ppermute x4, waiting for transfers between devices: 44.1 us -> 0.01 us  [to_h(): lax.ppermute(piece, 'dp', [(chip, (chip + 8 * step) % ways) for chip in r...]
    all_to_all x4 -> x3, waiting for transfers between devices: 5.54 us -> 39.5 us  [the longest x1 21.4 us: shards(): back = after(lax.all_to_all(back, 'dp', 0, 0), returned[3][1])]
    ppermute x65 -> x64, waiting for transfers between devices: 109 us -> 78.8 us  [flip(): lax.ppermute(piece, 'dp', [(chip, chip ^ mask) for chip in range(ways)])]
    ppermute x4, waiting for transfers between devices: 19.9 us -> 0.01 us  [from_h(): lax.ppermute(piece, 'dp', [(chip, (chip - 8 * step) % ways) for chip in r...]
    unnamed x255 -> x222, local copies, waits for them, and re-layouts: 32.5 us -> 19.1 us
    ppermute x12 -> x9, starting transfers between devices: 42.9 us -> 32.6 us  [core_swap(): return lax.ppermute(piece, 'mp', [(0, 1), (1, 0)])]
    concatenate x8 -> x0, local copies, waits for them, and re-layouts: 7.4 us -> none  [the longest x4 5.16 us: gather_weight(): jnp.concatenate([held] + [from_h(held, step) for step in range(1, groups)...]
    all_to_all x4 -> x3, starting transfers between devices: 22 us -> 15.8 us  [the longest x1 7.76 us: shards(): lax.all_to_all(jnp.broadcast_to(facts, (chips, facts.shape[1])), 'dp', 0,...]
  transfers between devices with their start and end apart: 90 -> 85, of which waited for: 34 -> 32; matrix products, arithmetic and copies ran while one was open for 25% -> 26% of each run, Pallas kernels for 0% -> 0%
where the time goes in v2:
time: 393 us; the launch traced here: 387 us
  starting transfers between devices  129 us (33%)
  waiting for transfers between devices  118 us (30%)
  other arithmetic  51.3 us (13%)
  local copies, waits for them, and re-layouts  42.4 us (11%)
  matrix products  34.7 us (9%)
  between operations  11.3 us (3%)
    ppermute x64, waiting for transfers between devices, flip(): lax.ppermute(piece, 'dp', [(chip, chip ^ mask) for chip in range(ways)])  78.8 us
    ppermute x64, starting transfers between devices, flip(): lax.ppermute(piece, 'dp', [(chip, chip ^ mask) for chip in range(ways)])  63.5 us
    ppermute x9, starting transfers between devices, core_swap(): return lax.ppermute(piece, 'mp', [(0, 1), (1, 0)])  32.6 us
    all_to_all x1, waiting for transfers between devices, shards(): back = after(lax.all_to_all(back, 'dp', 0, 0), returned[3][1])  21.4 us
    unnamed x222, local copies, waits for them, and re-layouts  19.1 us
    dot_general x6, matrix products, t_dot(): lax.dot_general(left, right, (((0,), (0,)), ((), ())), preferred_element_...  15.1 us
    all_to_all x1, waiting for transfers between devices, shards(): lax.all_to_all(after(looked, attn_held).reshape(chips, frames, rows), 'dp...  13.9 us
    dot_general x7, matrix products, dot(): return jnp.dot(left, right, preferred_element_type=F32)  9.94 us
  transfers between devices with their start and end apart: 85, of which 32 were waited for; matrix products, arithmetic and copies ran while one was open for 26% of the time, Pallas kernels for 0%

profile of v2, /device:TPU:1, one launch (start us, length us, event | category | flops | bytes accessed | tf_op | source)
XLA Modules:
  0.0 386.9 jit_solution(16361126550675652142)
XLA Ops:
  6.5 7.8 %all-to-all-start = ((f32[16,1,672]{2,1,0:T(1,128)}), f32[16,1,672]{2,1,0:T(1,128)S(1)}, u32[]{:S(2)}, u32[]{:S(2)}) async-start(f32[16,1,672]{2,1,0:T(1,128)} %broadcast_in_dim.83), calls=%async_computation | async-start | bytes 98304 | tf_op jit(solution)/shard_map/all_to_all | solution.py:209
  16.4 4.2 %all-to-all-done = f32[16,1,672]{2,1,0:T(1,128)S(1)} async-done(((f32[16,1,672]{2,1,0:T(1,128)}), f32[16,1,672]{2,1,0:T(1,128)S(1)}, u32[]{:S(2)}, u32[]{:S(2)}) %all-to-all-start) | async-done | bytes 43040 | tf_op jit(solution)/shard_map/all_to_all | solution.py:209
  23.2 1.9 collective-permute-start.4
  26.0 1.9 fusion.11
  28.9 2.6 collective-permute-start.1
  34.2 2.0 collective-permute-start.21
  38.2 1.6 add.513
  41.8 4.5 %all-to-all-start.1 = ((bf16[16,96,64]{1,2,0:T(8,128)(2,1)}), bf16[16,96,64]{1,2,0:T(8,128)(2,1)S(1)}, u32[]{:S(2)}, u32[]{:S(2)}) async-start(bf16[16,96,64]{1,2,0:T(8,128)(2,1)} %copy.254), calls=%async_computation.1 | async-start | bytes 524288 | tf_op jit(solution)/shard_map/all_to_all | solution.py:226
  46.3 3.0 collective-permute-done.21
  51.5 13.9 %all-to-all-done.1 = bf16[16,96,64]{1,2,0:T(8,128)(2,1)S(1)} async-done(((bf16[16,96,64]{1,2,0:T(8,128)(2,1)}), bf16[16,96,64]{1,2,0:T(8,128)(2,1)S(1)}, u32[]{:S(2)}, u32[]{:S(2)}) %all-to-all-start.1) | async-done | bytes 196640 | tf_op jit(solution)/shard_map/all_to_all | solution.py:226
  66.8 1.6 collective-permute-start.10
  71.3 5.3 %collective-permute-done.10 = bf16[256,1024]{1,0:T(8,128)(2,1)S(1)} collective-permute-done((bf16[256,1024]{1,0:T(8,128)(2,1)S(1)}, bf16[256,1024]{1,0:T(8,128)(2,1)S(1)}, u32[]{:S(2)}, u32[]{:S(2)}) %collective-permute-start.10) | collective-permute-done | bytes 524320 | tf_op jit(solution)/shard_map/ppermute | solution.py:31
  78.4 1.6 collective-permute-start.26
  83.2 8.1 %collective-permute-start.11 = (bf16[384,512]{1,0:T(8,128)(2,1)S(1)}, bf16[384,512]{1,0:T(8,128)(2,1)S(1)}, u32[]{:S(2)}, u32[]{:S(2)}) collective-permute-start(bf16[384,512]{1,0:T(8,128)(2,1)S(1)} %slice.533), channel_id=1, source_target_pairs={{0,1},{1,0},{2,3},{3,2},{4,5},{5,4},{6,7},{7,6},{8,9},{9,8},{10,11... | collective-permute-start | bytes 1179656 | tf_op jit(solution)/shard_map/ppermute | solution.py:26
  91.4 4.7 %collective-permute-done.27 = bf16[64,1280]{1,0:T(8,128)(2,1)S(1)} collective-permute-done((bf16[64,1280]{1,0:T(8,128)(2,1)S(1)}, bf16[64,1280]{1,0:T(8,128)(2,1)S(1)}, u32[]{:S(2)}, u32[]{:S(2)}) %collective-permute-start.27) | collective-permute-done | bytes 163872 | tf_op jit(solution)/shard_map/ppermute | solution.py:31
  96.1 3.5 collective-permute-done.28
  102.4 3.1 collective-permute-start.13
  107.2 7.3 %collective-permute-done.13 = bf16[96,1024]{1,0:T(8,128)(2,1)S(1)} collective-permute-done((bf16[96,1024]{1,0:T(8,128)(2,1)S(1)}, bf16[96,1024]{1,0:T(8,128)(2,1)S(1)}, u32[]{:S(2)}, u32[]{:S(2)}) %collective-permute-start.13) | collective-permute-done | bytes 196640 | tf_op jit(solution)/shard_map/ppermute | solution.py:31
  114.5 8.4 %collective-permute-done.14 = bf16[96,1024]{1,0:T(8,128)(2,1)S(1)} collective-permute-done((bf16[96,1024]{1,0:T(8,128)(2,1)S(1)}, bf16[96,1024]{1,0:T(8,128)(2,1)S(1)}, u32[]{:S(2)}, u32[]{:S(2)}) %collective-permute-start.14) | collective-permute-done | bytes 196640 | tf_op jit(solution)/shard_map/ppermute | solution.py:31
  123.5 2.5 collective-permute-start.17
  129.1 10.1 %collective-permute-done.17 = bf16[96,1024]{1,0:T(8,128)(2,1)S(1)} collective-permute-done((bf16[96,1024]{1,0:T(8,128)(2,1)S(1)}, bf16[96,1024]{1,0:T(8,128)(2,1)S(1)}, u32[]{:S(2)}, u32[]{:S(2)}) %collective-permute-start.17) | collective-permute-done | bytes 196640 | tf_op jit(solution)/shard_map/ppermute | solution.py:31
  141.1 2.0 collective-permute-done.31
  144.1 2.6 collective-permute-start.34
  148.7 3.7 collective-permute-done.34
  153.1 2.3 collective-permute-start.37
  156.5 2.1 collective-permute-done.35
  158.6 2.1 collective-permute-done.37
  160.7 2.2 fusion.249
  165.8 2.1 collective-permute-start.43
  170.2 2.0 fusion.251
  175.0 2.0 fusion.250
  183.9 3.7 collective-permute-start.66
  188.4 7.1 %collective-permute-done.49 = bf16[96,1024]{1,0:T(8,128)(2,1)S(1)} collective-permute-done((bf16[96,1024]{1,0:T(8,128)(2,1)S(1)}, bf16[96,1024]{1,0:T(8,128)(2,1)S(1)}, u32[]{:S(2)}, u32[]{:S(2)}) %collective-permute-start.49) | collective-permute-done | bytes 196640 | tf_op jit(solution)/shard_map/ppermute | solution.py:31
  200.9 4.5 %fusion.253 = (bf16[1024,1536]{1,0:T(8,128)(2,1)S(1)}, f32[1024,1536]{1,0:T(8,128)}) fusion(bf16[384,768]{1,0:T(8,128)(2,1)S(1)} %get-tuple-element.235, bf16[384,768]{1,0:T(8,128)(2,1)S(1)} %get-tuple-element.234, bf16[96,1024]{1,0:T(8,128)(2,1)S(1)} %copy-done.59, bf16[96,1024]{1,0:T(8,128)(2,1)S(1)} %copy-done.57, bf16[96,1024]{1,0:T(8,128)(2,1)S(1)} %copy-done.55, ...), kind=kOutput, calls=%fused_computation.582 | convolution fusion | flops 1215037440 | bytes 11403264 | tf_op jit(solution)/shard_map/dot_general | solution.py:138
  206.7 2.7 fusion.252
  213.9 1.7 collective-permute-start.55
  218.7 3.5 collective-permute-done.55
  224.5 17.6 %collective-permute-start.56 = (bf16[384,512]{1,0:T(8,128)(2,1)S(1)}, bf16[384,512]{1,0:T(8,128)(2,1)S(1)}, u32[]{:S(2)}, u32[]{:S(2)}) collective-permute-start(bf16[384,512]{1,0:T(8,128)(2,1)S(1)} %pad_maximum_fusion.25), channel_id=1, source_target_pairs={{0,1},{1,0},{2,3},{3,2},{4,5},{5,4},{6,7},{7,6},{8,9},{9,8},{10,11... | collective-permute-start | bytes 1179656 | tf_op jit(solution)/shard_map/ppermute | solution.py:26
  242.1 2.1 slice_add_fusion.2
  244.2 1.9 collective-permute-start.69
  248.0 1.6 copy-done.10
  253.2 2.7 slice_add_fusion
  259.2 6.9 %collective-permute-start.57 = (bf16[256,1024]{0,1:T(8,128)(2,1)}, bf16[256,1024]{0,1:T(8,128)(2,1)}, u32[]{:S(2)}, u32[]{:S(2)}) collective-permute-start(bf16[256,1024]{0,1:T(8,128)(2,1)} %get-tuple-element.247), channel_id=1, source_target_pairs={{0,4},{2,6},{4,0},{6,2},{8,12},{10,14},{12,8},{14,10},{16,20},{18,... | collective-permute-start | bytes 1572872 | tf_op jit(solution)/shard_map/ppermute | solution.py:31
  266.1 3.3 collective-permute-done.75
  269.4 1.6 collective-permute-start.71
  273.4 2.4 fusion.27
  275.7 1.8 copy.269
  277.5 3.5 all-to-all-start.2
  281.1 2.9 fusion.77
  284.0 1.9 copy.276
  287.2 2.1 fusion.33
  289.3 2.2 collective-permute-start.59
  292.7 21.4 %all-to-all-done.2 = bf16[16,112,64]{1,2,0:T(8,128)(2,1)S(1)} async-done(((bf16[16,112,64]{1,2,0:T(8,128)(2,1)}), bf16[16,112,64]{1,2,0:T(8,128)(2,1)S(1)}, u32[]{:S(2)}, u32[]{:S(2)}) %all-to-all-start.2) | async-done | bytes 229408 | tf_op jit(solution)/shard_map/all_to_all | solution.py:367
  314.0 2.0 collective-permute-start.76
  316.3 3.0 fusion.49
  329.9 3.5 multiply_reduce_fusion.13
  333.4 2.2 fusion.220
  339.2 5.7 %all-to-all-start.3 = ((f32[32,8,128]{2,1,0:T(8,128)}), f32[32,8,128]{2,1,0:T(8,128)S(1)}, u32[]{:S(2)}, u32[]{:S(2)}) async-start(f32[32,8,128]{2,1,0:T(8,128)} %broadcast_in_dim.92), calls=%async_computation.3 | async-start | bytes 262144 | tf_op jit(solution)/shard_map/all_to_all | solution.py:387
  352.7 3.4 collective-permute-done.62
  361.0 2.2 multiply_subtract_fusion.4
  373.9 2.2 copy.284
  376.2 2.2 copy.286
  378.4 2.2 copy.288
  382.8 1.7 multiply_subtract_fusion.2
  (557 shorter events, 123.7 us)
Async XLA Ops:
  2.9 17.7 %collective-permute-start = (bf16[2,64,1024]{2,1,0:T(8,128)(2,1)}, bf16[2,64,1024]{2,1,0:T(8,128)(2,1)}, u32[]{:S(2)}, u32[]{:S(2)}) collective-permute-start(bf16[2,64,1024]{2,1,0:T(8,128)(2,1)} %pad_maximum_fusion.31), channel_id=1, source_target_pairs={{0,1},{1,0},{2,3},{3,2},{4,5},{5,4},{6,7},{7,6},{8,9},{9,8},{10,11... | collective-permute-start | bytes 786440 | tf_op jit(solution)/shard_map/ppermute | solution.py:26
  3.8 28.7 %collective-permute-start.18 = (bf16[2,64,1536]{2,1,0:T(8,128)(2,1)S(1)}, bf16[2,64,1536]{2,1,0:T(8,128)(2,1)S(1)}, u32[]{:S(2)}, u32[]{:S(2)}) collective-permute-start(bf16[2,64,1536]{2,1,0:T(8,128)(2,1)S(1)} %pad_maximum_fusion.24), channel_id=1, source_target_pairs={{0,1},{1,0},{2,3},{3,2},{4,5},{5,4},{6,7},{7,6},{8,9},{9,8},{10,11... | collective-permute-start | bytes 1179656 | tf_op jit(solution)/shard_map/ppermute | solution.py:26
  5.0 31.2 %collective-permute-start.25 = (bf16[2,64,1280]{2,1,0:T(8,128)(2,1)S(1)}, bf16[2,64,1280]{2,1,0:T(8,128)(2,1)}, u32[]{:S(2)}, u32[]{:S(2)}) collective-permute-start(bf16[2,64,1280]{2,1,0:T(8,128)(2,1)S(1)} %maximum_maximum_fusion), channel_id=1, source_target_pairs={{0,1},{1,0},{2,3},{3,2},{4,5},{5,4},{6,7},{7,6},{8,9},{9,8},{10,11... | collective-permute-start | bytes 983048 | tf_op jit(solution)/shard_map/ppermute | solution.py:26
  6.5 14.1 %all-to-all-start = ((f32[16,1,672]{2,1,0:T(1,128)}), f32[16,1,672]{2,1,0:T(1,128)S(1)}, u32[]{:S(2)}, u32[]{:S(2)}) async-start(f32[16,1,672]{2,1,0:T(1,128)} %broadcast_in_dim.83), calls=%async_computation | async-start | bytes 98304 | tf_op jit(solution)/shard_map/all_to_all | solution.py:209
  23.2 8.3 %collective-permute-start.3 = (bf16[64,1024]{1,0:T(8,128)(2,1)S(1)}, bf16[64,1024]{1,0:T(8,128)(2,1)S(1)}, u32[]{:S(2)}, u32[]{:S(2)}) collective-permute-start(bf16[64,1024]{1,0:T(8,128)(2,1)S(1)} %get-tuple-element.310), channel_id=1, source_target_pairs={{0,8},{2,10},{4,12},{6,14},{8,0},{10,2},{12,4},{14,6},{16,24},{18,... | collective-permute-start | bytes 393224 | tf_op jit(solution)/shard_map/ppermute | solution.py:31
  23.2 8.3 %collective-permute-start.4 = (bf16[64,1024]{1,0:T(8,128)(2,1)S(1)}, bf16[64,1024]{1,0:T(8,128)(2,1)}, u32[]{:S(2)}, u32[]{:S(2)}) collective-permute-start(bf16[64,1024]{1,0:T(8,128)(2,1)S(1)} %get-tuple-element.309), channel_id=1, source_target_pairs={{0,10},{2,8},{4,14},{6,12},{8,2},{10,0},{12,6},{14,4},{16,26},{18,... | collective-permute-start | bytes 393224 | tf_op jit(solution)/shard_map/ppermute | solution.py:31
  28.9 8.9 %collective-permute-start.1 = (bf16[1536,64]{0,1:T(8,128)(2,1)}, bf16[1536,64]{0,1:T(8,128)(2,1)S(1)}, u32[]{:S(2)}, u32[]{:S(2)}) collective-permute-start(bf16[1536,64]{0,1:T(8,128)(2,1)} %fusion.11), channel_id=1, source_target_pairs={{0,1},{1,0},{2,3},{3,2},{4,5},{5,4},{6,7},{7,6},{8,9},{9,8},{10,11... | collective-permute-start | bytes 589832 | tf_op jit(solution)/shard_map/ppermute | solution.py:26
  33.5 12.8 %collective-permute-start.19 = (bf16[64,1536]{1,0:T(8,128)(2,1)}, bf16[64,1536]{1,0:T(8,128)(2,1)}, u32[]{:S(2)}, u32[]{:S(2)}) collective-permute-start(bf16[64,1536]{1,0:T(8,128)(2,1)} %get-tuple-element.291), channel_id=1, source_target_pairs={{0,2},{2,0},{4,6},{6,4},{8,10},{10,8},{12,14},{14,12},{16,18},{18,... | collective-permute-start | bytes 589832 | tf_op jit(solution)/shard_map/ppermute | solution.py:31
  34.0 12.3 %collective-permute-start.20 = (bf16[64,1536]{1,0:T(8,128)(2,1)}, bf16[64,1536]{1,0:T(8,128)(2,1)}, u32[]{:S(2)}, u32[]{:S(2)}) collective-permute-start(bf16[64,1536]{1,0:T(8,128)(2,1)} %get-tuple-element.293), channel_id=1, source_target_pairs={{0,8},{2,10},{4,12},{6,14},{8,0},{10,2},{12,4},{14,6},{16,24},{18,... | collective-permute-start | bytes 589832 | tf_op jit(solution)/shard_map/ppermute | solution.py:31
  34.2 15.2 %collective-permute-start.21 = (bf16[64,1536]{1,0:T(8,128)(2,1)}, bf16[64,1536]{1,0:T(8,128)(2,1)}, u32[]{:S(2)}, u32[]{:S(2)}) collective-permute-start(bf16[64,1536]{1,0:T(8,128)(2,1)} %get-tuple-element.292), channel_id=1, source_target_pairs={{0,10},{2,8},{4,14},{6,12},{8,2},{10,0},{12,6},{14,4},{16,26},{18,... | collective-permute-start | bytes 589832 | tf_op jit(solution)/shard_map/ppermute | solution.py:31
  37.3 29.4 %collective-permute-start.8 = (bf16[256,1024]{1,0:T(8,128)(2,1)S(1)}, bf16[256,1024]{1,0:T(8,128)(2,1)S(1)}, u32[]{:S(2)}, u32[]{:S(2)}) collective-permute-start(bf16[256,1024]{1,0:T(8,128)(2,1)S(1)} %bitcast.383), channel_id=1, source_target_pairs={{0,16},{2,18},{4,20},{6,22},{8,24},{10,26},{12,28},{14,30},{16,0},... | collective-permute-start | bytes 1572872 | tf_op jit(solution)/shard_map/ppermute | solution.py:44
  37.8 33.4 %collective-permute-start.9 = (bf16[256,1024]{1,0:T(8,128)(2,1)S(1)}, bf16[256,1024]{1,0:T(8,128)(2,1)S(1)}, u32[]{:S(2)}, u32[]{:S(2)}) collective-permute-start(bf16[256,1024]{1,0:T(8,128)(2,1)S(1)} %bitcast.384), channel_id=1, source_target_pairs={{0,4},{2,6},{4,0},{6,2},{8,12},{10,14},{12,8},{14,10},{16,20},{18,... | collective-permute-start | bytes 1572872 | tf_op jit(solution)/shard_map/ppermute | solution.py:31
  41.8 23.7 %all-to-all-start.1 = ((bf16[16,96,64]{1,2,0:T(8,128)(2,1)}), bf16[16,96,64]{1,2,0:T(8,128)(2,1)S(1)}, u32[]{:S(2)}, u32[]{:S(2)}) async-start(bf16[16,96,64]{1,2,0:T(8,128)(2,1)} %copy.254), calls=%async_computation.1 | async-start | bytes 524288 | tf_op jit(solution)/shard_map/all_to_all | solution.py:226
  66.8 9.8 %collective-permute-start.10 = (bf16[256,1024]{1,0:T(8,128)(2,1)S(1)}, bf16[256,1024]{1,0:T(8,128)(2,1)S(1)}, u32[]{:S(2)}, u32[]{:S(2)}) collective-permute-start(bf16[256,1024]{1,0:T(8,128)(2,1)S(1)} %collective-permute-done.8), channel_id=1, source_target_pairs={{0,4},{2,6},{4,0},{6,2},{8,12},{10,14},{12,8},{14,10},{16,20},{18,... | collective-permute-start | bytes 1572872 | tf_op jit(solution)/shard_map/ppermute | solution.py:31
  68.5 9.9 %collective-permute-start.5 = (bf16[96,1024]{1,0:T(8,128)(2,1)S(1)}, bf16[96,1024]{1,0:T(8,128)(2,1)S(1)}, u32[]{:S(2)}, u32[]{:S(2)}) collective-permute-start(bf16[96,1024]{1,0:T(8,128)(2,1)S(1)} %multiply_convert_fusion.7), channel_id=1, source_target_pairs={{0,2},{2,0},{4,6},{6,4},{8,10},{10,8},{12,14},{14,12},{16,18},{18,... | collective-permute-start | bytes 589832 | tf_op jit(solution)/shard_map/ppermute | solution.py:31
  69.8 10.2 %collective-permute-start.6 = (bf16[96,1024]{1,0:T(8,128)(2,1)S(1)}, bf16[96,1024]{1,0:T(8,128)(2,1)S(1)}, u32[]{:S(2)}, u32[]{:S(2)}) collective-permute-start(bf16[96,1024]{1,0:T(8,128)(2,1)S(1)} %multiply_convert_fusion.7), channel_id=1, source_target_pairs={{0,8},{2,10},{4,12},{6,14},{8,0},{10,2},{12,4},{14,6},{16,24},{18,... | collective-permute-start | bytes 589832 | tf_op jit(solution)/shard_map/ppermute | solution.py:31
  70.8 10.5 %collective-permute-start.7 = (bf16[96,1024]{1,0:T(8,128)(2,1)S(1)}, bf16[96,1024]{1,0:T(8,128)(2,1)S(1)}, u32[]{:S(2)}, u32[]{:S(2)}) collective-permute-start(bf16[96,1024]{1,0:T(8,128)(2,1)S(1)} %multiply_convert_fusion.7), channel_id=1, source_target_pairs={{0,10},{2,8},{4,14},{6,12},{8,2},{10,0},{12,6},{14,4},{16,26},{18,... | collective-permute-start | bytes 589832 | tf_op jit(solution)/shard_map/ppermute | solution.py:31
  71.2 34.4 %collective-permute-start.22 = (bf16[256,1536]{1,0:T(8,128)(2,1)S(1)}, bf16[256,1536]{1,0:T(8,128)(2,1)S(1)}, u32[]{:S(2)}, u32[]{:S(2)}) collective-permute-start(bf16[256,1536]{1,0:T(8,128)(2,1)S(1)} %bitcast.400), channel_id=1, source_target_pairs={{0,16},{2,18},{4,20},{6,22},{8,24},{10,26},{12,28},{14,30},{16,0},... | collective-permute-start | bytes 2359304 | tf_op jit(solution)/shard_map/ppermute | solution.py:44
  76.6 49.4 %collective-permute-start.23 = (bf16[256,1536]{1,0:T(8,128)(2,1)S(1)}, bf16[256,1536]{1,0:T(8,128)(2,1)S(1)}, u32[]{:S(2)}, u32[]{:S(2)}) collective-permute-start(bf16[256,1536]{1,0:T(8,128)(2,1)S(1)} %bitcast.401), channel_id=1, source_target_pairs={{0,4},{2,6},{4,0},{6,2},{8,12},{10,14},{12,8},{14,10},{16,20},{18,... | collective-permute-start | bytes 2359304 | tf_op jit(solution)/shard_map/ppermute | solution.py:31
  80.0 16.1 %collective-permute-start.27 = (bf16[64,1280]{1,0:T(8,128)(2,1)S(1)}, bf16[64,1280]{1,0:T(8,128)(2,1)S(1)}, u32[]{:S(2)}, u32[]{:S(2)}) collective-permute-start(bf16[64,1280]{1,0:T(8,128)(2,1)S(1)} %get-tuple-element.304), channel_id=1, source_target_pairs={{0,8},{2,10},{4,12},{6,14},{8,0},{10,2},{12,4},{14,6},{16,24},{18,... | collective-permute-start | bytes 491528 | tf_op jit(solution)/shard_map/ppermute | solution.py:31
  81.3 18.3 %collective-permute-start.28 = (bf16[64,1280]{1,0:T(8,128)(2,1)S(1)}, bf16[64,1280]{1,0:T(8,128)(2,1)S(1)}, u32[]{:S(2)}, u32[]{:S(2)}) collective-permute-start(bf16[64,1280]{1,0:T(8,128)(2,1)S(1)} %get-tuple-element.303), channel_id=1, source_target_pairs={{0,10},{2,8},{4,14},{6,12},{8,2},{10,0},{12,6},{14,4},{16,26},{18,... | collective-permute-start | bytes 491528 | tf_op jit(solution)/shard_map/ppermute | solution.py:31
  83.2 16.6 %collective-permute-start.11 = (bf16[384,512]{1,0:T(8,128)(2,1)S(1)}, bf16[384,512]{1,0:T(8,128)(2,1)S(1)}, u32[]{:S(2)}, u32[]{:S(2)}) collective-permute-start(bf16[384,512]{1,0:T(8,128)(2,1)S(1)} %slice.533), channel_id=1, source_target_pairs={{0,1},{1,0},{2,3},{3,2},{4,5},{5,4},{6,7},{7,6},{8,9},{9,8},{10,11... | collective-permute-start | bytes 1179656 | tf_op jit(solution)/shard_map/ppermute | solution.py:26
  102.4 12.1 %collective-permute-start.13 = (bf16[96,1024]{1,0:T(8,128)(2,1)S(1)}, bf16[96,1024]{1,0:T(8,128)(2,1)S(1)}, u32[]{:S(2)}, u32[]{:S(2)}) collective-permute-start(bf16[96,1024]{1,0:T(8,128)(2,1)S(1)} %get-tuple-element.290), channel_id=1, source_target_pairs={{0,8},{2,10},{4,12},{6,14},{8,0},{10,2},{12,4},{14,6},{16,24},{18,... | collective-permute-start | bytes 589832 | tf_op jit(solution)/shard_map/ppermute | solution.py:31
  105.5 17.4 %collective-permute-start.14 = (bf16[96,1024]{1,0:T(8,128)(2,1)S(1)}, bf16[96,1024]{1,0:T(8,128)(2,1)S(1)}, u32[]{:S(2)}, u32[]{:S(2)}) collective-permute-start(bf16[96,1024]{1,0:T(8,128)(2,1)S(1)} %get-tuple-element.289), channel_id=1, source_target_pairs={{0,10},{2,8},{4,14},{6,12},{8,2},{10,0},{12,6},{14,4},{16,26},{18,... | collective-permute-start | bytes 589832 | tf_op jit(solution)/shard_map/ppermute | solution.py:31
  105.6 17.9 %collective-permute-start.29 = (bf16[256,768]{1,0:T(8,128)(2,1)S(1)}, bf16[256,768]{1,0:T(8,128)(2,1)S(1)}, u32[]{:S(2)}, u32[]{:S(2)}) collective-permute-start(bf16[256,768]{1,0:T(8,128)(2,1)S(1)} %bitcast.405), channel_id=1, source_target_pairs={{0,16},{2,18},{4,20},{6,22},{8,24},{10,26},{12,28},{14,30},{16,0},... | collective-permute-start | bytes 1179656 | tf_op jit(solution)/shard_map/ppermute | solution.py:44
  107.2 19.4 %collective-permute-start.24 = (bf16[256,1536]{1,0:T(8,128)(2,1)S(1)}, bf16[256,1536]{1,0:T(8,128)(2,1)S(1)}, u32[]{:S(2)}, u32[]{:S(2)}) collective-permute-start(bf16[256,1536]{1,0:T(8,128)(2,1)S(1)} %collective-permute-done.22), channel_id=1, source_target_pairs={{0,4},{2,6},{4,0},{6,2},{8,12},{10,14},{12,8},{14,10},{16,20},{18,... | collective-permute-start | bytes 2359304 | tf_op jit(solution)/shard_map/ppermute | solution.py:31
  123.5 15.7 %collective-permute-start.17 = (bf16[96,1024]{1,0:T(8,128)(2,1)S(1)}, bf16[96,1024]{1,0:T(8,128)(2,1)S(1)}, u32[]{:S(2)}, u32[]{:S(2)}) collective-permute-start(bf16[96,1024]{1,0:T(8,128)(2,1)S(1)} %multiply_convert_fusion.6), channel_id=1, source_target_pairs={{0,10},{2,8},{4,14},{6,12},{8,2},{10,0},{12,6},{14,4},{16,26},{18,... | collective-permute-start | bytes 589832 | tf_op jit(solution)/shard_map/ppermute | solution.py:31
  126.0 15.0 %collective-permute-start.30 = (bf16[256,768]{1,0:T(8,128)(2,1)S(1)}, bf16[256,768]{1,0:T(8,128)(2,1)S(1)}, u32[]{:S(2)}, u32[]{:S(2)}) collective-permute-start(bf16[256,768]{1,0:T(8,128)(2,1)S(1)} %bitcast.406), channel_id=1, source_target_pairs={{0,4},{2,6},{4,0},{6,2},{8,12},{10,14},{12,8},{14,10},{16,20},{18,... | collective-permute-start | bytes 1179656 | tf_op jit(solution)/shard_map/ppermute | solution.py:31
  126.6 20.9 %collective-permute-start.38 = (bf16[256,512]{1,0:T(8,128)(2,1)S(1)}, bf16[256,512]{1,0:T(8,128)(2,1)}, u32[]{:S(2)}, u32[]{:S(2)}) collective-permute-start(bf16[256,512]{1,0:T(8,128)(2,1)S(1)} %bitcast.410), channel_id=1, source_target_pairs={{0,16},{2,18},{4,20},{6,22},{8,24},{10,26},{12,28},{14,30},{16,0},... | collective-permute-start | bytes 786440 | tf_op jit(solution)/shard_map/ppermute | solution.py:44
  128.5 14.6 %collective-permute-start.31 = (bf16[256,768]{1,0:T(8,128)(2,1)S(1)}, bf16[256,768]{1,0:T(8,128)(2,1)S(1)}, u32[]{:S(2)}, u32[]{:S(2)}) collective-permute-start(bf16[256,768]{1,0:T(8,128)(2,1)S(1)} %collective-permute-done.29), channel_id=1, source_target_pairs={{0,4},{2,6},{4,0},{6,2},{8,12},{10,14},{12,8},{14,10},{16,20},{18,... | collective-permute-start | bytes 1179656 | tf_op jit(solution)/shard_map/ppermute | solution.py:31
  144.1 8.2 %collective-permute-start.34 = (bf16[96,1024]{1,0:T(8,128)(2,1)S(1)}, bf16[96,1024]{1,0:T(8,128)(2,1)S(1)}, u32[]{:S(2)}, u32[]{:S(2)}) collective-permute-start(bf16[96,1024]{1,0:T(8,128)(2,1)S(1)} %get-tuple-element.286), channel_id=1, source_target_pairs={{0,10},{2,8},{4,14},{6,12},{8,2},{10,0},{12,6},{14,4},{16,26},{18,... | collective-permute-start | bytes 589832 | tf_op jit(solution)/shard_map/ppermute | solution.py:31
  146.8 8.8 %collective-permute-start.39 = (bf16[256,512]{1,0:T(8,128)(2,1)S(1)}, bf16[256,512]{1,0:T(8,128)(2,1)S(1)}, u32[]{:S(2)}, u32[]{:S(2)}) collective-permute-start(bf16[256,512]{1,0:T(8,128)(2,1)S(1)} %bitcast.411), channel_id=1, source_target_pairs={{0,4},{2,6},{4,0},{6,2},{8,12},{10,14},{12,8},{14,10},{16,20},{18,... | collective-permute-start | bytes 786440 | tf_op jit(solution)/shard_map/ppermute | solution.py:31
  147.5 9.0 %collective-permute-start.40 = (bf16[256,512]{1,0:T(8,128)(2,1)}, bf16[256,512]{1,0:T(8,128)(2,1)}, u32[]{:S(2)}, u32[]{:S(2)}) collective-permute-start(bf16[256,512]{1,0:T(8,128)(2,1)} %collective-permute-done.38), channel_id=1, source_target_pairs={{0,4},{2,6},{4,0},{6,2},{8,12},{10,14},{12,8},{14,10},{16,20},{18,... | collective-permute-start | bytes 786440 | tf_op jit(solution)/shard_map/ppermute | solution.py:31
  153.1 7.6 %collective-permute-start.37 = (bf16[96,1024]{1,0:T(8,128)(2,1)S(1)}, bf16[96,1024]{1,0:T(8,128)(2,1)}, u32[]{:S(2)}, u32[]{:S(2)}) collective-permute-start(bf16[96,1024]{1,0:T(8,128)(2,1)S(1)} %multiply_convert_fusion.5), channel_id=1, source_target_pairs={{0,10},{2,8},{4,14},{6,12},{8,2},{10,0},{12,6},{14,4},{16,26},{18,... | collective-permute-start | bytes 589832 | tf_op jit(solution)/shard_map/ppermute | solution.py:31
  172.3 7.9 %collective-permute-start.44 = (bf16[96,1024]{1,0:T(8,128)(2,1)S(1)}, bf16[96,1024]{1,0:T(8,128)(2,1)S(1)}, u32[]{:S(2)}, u32[]{:S(2)}) collective-permute-start(bf16[96,1024]{1,0:T(8,128)(2,1)S(1)} %get-tuple-element.282), channel_id=1, source_target_pairs={{0,2},{2,0},{4,6},{6,4},{8,10},{10,8},{12,14},{14,12},{16,18},{18,... | collective-permute-start | bytes 589832 | tf_op jit(solution)/shard_map/ppermute | solution.py:31
  180.7 7.4 %collective-permute-start.47 = (bf16[96,1024]{1,0:T(8,128)(2,1)S(1)}, bf16[96,1024]{1,0:T(8,128)(2,1)S(1)}, u32[]{:S(2)}, u32[]{:S(2)}) collective-permute-start(bf16[96,1024]{1,0:T(8,128)(2,1)S(1)} %fusion.206), channel_id=1, source_target_pairs={{0,2},{2,0},{4,6},{6,4},{8,10},{10,8},{12,14},{14,12},{16,18},{18,... | collective-permute-start | bytes 589832 | tf_op jit(solution)/shard_map/ppermute | solution.py:31
  183.1 12.4 %collective-permute-start.49 = (bf16[96,1024]{1,0:T(8,128)(2,1)S(1)}, bf16[96,1024]{1,0:T(8,128)(2,1)S(1)}, u32[]{:S(2)}, u32[]{:S(2)}) collective-permute-start(bf16[96,1024]{1,0:T(8,128)(2,1)S(1)} %fusion.206), channel_id=1, source_target_pairs={{0,10},{2,8},{4,14},{6,12},{8,2},{10,0},{12,6},{14,4},{16,26},{18,... | collective-permute-start | bytes 589832 | tf_op jit(solution)/shard_map/ppermute | solution.py:31
  183.9 30.0 %collective-permute-start.66 = (bf16[256,512]{0,1:T(8,128)(2,1)S(1)}, bf16[256,512]{0,1:T(8,128)(2,1)S(1)}, u32[]{:S(2)}, u32[]{:S(2)}) collective-permute-start(bf16[256,512]{0,1:T(8,128)(2,1)S(1)} %slice_add_fusion.4), channel_id=1, source_target_pairs={{0,16},{2,18},{4,20},{6,22},{8,24},{10,26},{12,28},{14,30},{16,0},... | collective-permute-start | bytes 786440 | tf_op jit(solution)/shard_map/ppermute | solution.py:49
  187.6 26.3 %collective-permute-start.65 = (bf16[256,512]{0,1:T(8,128)(2,1)S(1)}, bf16[256,512]{0,1:T(8,128)(2,1)S(1)}, u32[]{:S(2)}, u32[]{:S(2)}) collective-permute-start(bf16[256,512]{0,1:T(8,128)(2,1)S(1)} %get-tuple-element.37), channel_id=1, source_target_pairs={{0,4},{2,6},{4,0},{6,2},{8,12},{10,14},{12,8},{14,10},{16,20},{18,... | collective-permute-start | bytes 786440 | tf_op jit(solution)/shard_map/ppermute | solution.py:31
  198.2 11.9 %collective-permute-start.50 = (bf16[96,1024]{1,0:T(8,128)(2,1)S(1)}, bf16[96,1024]{1,0:T(8,128)(2,1)S(1)}, u32[]{:S(2)}, u32[]{:S(2)}) collective-permute-start(bf16[96,1024]{1,0:T(8,128)(2,1)S(1)} %get-tuple-element.279), channel_id=1, source_target_pairs={{0,2},{2,0},{4,6},{6,4},{8,10},{10,8},{12,14},{14,12},{16,18},{18,... | collective-permute-start | bytes 589832 | tf_op jit(solution)/shard_map/ppermute | solution.py:31
  199.4 11.8 %collective-permute-start.51 = (bf16[96,1024]{1,0:T(8,128)(2,1)S(1)}, bf16[96,1024]{1,0:T(8,128)(2,1)S(1)}, u32[]{:S(2)}, u32[]{:S(2)}) collective-permute-start(bf16[96,1024]{1,0:T(8,128)(2,1)S(1)} %get-tuple-element.281), channel_id=1, source_target_pairs={{0,8},{2,10},{4,12},{6,14},{8,0},{10,2},{12,4},{14,6},{16,24},{18,... | collective-permute-start | bytes 589832 | tf_op jit(solution)/shard_map/ppermute | solution.py:31
  199.4 13.0 %collective-permute-start.52 = (bf16[96,1024]{1,0:T(8,128)(2,1)S(1)}, bf16[96,1024]{1,0:T(8,128)(2,1)S(1)}, u32[]{:S(2)}, u32[]{:S(2)}) collective-permute-start(bf16[96,1024]{1,0:T(8,128)(2,1)S(1)} %get-tuple-element.280), channel_id=1, source_target_pairs={{0,10},{2,8},{4,14},{6,12},{8,2},{10,0},{12,6},{14,4},{16,26},{18,... | collective-permute-start | bytes 589832 | tf_op jit(solution)/shard_map/ppermute | solution.py:31
  210.1 42.5 %collective-permute-start.70 = (bf16[256,1536]{1,0:T(8,128)(2,1)}, bf16[256,1536]{1,0:T(8,128)(2,1)}, u32[]{:S(2)}, u32[]{:S(2)}) collective-permute-start(bf16[256,1536]{1,0:T(8,128)(2,1)} %get-tuple-element.237), channel_id=1, source_target_pairs={{0,4},{2,6},{4,0},{6,2},{8,12},{10,14},{12,8},{14,10},{16,20},{18,... | collective-permute-start | bytes 2359304 | tf_op jit(solution)/shard_map/ppermute | solution.py:31
  211.2 30.9 %collective-permute-start.67 = (bf16[256,768]{0,1:T(8,128)(2,1)S(1)}, bf16[256,768]{0,1:T(8,128)(2,1)}, u32[]{:S(2)}, u32[]{:S(2)}) collective-permute-start(bf16[256,768]{0,1:T(8,128)(2,1)S(1)} %get-tuple-element.249), channel_id=1, source_target_pairs={{0,4},{2,6},{4,0},{6,2},{8,12},{10,14},{12,8},{14,10},{16,20},{18,... | collective-permute-start | bytes 1179656 | tf_op jit(solution)/shard_map/ppermute | solution.py:31
  213.9 8.3 %collective-permute-start.55 = (bf16[96,1024]{1,0:T(8,128)(2,1)S(1)}, bf16[96,1024]{1,0:T(8,128)(2,1)}, u32[]{:S(2)}, u32[]{:S(2)}) collective-permute-start(bf16[96,1024]{1,0:T(8,128)(2,1)S(1)} %get-tuple-element.222), channel_id=1, source_target_pairs={{0,10},{2,8},{4,14},{6,12},{8,2},{10,0},{12,6},{14,4},{16,26},{18,... | collective-permute-start | bytes 589832 | tf_op jit(solution)/shard_map/ppermute | solution.py:31
  224.5 23.1 %collective-permute-start.56 = (bf16[384,512]{1,0:T(8,128)(2,1)S(1)}, bf16[384,512]{1,0:T(8,128)(2,1)S(1)}, u32[]{:S(2)}, u32[]{:S(2)}) collective-permute-start(bf16[384,512]{1,0:T(8,128)(2,1)S(1)} %pad_maximum_fusion.25), channel_id=1, source_target_pairs={{0,1},{1,0},{2,3},{3,2},{4,5},{5,4},{6,7},{7,6},{8,9},{9,8},{10,11... | collective-permute-start | bytes 1179656 | tf_op jit(solution)/shard_map/ppermute | solution.py:26
  244.2 36.9 %collective-permute-start.69 = (bf16[256,768]{0,1:T(8,128)(2,1)}, bf16[256,768]{0,1:T(8,128)(2,1)}, u32[]{:S(2)}, u32[]{:S(2)}) collective-permute-start(bf16[256,768]{0,1:T(8,128)(2,1)} %slice_add_fusion.2), channel_id=1, source_target_pairs={{0,16},{2,18},{4,20},{6,22},{8,24},{10,26},{12,28},{14,30},{16,0},... | collective-permute-start | bytes 1179656 | tf_op jit(solution)/shard_map/ppermute | solution.py:49
  246.1 35.0 %collective-permute-start.68 = (bf16[256,768]{0,1:T(8,128)(2,1)}, bf16[256,768]{0,1:T(8,128)(2,1)}, u32[]{:S(2)}, u32[]{:S(2)}) collective-permute-start(bf16[256,768]{0,1:T(8,128)(2,1)} %get-tuple-element.38), channel_id=1, source_target_pairs={{0,4},{2,6},{4,0},{6,2},{8,12},{10,14},{12,8},{14,10},{16,20},{18,... | collective-permute-start | bytes 1179656 | tf_op jit(solution)/shard_map/ppermute | solution.py:31
  250.5 8.0 %collective-permute-start.73 = (bf16[96,1024]{1,0:T(8,128)(2,1)S(1)}, bf16[96,1024]{1,0:T(8,128)(2,1)S(1)}, u32[]{:S(2)}, u32[]{:S(2)}) collective-permute-start(bf16[96,1024]{1,0:T(8,128)(2,1)S(1)} %get-tuple-element.276), channel_id=1, source_target_pairs={{0,2},{2,0},{4,6},{6,4},{8,10},{10,8},{12,14},{14,12},{16,18},{18,... | collective-permute-start | bytes 589832 | tf_op jit(solution)/shard_map/ppermute | solution.py:31
  251.4 7.8 %collective-permute-start.74 = (bf16[96,1024]{1,0:T(8,128)(2,1)S(1)}, bf16[96,1024]{1,0:T(8,128)(2,1)S(1)}, u32[]{:S(2)}, u32[]{:S(2)}) collective-permute-start(bf16[96,1024]{1,0:T(8,128)(2,1)S(1)} %get-tuple-element.278), channel_id=1, source_target_pairs={{0,8},{2,10},{4,12},{6,14},{8,0},{10,2},{12,4},{14,6},{16,24},{18,... | collective-permute-start | bytes 589832 | tf_op jit(solution)/shard_map/ppermute | solution.py:31
  252.6 16.7 %collective-permute-start.75 = (bf16[96,1024]{1,0:T(8,128)(2,1)S(1)}, bf16[96,1024]{1,0:T(8,128)(2,1)S(1)}, u32[]{:S(2)}, u32[]{:S(2)}) collective-permute-start(bf16[96,1024]{1,0:T(8,128)(2,1)S(1)} %get-tuple-element.277), channel_id=1, source_target_pairs={{0,10},{2,8},{4,14},{6,12},{8,2},{10,0},{12,6},{14,4},{16,26},{18,... | collective-permute-start | bytes 589832 | tf_op jit(solution)/shard_map/ppermute | solution.py:31
  258.5 57.8 %collective-permute-start.72 = (bf16[256,1536]{1,0:T(8,128)(2,1)}, bf16[256,1536]{1,0:T(8,128)(2,1)}, u32[]{:S(2)}, u32[]{:S(2)}) collective-permute-start(bf16[256,1536]{1,0:T(8,128)(2,1)} %slice_add_fusion), channel_id=1, source_target_pairs={{0,16},{2,18},{4,20},{6,22},{8,24},{10,26},{12,28},{14,30},{16,0},... | collective-permute-start | bytes 2359304 | tf_op jit(solution)/shard_map/ppermute | solution.py:49
  259.2 28.0 %collective-permute-start.57 = (bf16[256,1024]{0,1:T(8,128)(2,1)}, bf16[256,1024]{0,1:T(8,128)(2,1)}, u32[]{:S(2)}, u32[]{:S(2)}) collective-permute-start(bf16[256,1024]{0,1:T(8,128)(2,1)} %get-tuple-element.247), channel_id=1, source_target_pairs={{0,4},{2,6},{4,0},{6,2},{8,12},{10,14},{12,8},{14,10},{16,20},{18,... | collective-permute-start | bytes 1572872 | tf_op jit(solution)/shard_map/ppermute | solution.py:31
  269.4 46.9 %collective-permute-start.71 = (bf16[256,1536]{1,0:T(8,128)(2,1)}, bf16[256,1536]{1,0:T(8,128)(2,1)}, u32[]{:S(2)}, u32[]{:S(2)}) collective-permute-start(bf16[256,1536]{1,0:T(8,128)(2,1)} %get-tuple-element.39), channel_id=1, source_target_pairs={{0,4},{2,6},{4,0},{6,2},{8,12},{10,14},{12,8},{14,10},{16,20},{18,... | collective-permute-start | bytes 2359304 | tf_op jit(solution)/shard_map/ppermute | solution.py:31
  277.5 36.5 %all-to-all-start.2 = ((bf16[16,112,64]{1,2,0:T(8,128)(2,1)}), bf16[16,112,64]{1,2,0:T(8,128)(2,1)S(1)}, u32[]{:S(2)}, u32[]{:S(2)}) async-start(bf16[16,112,64]{1,2,0:T(8,128)(2,1)} %bitcast.399), calls=%async_computation.2 | async-start | bytes 524288 | tf_op jit(solution)/shard_map/all_to_all | solution.py:367
  289.3 44.1 %collective-permute-start.59 = (bf16[256,1024]{0,1:T(8,128)(2,1)}, bf16[256,1024]{0,1:T(8,128)(2,1)}, u32[]{:S(2)}, u32[]{:S(2)}) collective-permute-start(bf16[256,1024]{0,1:T(8,128)(2,1)} %fusion.33), channel_id=1, source_target_pairs={{0,16},{2,18},{4,20},{6,22},{8,24},{10,26},{12,28},{14,30},{16,0},... | collective-permute-start | bytes 1572872 | tf_op jit(solution)/shard_map/ppermute | solution.py:49
  291.5 41.9 %collective-permute-start.58 = (bf16[256,1024]{0,1:T(8,128)(2,1)}, bf16[256,1024]{0,1:T(8,128)(2,1)}, u32[]{:S(2)}, u32[]{:S(2)}) collective-permute-start(bf16[256,1024]{0,1:T(8,128)(2,1)} %get-tuple-element.36), channel_id=1, source_target_pairs={{0,4},{2,6},{4,0},{6,2},{8,12},{10,14},{12,8},{14,10},{16,20},{18,... | collective-permute-start | bytes 1572872 | tf_op jit(solution)/shard_map/ppermute | solution.py:31
  314.0 9.9 %collective-permute-start.76 = (bf16[16,112,64]{1,2,0:T(8,128)(2,1)S(1)}, bf16[16,112,64]{1,2,0:T(8,128)(2,1)}, u32[]{:S(2)}, u32[]{:S(2)}) collective-permute-start(bf16[16,112,64]{1,2,0:T(8,128)(2,1)S(1)} %all-to-all-done.2), channel_id=1, source_target_pairs={{0,1},{1,0},{2,3},{3,2},{4,5},{5,4},{6,7},{7,6},{8,9},{9,8},{10,11... | collective-permute-start | bytes 688136 | tf_op jit(solution)/shard_map/ppermute | solution.py:26
  321.4 26.3 %collective-permute-start.77 = (bf16[64,2816]{1,0:T(8,128)(2,1)}, bf16[64,2816]{1,0:T(8,128)(2,1)}, u32[]{:S(2)}, u32[]{:S(2)}) collective-permute-start(bf16[64,2816]{1,0:T(8,128)(2,1)} %get-tuple-element.250), channel_id=1, source_target_pairs={{0,2},{2,0},{4,6},{6,4},{8,10},{10,8},{12,14},{14,12},{16,18},{18,... | collective-permute-start | bytes 1081352 | tf_op jit(solution)/shard_map/ppermute | solution.py:31
  322.3 25.6 %collective-permute-start.78 = (bf16[64,2816]{1,0:T(8,128)(2,1)}, bf16[64,2816]{1,0:T(8,128)(2,1)}, u32[]{:S(2)}, u32[]{:S(2)}) collective-permute-start(bf16[64,2816]{1,0:T(8,128)(2,1)} %get-tuple-element.252), channel_id=1, source_target_pairs={{0,8},{2,10},{4,12},{6,14},{8,0},{10,2},{12,4},{14,6},{16,24},{18,... | collective-permute-start | bytes 1081352 | tf_op jit(solution)/shard_map/ppermute | solution.py:31
  323.9 23.9 %collective-permute-start.79 = (bf16[64,2816]{1,0:T(8,128)(2,1)}, bf16[64,2816]{1,0:T(8,128)(2,1)}, u32[]{:S(2)}, u32[]{:S(2)}) collective-permute-start(bf16[64,2816]{1,0:T(8,128)(2,1)} %get-tuple-element.251), channel_id=1, source_target_pairs={{0,10},{2,8},{4,14},{6,12},{8,2},{10,0},{12,6},{14,4},{16,26},{18,... | collective-permute-start | bytes 1081352 | tf_op jit(solution)/shard_map/ppermute | solution.py:31
  339.2 18.5 %all-to-all-start.3 = ((f32[32,8,128]{2,1,0:T(8,128)}), f32[32,8,128]{2,1,0:T(8,128)S(1)}, u32[]{:S(2)}, u32[]{:S(2)}) async-start(f32[32,8,128]{2,1,0:T(8,128)} %broadcast_in_dim.92), calls=%async_computation.3 | async-start | bytes 262144 | tf_op jit(solution)/shard_map/all_to_all | solution.py:387
  347.8 8.3 %collective-permute-start.62 = (bf16[64,1024]{1,0:T(8,128)(2,1)S(1)}, bf16[64,1024]{1,0:T(8,128)(2,1)S(1)}, u32[]{:S(2)}, u32[]{:S(2)}) collective-permute-start(bf16[64,1024]{1,0:T(8,128)(2,1)S(1)} %get-tuple-element.306), channel_id=1, source_target_pairs={{0,10},{2,8},{4,14},{6,12},{8,2},{10,0},{12,6},{14,4},{16,26},{18,... | collective-permute-start | bytes 393224 | tf_op jit(solution)/shard_map/ppermute | solution.py:31
  349.5 20.8 %collective-permute-start.80 = (bf16[2,64,2816]{2,1,0:T(8,128)(2,1)S(1)}, bf16[2,64,2816]{2,1,0:T(8,128)(2,1)S(1)}, u32[]{:S(2)}, u32[]{:S(2)}) collective-permute-start(bf16[2,64,2816]{2,1,0:T(8,128)(2,1)S(1)} %dynamic-slice_bitcast_fusion), channel_id=1, source_target_pairs={{0,1},{1,0},{2,3},{3,2},{4,5},{5,4},{6,7},{7,6},{8,9},{9,8},{10,11... | collective-permute-start | bytes 2162696 | tf_op jit(solution)/shard_map/ppermute | solution.py:26
  (127 other events, 960.4 us)

commit v3 on v2

--- a/solution.py
+++ b/solution.py
@@ -1,6 +1,7 @@
 import jax
 import jax.numpy as jnp
 from jax import lax
+from jax.experimental.layout import Layout, with_layout_constraint
 from jax.sharding import PartitionSpec as P
 
 HEAD_DIM = 64
@@ -18,6 +19,18 @@
 RATE_MATRIX = 0.03
 RATE_TABLE = 0.5
 
+DEADLINES = [
+    ("attn_b", "known"),
+    ("gate_t", "last_x"),
+    ("g_attn_y", "embedded"),
+    ("g_head_y", "head_y0"),
+    ("g_down_y", "down_y0"),
+    ("g_gate_y", "gate_y0"),
+    ("g_attn_y", "attn_y0"),
+    ("down_z", "ffn"),
+    ("last_t", "head"),
+]
+
 BF = jnp.bfloat16
 F32 = jnp.float32
 
@@ -86,21 +99,32 @@
     return lax.optimization_barrier((value, earlier))[0]
 
 
-def gather_weight(held):
+def hook(ready, step, value):
+    early = [ready[name] for name, place in DEADLINES if place == step]
+    return after(value, *early) if early else value
+
+
+def gather_weight(ready, name, held):
     groups = lax.axis_size("dp") // 8
     near = [held] + [from_h(held, step) for step in range(1, groups)]
-    return near + [other_y(block) for block in near]
-
-
-def scatter_grad(blocks):
+    far = [other_y(block) for block in near]
+    ready[name + "_h"], ready[name + "_y"], ready[name + "_z"] = near[1:], far[0], far[1:]
+    return near + far
+
+
+def scatter_grad(ready, name, blocks):
     groups = len(blocks) // 2
     nears = []
     for step in range(1, groups):
         nears.append(blocks[step] + other_y(blocks[groups + step].astype(BF)).astype(F32))
-    total = blocks[0] + other_y(after(blocks[groups].astype(BF), nears)).astype(F32)
+    ready["g_" + name + "_y"] = nears
+    sent = hook(ready, name + "_y0", blocks[groups].astype(BF))
+    total = blocks[0] + other_y(sent).astype(F32)
+    ready["g_" + name + "_z"] = total
     for step, near in enumerate(nears, 1):
         total = total + to_h(near.astype(BF), step).astype(F32)
-    return total, nears
+    ready["g_" + name + "_h"] = total
+    return total
 
 
 def split_cores(parts, core):
@@ -171,6 +195,7 @@
     context, codes, delays, counts = args[:4]
     params, firsts, seconds = args[4:11], args[11:18], args[18:25]
     w_attn_in, w_attn_out, w_gate_up, w_down, w_head, embed_table, norm_gains = params
+    ready = {}
     chips = lax.axis_size("dp")
     groups = chips // 8
     chip = lax.axis_index("dp")
@@ -202,14 +227,15 @@
     attn_pack = pack(*[halves(w_attn_in[:, :, k]) for k in range(3)], halves(out_t))
     attn_both = both_halves(attn_pack, core)
     attn_held = peer_exchange(attn_both, slot)
+    ready["attn_b"], ready["attn_t"] = attn_both, attn_held
 
     targets = pick_targets(codes, delays)
     facts = jnp.concatenate([targets.T, counts[None]], axis=0).astype(F32)
     facts = jnp.concatenate([facts.reshape(1, -1), norm_gains.reshape(1, -1)], axis=1)
     facts = lax.all_to_all(
-        jnp.broadcast_to(facts, (chips, facts.shape[1])), "dp", 0, 0, tiled=True
-    )
-    facts = after(facts, attn_both)
+        jnp.broadcast_to(hook(ready, "facts", facts), (chips, facts.shape[1])), "dp", 0, 0, tiled=True
+    )
+    facts = hook(ready, "known", facts)
     gain_all = facts[:, 3 * frames :].reshape(chips, 6, rows).astype(BF)
     facts = facts[:, : 3 * frames].reshape(chips, 3, frames).astype(jnp.int32)
 
@@ -219,18 +245,21 @@
     last_both = both_halves(last_pack, core)
     heads_wide = w_attn_out.shape[1] // 2
 
+    gate_held = peer_exchange(hook(ready, "gate_x", gate_both), slot)
+    ready["gate_t"] = gate_held
+    last_held = peer_exchange(hook(ready, "last_x", last_both), slot)
+    ready["last_t"] = last_held
+    attn_blocks = gather_weight(ready, "attn", attn_held.reshape(TP * rows, -1))
+    gate_blocks = gather_weight(ready, "gate", gate_held.reshape(TP * rows, -1))
+    down_blocks = gather_weight(ready, "down", last_held[..., :ffn_wide].reshape(TP * rows, -1))
+    head_blocks = gather_weight(ready, "head", last_held[..., ffn_wide:].reshape(TP * rows, -1))
+
     vocab_ids = core * vocab_half + lax.broadcasted_iota(jnp.int32, (1, vocab_half), 1)
     all_hot = (facts[:, 0].reshape(-1, 1) == vocab_ids).astype(BF)
     looked = dot(all_hot, embed_table[0].astype(BF)).astype(BF)
     looked = looked + core_swap(looked)
-    looked = lax.all_to_all(after(looked, attn_held).reshape(chips, frames, rows), "dp", 0, 0)
-
-    gate_held = peer_exchange(after(gate_both, attn_held), slot)
-    last_held = peer_exchange(after(last_both, gate_held), slot)
-    attn_blocks = gather_weight(attn_held.reshape(TP * rows, -1))
-    gate_blocks = gather_weight(gate_held.reshape(TP * rows, -1))
-    down_blocks = gather_weight(last_held[..., :ffn_wide].reshape(TP * rows, -1))
-    head_blocks = gather_weight(last_held[..., ffn_wide:].reshape(TP * rows, -1))
+    looked = lax.all_to_all(hook(ready, "looked", looked).reshape(chips, frames, rows), "dp", 0, 0)
+
     full_attn, full_gate, full_down, full_head = [
         jnp.concatenate(blocks) for blocks in (attn_blocks, gate_blocks, down_blocks, head_blocks)
     ]
@@ -270,11 +299,11 @@
     stream = moved[:frames]
     gains = moved[frames : frames + 3]
 
-    attn_norm, attn_scale = norm_parts(stream)
+    attn_norm, attn_scale = norm_parts(hook(ready, "norm", stream))
     attn_low = group_gather((attn_norm * gains[0]).astype(BF))
-    qkv = dot(attn_low, full_in).astype(BF)
+    qkv = dot(hook(ready, "qkv", attn_low), full_in).astype(BF)
     kv_other = core_swap(qkv[:, heads_wide:]).astype(F32)
-    query = qkv[:, :heads_wide].astype(F32)
+    query = hook(ready, "attend", qkv[:, :heads_wide]).astype(F32)
     key_self = qkv[:, heads_wide : 2 * heads_wide].astype(F32)
     val_self = qkv[:, 2 * heads_wide :].astype(F32)
     key_gap = kv_other[:, :heads_wide] - key_self
@@ -286,17 +315,17 @@
     prob_other = by_core(core, 0.0, jax.nn.sigmoid(gap))
     prob_self = by_core(core, 1.0, jax.nn.sigmoid(-gap))
     attended = (val_self + prob_other * val_gap).astype(BF)
-    residual = stream + group_scatter(dot_t(attended, full_out))
+    residual = hook(ready, "add1", stream) + group_scatter(dot_t(attended, full_out))
     ffn_norm, ffn_scale = norm_parts(residual)
     ffn_low = group_gather((ffn_norm * gains[1]).astype(BF))
-    gate_up = dot(ffn_low, full_gate)
+    gate_up = dot(hook(ready, "ffn", ffn_low), full_gate)
     gate, up = gate_up[:, :ffn_wide], gate_up[:, ffn_wide:]
     sig = jax.nn.sigmoid(gate)
     hidden = (gate * sig * up).astype(BF)
-    output = residual + group_scatter(dot_t(hidden, full_down))
+    output = hook(ready, "add2", residual) + group_scatter(dot_t(hook(ready, "down", hidden), full_down))
     head_norm, head_scale = norm_parts(output)
     head_low = group_gather((head_norm * gains[2]).astype(BF))
-    logits = dot(head_low, full_head)
+    logits = dot(hook(ready, "head", head_low), full_head)
     vocab_part = logits.shape[1]
     part_ids = slot * vocab_part + lax.broadcasted_iota(jnp.int32, (1, vocab_part), 1)
     picks = group_targets[:, None] == part_ids
@@ -320,51 +349,65 @@
         (part_exp * factor[:, None] - picks.astype(F32)) * weight_row[:, None]
     ).astype(BF)
     d_head_in = group_scatter(dot_t(d_logits, full_head))
-    grad_head = t_dot(head_low, d_logits)
-    d_output, gain_head = norm_back(head_norm, head_scale, gains[2], d_head_in)
+    def by_blocks(left, right):
+        return [t_dot(part, right) for part in jnp.split(left, 2 * groups, axis=1)]
+
+    grad_head = lax.optimization_barrier(by_blocks(head_low, d_logits))
+    sum_head = scatter_grad(ready, "head", grad_head)
+    d_output, gain_head = norm_back(
+        head_norm, head_scale, gains[2], hook(ready, "back1", d_head_in)
+    )
     d_output_low = group_gather(d_output.astype(BF))
-    d_hidden = dot(d_output_low, full_down)
+    d_hidden = dot(hook(ready, "dffn", d_output_low), full_down)
     d_gate = d_hidden * up * (sig * (1.0 + gate * (1.0 - sig)))
     d_up = d_hidden * (gate * sig)
     d_gate_up = jnp.concatenate([d_gate, d_up], axis=1).astype(BF)
     d_ffn_in = group_scatter(dot_t(d_gate_up, full_gate))
-    grad_down = t_dot(d_output_low, hidden)
-    grad_gate = t_dot(ffn_low, d_gate_up)
-    d_norm_ffn, gain_ffn = norm_back(ffn_norm, ffn_scale, gains[1], d_ffn_in)
+    sum_down = scatter_grad(ready, "down", by_blocks(d_output_low, hidden))
+    sum_gate = scatter_grad(ready, "gate", by_blocks(ffn_low, d_gate_up))
+    d_norm_ffn, gain_ffn = norm_back(
+        ffn_norm, ffn_scale, gains[1], hook(ready, "back2", d_ffn_in)
+    )
     d_residual = d_output + d_norm_ffn
     d_res_low = group_gather(d_residual.astype(BF))
-    d_attended = dot(d_res_low, full_out)
+    d_attended = dot(hook(ready, "datt", d_res_low), full_out)
     pull = wide_dot(d_attended * val_gap, head_sum)
     d_score = prob_other * prob_self * pull * 0.125
     d_query = d_score * key_gap
     d_key_other = d_score * query
     d_val_other = prob_other * d_attended
-    d_kv = core_swap(jnp.concatenate([d_key_other, d_val_other], axis=1).astype(BF)).astype(F32)
+    d_kv = core_swap(
+        hook(ready, "swap", jnp.concatenate([d_key_other, d_val_other], axis=1).astype(BF))
+    ).astype(F32)
     d_key = d_kv[:, :heads_wide] - d_key_other
     d_val = d_kv[:, heads_wide:] + prob_self * d_attended
     d_qkv = jnp.concatenate([d_query, d_key, d_val], axis=1).astype(BF)
-    d_attn_in = group_scatter(dot_t(d_qkv, full_in))
-    grad_attn = jnp.concatenate([t_dot(attn_low, d_qkv), t_dot(d_res_low, attended)], axis=1)
-    d_norm_attn, gain_attn = norm_back(attn_norm, attn_scale, gains[0], d_attn_in)
+    d_attn_in = group_scatter(dot_t(hook(ready, "dqkv", d_qkv), full_in))
+    grad_attn = [
+        jnp.concatenate(pair, axis=1)
+        for pair in zip(by_blocks(attn_low, d_qkv), by_blocks(d_res_low, attended))
+    ]
+    sum_attn = scatter_grad(ready, "attn", grad_attn)
+    d_norm_attn, gain_attn = norm_back(
+        attn_norm, attn_scale, gains[0], hook(ready, "back3", d_attn_in)
+    )
     d_stream = (d_residual + d_norm_attn).astype(BF)
 
-    returned = [
-        scatter_grad(jnp.split(grad, 2 * groups))
-        for grad in (grad_head, grad_down, grad_gate, grad_attn)
-    ]
-    sum_head, sum_down, sum_gate, sum_attn = [total for total, _ in returned]
-    sq_head, sq_down, sq_gate, sq_attn = [jnp.sum(total * total) for total, _ in returned]
+    sums = [sum_head, sum_down, sum_gate, sum_attn]
+    sq_head, sq_down, sq_gate, sq_attn = [jnp.sum(total * total) for total in sums]
     sum_ffn = jnp.concatenate([sum_gate.astype(BF), sum_down.astype(BF), sum_head.astype(BF)], axis=1)
+    sum_ffn = hook(ready, "sumffn", sum_ffn)
     sum_ffn = peer_exchange(sum_ffn.reshape(TP, rows, -1), slot)
     ffn_zero, ffn_one = split_cores(sum_ffn.reshape(2, 2, rows, -1), core)
     sum_attn = peer_exchange(sum_attn.astype(BF).reshape(TP, rows, -1), slot)
     attn_zero, attn_one = split_cores(sum_attn.reshape(2, 2, rows, -1), core)
 
     gain_rows = jnp.stack([gain_attn, gain_ffn, gain_head]).astype(BF)
+    d_stream = hook(ready, "embed", d_stream)
     back = jnp.concatenate([d_stream, gain_rows, jnp.zeros((13, width), BF)], axis=0)
     back = dot_t(back, order).astype(BF)
     back = jnp.swapaxes(back.reshape(frames + 16, chips, rows), 0, 1)
-    back = after(lax.all_to_all(back, "dp", 0, 0), returned[3][1])
+    back = hook(ready, "embedded", lax.all_to_all(back, "dp", 0, 0))
     gain_mine = jnp.sum(back[:, frames : frames + 3].astype(F32), axis=0)
     back_other = core_swap(back)
     gain_theirs = jnp.sum(back_other[:, frames : frames + 3].astype(F32), axis=0)
@@ -409,6 +452,8 @@
     )
     g_down = jnp.swapaxes(join_hidden(unpack(ffn_zero, ffn_one, 2 * ffn_wide, ffn_wide)), 1, 2)
     g_head = join(unpack(ffn_zero, ffn_one, 3 * ffn_wide, vocab_part))
+    g_in = with_layout_constraint(g_in, Layout((0, 2, 1, 3)))
+    g_gate = with_layout_constraint(g_gate, Layout((0, 1, 2, 3)))
     grads = (g_in, g_out, g_gate, g_down, g_head, grad_embed[None], grad_gains)
     rates = (RATE_MATRIX,) * 5 + (RATE_TABLE, RATE_TABLE)
     updates = [

time: 393 us -> 385 us (0.980)
  local copies, waits for them, and re-layouts: 42.4 us -> 24.5 us
  starting transfers between devices: 129 us -> 142 us
  waiting for transfers between devices: 118 us -> 109 us
  matrix products: 34.7 us -> 41.2 us
    all_to_all x3, waiting for transfers between devices: 39.5 us -> 16 us  [the longest x1 15.1 us: shards(): lax.all_to_all(hook(ready, 'looked', looked).reshape(chips, frames, rows)...]
    ppermute x4, starting transfers between devices: 8.5 us -> 24.4 us  [to_h(): lax.ppermute(piece, 'dp', [(chip, (chip + 8 * step) % ways) for chip in r...]
    unnamed x222 -> x159, local copies, waits for them, and re-layouts: 19.1 us -> 6.93 us
    ppermute x9, starting transfers between devices: 32.6 us -> 21.7 us  [core_swap(): return lax.ppermute(piece, 'mp', [(0, 1), (1, 0)])]
    sub x7, other arithmetic: 9.42 us -> 17 us  [adam(): weight * (1.0 - rate * DECAY) - rate * adam_step]
    ppermute x64, waiting for transfers between devices: 78.8 us -> 85.9 us  [flip(): lax.ppermute(piece, 'dp', [(chip, chip ^ mask) for chip in range(ways)])]
    ppermute x4, waiting for transfers between devices: 0.01 us -> 7.09 us  [to_h(): lax.ppermute(piece, 'dp', [(chip, (chip + 8 * step) % ways) for chip in r...]
    dot_general x6 -> x21, matrix products: 15.1 us -> 21.3 us  [t_dot(): lax.dot_general(left, right, (((0,), (0,)), ((), ())), preferred_element_...]
  transfers between devices with their start and end apart: 85 -> 85, of which waited for: 32 -> 29; matrix products, arithmetic and copies ran while one was open for 26% -> 24% of each run, Pallas kernels for 0% -> 0%
where the time goes in v3:
time: 385 us; the launch traced here: 379 us
  starting transfers between devices  142 us (37%)
  waiting for transfers between devices  109 us (28%)
  other arithmetic  50.5 us (13%)
  matrix products  41.2 us (11%)
  local copies, waits for them, and re-layouts  24.5 us (6%)
  between operations  11.5 us (3%)
    ppermute x64, waiting for transfers between devices, flip(): lax.ppermute(piece, 'dp', [(chip, chip ^ mask) for chip in range(ways)])  85.9 us
    ppermute x64, starting transfers between devices, flip(): lax.ppermute(piece, 'dp', [(chip, chip ^ mask) for chip in range(ways)])  67.1 us
    ppermute x4, starting transfers between devices, to_h(): lax.ppermute(piece, 'dp', [(chip, (chip + 8 * step) % ways) for chip in r...  24.4 us
    ppermute x9, starting transfers between devices, core_swap(): return lax.ppermute(piece, 'mp', [(0, 1), (1, 0)])  21.7 us
    dot_general x21, matrix products, t_dot(): lax.dot_general(left, right, (((0,), (0,)), ((), ())), preferred_element_...  21.3 us
    sub x7, other arithmetic, adam(): weight * (1.0 - rate * DECAY) - rate * adam_step  17 us
    all_to_all x1, waiting for transfers between devices, shards(): lax.all_to_all(hook(ready, 'looked', looked).reshape(chips, frames, rows)...  15.1 us
    dot_general x7, matrix products, dot(): return jnp.dot(left, right, preferred_element_type=F32)  10.5 us
  transfers between devices with their start and end apart: 85, of which 29 were waited for; matrix products, arithmetic and copies ran while one was open for 24% of the time, Pallas kernels for 0%

profile of v3, /device:TPU:1, one launch (start us, length us, event | category | flops | bytes accessed | tf_op | source)
XLA Modules:
  0.0 378.9 jit_solution(10313949289842112190)
XLA Ops:
  4.9 8.0 %all-to-all-start = ((f32[16,1,672]{2,1,0:T(1,128)}), f32[16,1,672]{2,1,0:T(1,128)S(1)}, u32[]{:S(2)}, u32[]{:S(2)}) async-start(f32[16,1,672]{2,1,0:T(1,128)} %broadcast_in_dim.83), calls=%async_computation | async-start | bytes 98304 | tf_op jit(solution)/shard_map/all_to_all | solution.py:235
  25.8 2.2 fusion.11
  28.0 2.3 collective-permute-start.1
  30.3 2.1 maximum_select_fusion.1
  40.8 4.2 %all-to-all-start.1 = ((bf16[16,96,64]{1,2,0:T(8,128)(2,1)}), bf16[16,96,64]{1,2,0:T(8,128)(2,1)S(1)}, u32[]{:S(2)}, u32[]{:S(2)}) async-start(bf16[16,96,64]{1,2,0:T(8,128)(2,1)} %copy.296), calls=%async_computation.1 | async-start | bytes 524288 | tf_op jit(solution)/shard_map/all_to_all | solution.py:261
  45.1 5.3 %collective-permute-done.22 = bf16[64,1536]{1,0:T(8,128)(2,1)} collective-permute-done((bf16[64,1536]{1,0:T(8,128)(2,1)}, bf16[64,1536]{1,0:T(8,128)(2,1)}, u32[]{:S(2)}, u32[]{:S(2)}) %collective-permute-start.22) | collective-permute-done | bytes 196640 | tf_op jit(solution)/shard_map/ppermute | solution.py:44
  52.5 15.1 %all-to-all-done.1 = bf16[16,96,64]{1,2,0:T(8,128)(2,1)S(1)} async-done(((bf16[16,96,64]{1,2,0:T(8,128)(2,1)}), bf16[16,96,64]{1,2,0:T(8,128)(2,1)S(1)}, u32[]{:S(2)}, u32[]{:S(2)}) %all-to-all-start.1) | async-done | bytes 196640 | tf_op jit(solution)/shard_map/all_to_all | solution.py:261
  68.9 1.6 collective-permute-start.10
  70.6 1.8 collective-permute-start.4
  74.8 5.4 %collective-permute-done.10 = bf16[256,1024]{1,0:T(8,128)(2,1)S(1)} collective-permute-done((bf16[256,1024]{1,0:T(8,128)(2,1)}, bf16[256,1024]{1,0:T(8,128)(2,1)S(1)}, u32[]{:S(2)}, u32[]{:S(2)}) %collective-permute-start.10) | collective-permute-done | bytes 524320 | tf_op jit(solution)/shard_map/ppermute | solution.py:44
  80.2 1.6 collective-permute-start.29
  86.8 12.2 %collective-permute-done.24 = bf16[64,1280]{1,0:T(8,128)(2,1)S(1)} collective-permute-done((bf16[64,1280]{1,0:T(8,128)(2,1)S(1)}, bf16[64,1280]{1,0:T(8,128)(2,1)S(1)}, u32[]{:S(2)}, u32[]{:S(2)}) %collective-permute-start.24) | collective-permute-done | bytes 163872 | tf_op jit(solution)/shard_map/ppermute | solution.py:44
  99.0 4.9 %collective-permute-start.11 = (bf16[384,512]{1,0:T(8,128)(2,1)S(1)}, bf16[384,512]{1,0:T(8,128)(2,1)S(1)}, u32[]{:S(2)}, u32[]{:S(2)}) collective-permute-start(bf16[384,512]{1,0:T(8,128)(2,1)S(1)} %slice.530), channel_id=1, source_target_pairs={{0,1},{1,0},{2,3},{3,2},{4,5},{5,4},{6,7},{7,6},{8,9},{9,8},{10,11... | collective-permute-start | bytes 1179656 | tf_op jit(solution)/shard_map/ppermute | solution.py:39
  107.2 2.4 collective-permute-start.14
  112.1 2.2 collective-permute-done.14
  114.3 9.6 %collective-permute-done.13 = bf16[96,1024]{1,0:T(8,128)(2,1)S(1)} collective-permute-done((bf16[96,1024]{1,0:T(8,128)(2,1)S(1)}, bf16[96,1024]{1,0:T(8,128)(2,1)S(1)}, u32[]{:S(2)}, u32[]{:S(2)}) %collective-permute-start.13) | collective-permute-done | bytes 196640 | tf_op jit(solution)/shard_map/ppermute | solution.py:44
  126.0 2.2 collective-permute-start.16
  128.2 4.0 %collective-permute-done.17 = bf16[96,1024]{1,0:T(8,128)(2,1)S(1)} collective-permute-done((bf16[96,1024]{1,0:T(8,128)(2,1)S(1)}, bf16[96,1024]{1,0:T(8,128)(2,1)S(1)}, u32[]{:S(2)}, u32[]{:S(2)}) %collective-permute-start.17) | collective-permute-done | bytes 196640 | tf_op jit(solution)/shard_map/ppermute | solution.py:44
  132.3 2.6 collective-permute-start.15
  135.7 2.2 collective-permute-done.16
  138.8 3.1 fusion.38
  142.3 6.9 %collective-permute-done.31 = bf16[256,768]{1,0:T(8,128)(2,1)S(1)} collective-permute-done((bf16[256,768]{1,0:T(8,128)(2,1)S(1)}, bf16[256,768]{1,0:T(8,128)(2,1)S(1)}, u32[]{:S(2)}, u32[]{:S(2)}) %collective-permute-start.31) | collective-permute-done | bytes 393248 | tf_op jit(solution)/shard_map/ppermute | solution.py:44
  150.3 2.6 collective-permute-start.32
  155.8 2.6 collective-permute-done.33
  159.4 2.4 collective-permute-start.36
  163.4 1.7 collective-permute-done.37
  165.2 2.3 collective-permute-done.36
  168.8 2.0 fusion.247
  171.4 2.1 collective-permute-start.43
  177.8 5.1 %collective-permute-start.64 = (bf16[256,512]{1,0:T(8,128)(2,1)S(1)}, bf16[256,512]{1,0:T(8,128)(2,1)S(1)}, u32[]{:S(2)}, u32[]{:S(2)}) collective-permute-start(bf16[256,512]{1,0:T(8,128)(2,1)S(1)} %fusion.92), channel_id=1, source_target_pairs={{0,4},{2,6},{4,0},{6,2},{8,12},{10,14},{12,8},{14,10},{16,20},{18,... | collective-permute-start | bytes 786440 | tf_op jit(solution)/shard_map/ppermute | solution.py:44
  182.9 1.8 fusion.248
  188.7 1.6 collective-permute-done.46
  195.6 14.5 %collective-permute-start.66 = (bf16[256,512]{1,0:T(8,128)(2,1)S(1)}, bf16[256,512]{1,0:T(8,128)(2,1)S(1)}, u32[]{:S(2)}, u32[]{:S(2)}) collective-permute-start(bf16[256,512]{1,0:T(8,128)(2,1)S(1)} %convert_add_fusion.1), channel_id=1, source_target_pairs={{0,16},{2,18},{4,20},{6,22},{8,24},{10,26},{12,28},{14,30},{16,0},... | collective-permute-start | bytes 786440 | tf_op jit(solution)/shard_map/ppermute | solution.py:62
  212.6 1.5 convolution_convert_fusion.1
  216.1 2.5 fusion.249
  220.3 2.8 collective-permute-start.51
  224.5 2.3 collective-permute-done.51
  226.8 3.9 %collective-permute-done.50 = bf16[96,1024]{1,0:T(8,128)(2,1)S(1)} collective-permute-done((bf16[96,1024]{1,0:T(8,128)(2,1)S(1)}, bf16[96,1024]{1,0:T(8,128)(2,1)S(1)}, u32[]{:S(2)}, u32[]{:S(2)}) %collective-permute-start.50) | collective-permute-done | bytes 196640 | tf_op jit(solution)/shard_map/ppermute | solution.py:44
  231.7 2.2 collective-permute-start.53
  234.4 5.0 %collective-permute-start.69 = (bf16[256,768]{1,0:T(8,128)(2,1)S(1)}, bf16[256,768]{1,0:T(8,128)(2,1)S(1)}, u32[]{:S(2)}, u32[]{:S(2)}) collective-permute-start(bf16[256,768]{1,0:T(8,128)(2,1)S(1)} %convolution_add_fusion.2), channel_id=1, source_target_pairs={{0,16},{2,18},{4,20},{6,22},{8,24},{10,26},{12,28},{14,30},{16,0},... | collective-permute-start | bytes 1179656 | tf_op jit(solution)/shard_map/ppermute | solution.py:62
  239.9 2.7 collective-permute-done.53
  245.1 10.1 %collective-permute-start.56 = (bf16[384,512]{1,0:T(8,128)(2,1)S(1)}, bf16[384,512]{1,0:T(8,128)(2,1)S(1)}, u32[]{:S(2)}, u32[]{:S(2)}) collective-permute-start(bf16[384,512]{1,0:T(8,128)(2,1)S(1)} %pad_maximum_fusion.24), channel_id=1, source_target_pairs={{0,1},{1,0},{2,3},{3,2},{4,5},{5,4},{6,7},{7,6},{8,9},{9,8},{10,11... | collective-permute-start | bytes 1179656 | tf_op jit(solution)/shard_map/ppermute | solution.py:39
  258.1 1.5 convolution_add_fusion
  259.6 2.7 collective-permute-start.72
  266.3 2.4 collective-permute-start.75
  272.0 1.8 fusion.229
  275.1 8.6 %collective-permute-done.75 = bf16[96,1024]{1,0:T(8,128)(2,1)S(1)} collective-permute-done((bf16[96,1024]{1,0:T(8,128)(2,1)S(1)}, bf16[96,1024]{1,0:T(8,128)(2,1)S(1)}, u32[]{:S(2)}, u32[]{:S(2)}) %collective-permute-start.75) | collective-permute-done | bytes 196640 | tf_op jit(solution)/shard_map/ppermute | solution.py:44
  284.7 3.2 collective-permute-done.74
  290.5 5.4 %all-to-all-start.2 = ((bf16[16,112,64]{1,2,0:T(8,128)(2,1)}), bf16[16,112,64]{1,2,0:T(8,128)(2,1)S(1)}, u32[]{:S(2)}, u32[]{:S(2)}) async-start(bf16[16,112,64]{1,2,0:T(8,128)(2,1)} %bitcast.118), calls=%async_computation.2 | async-start | bytes 524288 | tf_op jit(solution)/shard_map/all_to_all | solution.py:410
  295.9 1.6 convolution_convert_fusion.5
  299.7 2.0 maximum_add_fusion.1
  301.6 2.3 collective-permute-start.59
  305.1 1.7 collective-permute-start.76
  307.0 3.3 fusion.227
  317.3 2.5 multiply_reduce_fusion.13
  319.8 7.1 %collective-permute-done.59 = bf16[256,1024]{1,0:T(8,128)(2,1)} collective-permute-done((bf16[256,1024]{1,0:T(8,128)(2,1)}, bf16[256,1024]{1,0:T(8,128)(2,1)}, u32[]{:S(2)}, u32[]{:S(2)}) %collective-permute-start.59) | collective-permute-done | bytes 524320 | tf_op jit(solution)/shard_map/ppermute | solution.py:62
  326.9 2.2 fusion.67
  331.7 7.4 %all-to-all-start.3 = ((f32[32,8,128]{2,1,0:T(8,128)}), f32[32,8,128]{2,1,0:T(8,128)S(1)}, u32[]{:S(2)}, u32[]{:S(2)}) async-start(f32[32,8,128]{2,1,0:T(8,128)} %broadcast_in_dim.92), calls=%async_computation.3 | async-start | bytes 262144 | tf_op jit(solution)/shard_map/all_to_all | solution.py:430
  339.1 1.5 collective-permute-start.61
  346.1 3.8 %collective-permute-done.62 = bf16[64,1024]{1,0:T(8,128)(2,1)S(1)} collective-permute-done((bf16[64,1024]{1,0:T(8,128)(2,1)S(1)}, bf16[64,1024]{1,0:T(8,128)(2,1)S(1)}, u32[]{:S(2)}, u32[]{:S(2)}) %collective-permute-start.62) | collective-permute-done | bytes 131104 | tf_op jit(solution)/shard_map/ppermute | solution.py:44
  355.4 2.2 multiply_subtract_fusion.4
  359.8 1.8 multiply_subtract_fusion.1
  365.5 7.5 %multiply_subtract_fusion = (f32[2,64,2,1408]{3,2,1,0:T(2,128)}, f32[2,64,2,1408]{3,2,1,0:T(2,128)}, f32[2,64,2,1408]{3,2,1,0:T(2,128)}) fusion(f32[2,64,2,1408]{3,2,1,0:T(2,128)S(1)} %copy-done, f32[]{:T(128)S(6)} %min.3, bf16[2,64,1,1408]{3,2,1,0:T(2,128)(2,1)S(1)} %copy.324, bf16[2,64,1,1408]{3,2,1,0:T(2,128)(2,1)S(1)} %copy.323, ...), kind=kLoop, calls=%fused_computation.27 | loop fusion | flops 6848512 | bytes 9371652 | tf_op jit(solution)/shard_map/sub | solution.py:184
  373.0 1.7 multiply_subtract_fusion.2
  (506 shorter events, 120.0 us)
Async XLA Ops:
  3.8 15.5 %collective-permute-start = (bf16[2,64,1024]{2,1,0:T(8,128)(2,1)}, bf16[2,64,1024]{2,1,0:T(8,128)(2,1)}, u32[]{:S(2)}, u32[]{:S(2)}) collective-permute-start(bf16[2,64,1024]{2,1,0:T(8,128)(2,1)} %pad_maximum_fusion.29), channel_id=1, source_target_pairs={{0,1},{1,0},{2,3},{3,2},{4,5},{5,4},{6,7},{7,6},{8,9},{9,8},{10,11... | collective-permute-start | bytes 786440 | tf_op jit(solution)/shard_map/ppermute | solution.py:39
  4.9 14.4 %all-to-all-start = ((f32[16,1,672]{2,1,0:T(1,128)}), f32[16,1,672]{2,1,0:T(1,128)S(1)}, u32[]{:S(2)}, u32[]{:S(2)}) async-start(f32[16,1,672]{2,1,0:T(1,128)} %broadcast_in_dim.83), calls=%async_computation | async-start | bytes 98304 | tf_op jit(solution)/shard_map/all_to_all | solution.py:235
  13.9 14.0 %collective-permute-start.18 = (bf16[2,64,1280]{2,1,0:T(8,128)(2,1)}, bf16[2,64,1280]{2,1,0:T(8,128)(2,1)}, u32[]{:S(2)}, u32[]{:S(2)}) collective-permute-start(bf16[2,64,1280]{2,1,0:T(8,128)(2,1)} %maximum_maximum_fusion), channel_id=1, source_target_pairs={{0,1},{1,0},{2,3},{3,2},{4,5},{5,4},{6,7},{7,6},{8,9},{9,8},{10,11... | collective-permute-start | bytes 983048 | tf_op jit(solution)/shard_map/ppermute | solution.py:39
  16.6 15.8 %collective-permute-start.19 = (bf16[2,64,1536]{2,1,0:T(8,128)(2,1)}, bf16[2,64,1536]{2,1,0:T(8,128)(2,1)}, u32[]{:S(2)}, u32[]{:S(2)}) collective-permute-start(bf16[2,64,1536]{2,1,0:T(8,128)(2,1)} %pad_maximum_fusion.23), channel_id=1, source_target_pairs={{0,1},{1,0},{2,3},{3,2},{4,5},{5,4},{6,7},{7,6},{8,9},{9,8},{10,11... | collective-permute-start | bytes 1179656 | tf_op jit(solution)/shard_map/ppermute | solution.py:39
  21.3 13.5 %collective-permute-start.6 = (bf16[64,1024]{1,0:T(8,128)(2,1)}, bf16[64,1024]{1,0:T(8,128)(2,1)}, u32[]{:S(2)}, u32[]{:S(2)}) collective-permute-start(bf16[64,1024]{1,0:T(8,128)(2,1)} %get-tuple-element.246), channel_id=1, source_target_pairs={{0,8},{2,10},{4,12},{6,14},{8,0},{10,2},{12,4},{14,6},{16,24},{18,... | collective-permute-start | bytes 393224 | tf_op jit(solution)/shard_map/ppermute | solution.py:44
  22.0 14.1 %collective-permute-start.7 = (bf16[64,1024]{1,0:T(8,128)(2,1)}, bf16[64,1024]{1,0:T(8,128)(2,1)}, u32[]{:S(2)}, u32[]{:S(2)}) collective-permute-start(bf16[64,1024]{1,0:T(8,128)(2,1)} %get-tuple-element.245), channel_id=1, source_target_pairs={{0,10},{2,8},{4,14},{6,12},{8,2},{10,0},{12,6},{14,4},{16,26},{18,... | collective-permute-start | bytes 393224 | tf_op jit(solution)/shard_map/ppermute | solution.py:44
  23.2 13.9 %collective-permute-start.5 = (bf16[64,1024]{1,0:T(8,128)(2,1)}, bf16[64,1024]{1,0:T(8,128)(2,1)}, u32[]{:S(2)}, u32[]{:S(2)}) collective-permute-start(bf16[64,1024]{1,0:T(8,128)(2,1)} %get-tuple-element.244), channel_id=1, source_target_pairs={{0,2},{2,0},{4,6},{6,4},{8,10},{10,8},{12,14},{14,12},{16,18},{18,... | collective-permute-start | bytes 393224 | tf_op jit(solution)/shard_map/ppermute | solution.py:44
  28.0 10.8 %collective-permute-start.1 = (bf16[1536,64]{0,1:T(8,128)(2,1)S(1)}, bf16[1536,64]{0,1:T(8,128)(2,1)S(1)}, u32[]{:S(2)}, u32[]{:S(2)}) collective-permute-start(bf16[1536,64]{0,1:T(8,128)(2,1)S(1)} %fusion.11), channel_id=1, source_target_pairs={{0,1},{1,0},{2,3},{3,2},{4,5},{5,4},{6,7},{7,6},{8,9},{9,8},{10,11... | collective-permute-start | bytes 589832 | tf_op jit(solution)/shard_map/ppermute | solution.py:39
  34.4 10.6 %collective-permute-start.21 = (bf16[64,1536]{1,0:T(8,128)(2,1)}, bf16[64,1536]{1,0:T(8,128)(2,1)}, u32[]{:S(2)}, u32[]{:S(2)}) collective-permute-start(bf16[64,1536]{1,0:T(8,128)(2,1)} %get-tuple-element.223), channel_id=1, source_target_pairs={{0,8},{2,10},{4,12},{6,14},{8,0},{10,2},{12,4},{14,6},{16,24},{18,... | collective-permute-start | bytes 589832 | tf_op jit(solution)/shard_map/ppermute | solution.py:44
  34.8 15.5 %collective-permute-start.22 = (bf16[64,1536]{1,0:T(8,128)(2,1)}, bf16[64,1536]{1,0:T(8,128)(2,1)}, u32[]{:S(2)}, u32[]{:S(2)}) collective-permute-start(bf16[64,1536]{1,0:T(8,128)(2,1)} %get-tuple-element.222), channel_id=1, source_target_pairs={{0,10},{2,8},{4,14},{6,12},{8,2},{10,0},{12,6},{14,4},{16,26},{18,... | collective-permute-start | bytes 589832 | tf_op jit(solution)/shard_map/ppermute | solution.py:44
  36.1 14.2 %collective-permute-start.20 = (bf16[64,1536]{1,0:T(8,128)(2,1)}, bf16[64,1536]{1,0:T(8,128)(2,1)}, u32[]{:S(2)}, u32[]{:S(2)}) collective-permute-start(bf16[64,1536]{1,0:T(8,128)(2,1)} %get-tuple-element.221), channel_id=1, source_target_pairs={{0,2},{2,0},{4,6},{6,4},{8,10},{10,8},{12,14},{14,12},{16,18},{18,... | collective-permute-start | bytes 589832 | tf_op jit(solution)/shard_map/ppermute | solution.py:44
  38.2 30.6 %collective-permute-start.8 = (bf16[256,1024]{1,0:T(8,128)(2,1)S(1)}, bf16[256,1024]{1,0:T(8,128)(2,1)}, u32[]{:S(2)}, u32[]{:S(2)}) collective-permute-start(bf16[256,1024]{1,0:T(8,128)(2,1)S(1)} %bitcast.413), channel_id=1, source_target_pairs={{0,16},{2,18},{4,20},{6,22},{8,24},{10,26},{12,28},{14,30},{16,0},... | collective-permute-start | bytes 1572872 | tf_op jit(solution)/shard_map/ppermute | solution.py:57
  38.7 34.6 %collective-permute-start.9 = (bf16[256,1024]{1,0:T(8,128)(2,1)S(1)}, bf16[256,1024]{1,0:T(8,128)(2,1)}, u32[]{:S(2)}, u32[]{:S(2)}) collective-permute-start(bf16[256,1024]{1,0:T(8,128)(2,1)S(1)} %bitcast.414), channel_id=1, source_target_pairs={{0,4},{2,6},{4,0},{6,2},{8,12},{10,14},{12,8},{14,10},{16,20},{18,... | collective-permute-start | bytes 1572872 | tf_op jit(solution)/shard_map/ppermute | solution.py:44
  40.8 26.8 %all-to-all-start.1 = ((bf16[16,96,64]{1,2,0:T(8,128)(2,1)}), bf16[16,96,64]{1,2,0:T(8,128)(2,1)S(1)}, u32[]{:S(2)}, u32[]{:S(2)}) async-start(bf16[16,96,64]{1,2,0:T(8,128)(2,1)} %copy.296), calls=%async_computation.1 | async-start | bytes 524288 | tf_op jit(solution)/shard_map/all_to_all | solution.py:261
  68.9 11.3 %collective-permute-start.10 = (bf16[256,1024]{1,0:T(8,128)(2,1)}, bf16[256,1024]{1,0:T(8,128)(2,1)S(1)}, u32[]{:S(2)}, u32[]{:S(2)}) collective-permute-start(bf16[256,1024]{1,0:T(8,128)(2,1)} %collective-permute-done.8), channel_id=1, source_target_pairs={{0,4},{2,6},{4,0},{6,2},{8,12},{10,14},{12,8},{14,10},{16,20},{18,... | collective-permute-start | bytes 1572872 | tf_op jit(solution)/shard_map/ppermute | solution.py:44
  70.6 12.5 %collective-permute-start.4 = (bf16[96,1024]{1,0:T(8,128)(2,1)S(1)}, bf16[96,1024]{1,0:T(8,128)(2,1)S(1)}, u32[]{:S(2)}, u32[]{:S(2)}) collective-permute-start(bf16[96,1024]{1,0:T(8,128)(2,1)S(1)} %multiply_convert_fusion.7), channel_id=1, source_target_pairs={{0,10},{2,8},{4,14},{6,12},{8,2},{10,0},{12,6},{14,4},{16,26},{18,... | collective-permute-start | bytes 589832 | tf_op jit(solution)/shard_map/ppermute | solution.py:44
  72.4 12.2 %collective-permute-start.3 = (bf16[96,1024]{1,0:T(8,128)(2,1)S(1)}, bf16[96,1024]{1,0:T(8,128)(2,1)S(1)}, u32[]{:S(2)}, u32[]{:S(2)}) collective-permute-start(bf16[96,1024]{1,0:T(8,128)(2,1)S(1)} %multiply_convert_fusion.7), channel_id=1, source_target_pairs={{0,8},{2,10},{4,12},{6,14},{8,0},{10,2},{12,4},{14,6},{16,24},{18,... | collective-permute-start | bytes 589832 | tf_op jit(solution)/shard_map/ppermute | solution.py:44
  72.8 12.6 %collective-permute-start.2 = (bf16[96,1024]{1,0:T(8,128)(2,1)S(1)}, bf16[96,1024]{1,0:T(8,128)(2,1)S(1)}, u32[]{:S(2)}, u32[]{:S(2)}) collective-permute-start(bf16[96,1024]{1,0:T(8,128)(2,1)S(1)} %multiply_convert_fusion.7), channel_id=1, source_target_pairs={{0,2},{2,0},{4,6},{6,4},{8,10},{10,8},{12,14},{14,12},{16,18},{18,... | collective-permute-start | bytes 589832 | tf_op jit(solution)/shard_map/ppermute | solution.py:44
  73.4 37.4 %collective-permute-start.28 = (bf16[256,1536]{1,0:T(8,128)(2,1)}, bf16[256,1536]{1,0:T(8,128)(2,1)S(1)}, u32[]{:S(2)}, u32[]{:S(2)}) collective-permute-start(bf16[256,1536]{1,0:T(8,128)(2,1)} %bitcast.84), channel_id=1, source_target_pairs={{0,16},{2,18},{4,20},{6,22},{8,24},{10,26},{12,28},{14,30},{16,0},... | collective-permute-start | bytes 2359304 | tf_op jit(solution)/shard_map/ppermute | solution.py:57
  80.2 58.6 %collective-permute-start.29 = (bf16[256,1536]{1,0:T(8,128)(2,1)}, bf16[256,1536]{1,0:T(8,128)(2,1)S(1)}, u32[]{:S(2)}, u32[]{:S(2)}) collective-permute-start(bf16[256,1536]{1,0:T(8,128)(2,1)} %bitcast.84), channel_id=1, source_target_pairs={{0,4},{2,6},{4,0},{6,2},{8,12},{10,14},{12,8},{14,10},{16,20},{18,... | collective-permute-start | bytes 2359304 | tf_op jit(solution)/shard_map/ppermute | solution.py:44
  83.1 15.8 %collective-permute-start.24 = (bf16[64,1280]{1,0:T(8,128)(2,1)S(1)}, bf16[64,1280]{1,0:T(8,128)(2,1)S(1)}, u32[]{:S(2)}, u32[]{:S(2)}) collective-permute-start(bf16[64,1280]{1,0:T(8,128)(2,1)S(1)} %get-tuple-element.238), channel_id=1, source_target_pairs={{0,8},{2,10},{4,12},{6,14},{8,0},{10,2},{12,4},{14,6},{16,24},{18,... | collective-permute-start | bytes 491528 | tf_op jit(solution)/shard_map/ppermute | solution.py:44
  84.6 19.3 %collective-permute-start.25 = (bf16[64,1280]{1,0:T(8,128)(2,1)S(1)}, bf16[64,1280]{1,0:T(8,128)(2,1)S(1)}, u32[]{:S(2)}, u32[]{:S(2)}) collective-permute-start(bf16[64,1280]{1,0:T(8,128)(2,1)S(1)} %get-tuple-element.237), channel_id=1, source_target_pairs={{0,10},{2,8},{4,14},{6,12},{8,2},{10,0},{12,6},{14,4},{16,26},{18,... | collective-permute-start | bytes 491528 | tf_op jit(solution)/shard_map/ppermute | solution.py:44
  85.4 18.5 %collective-permute-start.23 = (bf16[64,1280]{1,0:T(8,128)(2,1)S(1)}, bf16[64,1280]{1,0:T(8,128)(2,1)S(1)}, u32[]{:S(2)}, u32[]{:S(2)}) collective-permute-start(bf16[64,1280]{1,0:T(8,128)(2,1)S(1)} %get-tuple-element.236), channel_id=1, source_target_pairs={{0,2},{2,0},{4,6},{6,4},{8,10},{10,8},{12,14},{14,12},{16,18},{18,... | collective-permute-start | bytes 491528 | tf_op jit(solution)/shard_map/ppermute | solution.py:44
  109.6 14.3 %collective-permute-start.13 = (bf16[96,1024]{1,0:T(8,128)(2,1)S(1)}, bf16[96,1024]{1,0:T(8,128)(2,1)S(1)}, u32[]{:S(2)}, u32[]{:S(2)}) collective-permute-start(bf16[96,1024]{1,0:T(8,128)(2,1)S(1)} %get-tuple-element.226), channel_id=1, source_target_pairs={{0,8},{2,10},{4,12},{6,14},{8,0},{10,2},{12,4},{14,6},{16,24},{18,... | collective-permute-start | bytes 589832 | tf_op jit(solution)/shard_map/ppermute | solution.py:44
  109.6 14.3 %collective-permute-start.12 = (bf16[96,1024]{1,0:T(8,128)(2,1)S(1)}, bf16[96,1024]{1,0:T(8,128)(2,1)S(1)}, u32[]{:S(2)}, u32[]{:S(2)}) collective-permute-start(bf16[96,1024]{1,0:T(8,128)(2,1)S(1)} %get-tuple-element.224), channel_id=1, source_target_pairs={{0,2},{2,0},{4,6},{6,4},{8,10},{10,8},{12,14},{14,12},{16,18},{18,... | collective-permute-start | bytes 589832 | tf_op jit(solution)/shard_map/ppermute | solution.py:44
  110.8 13.9 %collective-permute-start.26 = (bf16[256,768]{1,0:T(8,128)(2,1)S(1)}, bf16[256,768]{1,0:T(8,128)(2,1)S(1)}, u32[]{:S(2)}, u32[]{:S(2)}) collective-permute-start(bf16[256,768]{1,0:T(8,128)(2,1)S(1)} %bitcast.434), channel_id=1, source_target_pairs={{0,16},{2,18},{4,20},{6,22},{8,24},{10,26},{12,28},{14,30},{16,0},... | collective-permute-start | bytes 1179656 | tf_op jit(solution)/shard_map/ppermute | solution.py:57
  114.3 24.5 %collective-permute-start.30 = (bf16[256,1536]{1,0:T(8,128)(2,1)S(1)}, bf16[256,1536]{1,0:T(8,128)(2,1)S(1)}, u32[]{:S(2)}, u32[]{:S(2)}) collective-permute-start(bf16[256,1536]{1,0:T(8,128)(2,1)S(1)} %collective-permute-done.28), channel_id=1, source_target_pairs={{0,4},{2,6},{4,0},{6,2},{8,12},{10,14},{12,8},{14,10},{16,20},{18,... | collective-permute-start | bytes 2359304 | tf_op jit(solution)/shard_map/ppermute | solution.py:44
  124.7 14.1 %collective-permute-start.27 = (bf16[256,768]{1,0:T(8,128)(2,1)S(1)}, bf16[256,768]{1,0:T(8,128)(2,1)S(1)}, u32[]{:S(2)}, u32[]{:S(2)}) collective-permute-start(bf16[256,768]{1,0:T(8,128)(2,1)S(1)} %collective-permute-done.26), channel_id=1, source_target_pairs={{0,4},{2,6},{4,0},{6,2},{8,12},{10,14},{12,8},{14,10},{16,20},{18,... | collective-permute-start | bytes 1179656 | tf_op jit(solution)/shard_map/ppermute | solution.py:44
  126.0 11.9 %collective-permute-start.16 = (bf16[96,1024]{1,0:T(8,128)(2,1)S(1)}, bf16[96,1024]{1,0:T(8,128)(2,1)S(1)}, u32[]{:S(2)}, u32[]{:S(2)}) collective-permute-start(bf16[96,1024]{1,0:T(8,128)(2,1)S(1)} %multiply_convert_fusion.6), channel_id=1, source_target_pairs={{0,8},{2,10},{4,12},{6,14},{8,0},{10,2},{12,4},{14,6},{16,24},{18,... | collective-permute-start | bytes 589832 | tf_op jit(solution)/shard_map/ppermute | solution.py:44
  137.9 11.3 %collective-permute-start.31 = (bf16[256,768]{1,0:T(8,128)(2,1)S(1)}, bf16[256,768]{1,0:T(8,128)(2,1)S(1)}, u32[]{:S(2)}, u32[]{:S(2)}) collective-permute-start(bf16[256,768]{1,0:T(8,128)(2,1)S(1)} %bitcast.435), channel_id=1, source_target_pairs={{0,4},{2,6},{4,0},{6,2},{8,12},{10,14},{12,8},{14,10},{16,20},{18,... | collective-permute-start | bytes 1179656 | tf_op jit(solution)/shard_map/ppermute | solution.py:44
  138.3 15.6 %collective-permute-start.38 = (bf16[256,512]{1,0:T(8,128)(2,1)}, bf16[256,512]{1,0:T(8,128)(2,1)}, u32[]{:S(2)}, u32[]{:S(2)}) collective-permute-start(bf16[256,512]{1,0:T(8,128)(2,1)} %bitcast.86), channel_id=1, source_target_pairs={{0,16},{2,18},{4,20},{6,22},{8,24},{10,26},{12,28},{14,30},{16,0},... | collective-permute-start | bytes 786440 | tf_op jit(solution)/shard_map/ppermute | solution.py:57
  150.2 8.2 %collective-permute-start.33 = (bf16[96,1024]{1,0:T(8,128)(2,1)S(1)}, bf16[96,1024]{1,0:T(8,128)(2,1)S(1)}, u32[]{:S(2)}, u32[]{:S(2)}) collective-permute-start(bf16[96,1024]{1,0:T(8,128)(2,1)S(1)} %get-tuple-element.220), channel_id=1, source_target_pairs={{0,8},{2,10},{4,12},{6,14},{8,0},{10,2},{12,4},{14,6},{16,24},{18,... | collective-permute-start | bytes 589832 | tf_op jit(solution)/shard_map/ppermute | solution.py:44
  153.4 15.4 %collective-permute-start.39 = (bf16[256,512]{1,0:T(8,128)(2,1)}, bf16[256,512]{1,0:T(8,128)(2,1)}, u32[]{:S(2)}, u32[]{:S(2)}) collective-permute-start(bf16[256,512]{1,0:T(8,128)(2,1)} %bitcast.86), channel_id=1, source_target_pairs={{0,4},{2,6},{4,0},{6,2},{8,12},{10,14},{12,8},{14,10},{16,20},{18,... | collective-permute-start | bytes 786440 | tf_op jit(solution)/shard_map/ppermute | solution.py:44
  153.9 14.9 %collective-permute-start.40 = (bf16[256,512]{1,0:T(8,128)(2,1)}, bf16[256,512]{1,0:T(8,128)(2,1)}, u32[]{:S(2)}, u32[]{:S(2)}) collective-permute-start(bf16[256,512]{1,0:T(8,128)(2,1)} %collective-permute-done.38), channel_id=1, source_target_pairs={{0,4},{2,6},{4,0},{6,2},{8,12},{10,14},{12,8},{14,10},{16,20},{18,... | collective-permute-start | bytes 786440 | tf_op jit(solution)/shard_map/ppermute | solution.py:44
  177.8 17.7 %collective-permute-start.64 = (bf16[256,512]{1,0:T(8,128)(2,1)S(1)}, bf16[256,512]{1,0:T(8,128)(2,1)S(1)}, u32[]{:S(2)}, u32[]{:S(2)}) collective-permute-start(bf16[256,512]{1,0:T(8,128)(2,1)S(1)} %fusion.92), channel_id=1, source_target_pairs={{0,4},{2,6},{4,0},{6,2},{8,12},{10,14},{12,8},{14,10},{16,20},{18,... | collective-permute-start | bytes 786440 | tf_op jit(solution)/shard_map/ppermute | solution.py:44
  192.8 18.0 %collective-permute-start.49 = (bf16[96,1024]{1,0:T(8,128)(2,1)S(1)}, bf16[96,1024]{1,0:T(8,128)(2,1)S(1)}, u32[]{:S(2)}, u32[]{:S(2)}) collective-permute-start(bf16[96,1024]{1,0:T(8,128)(2,1)S(1)} %fusion.211), channel_id=1, source_target_pairs={{0,10},{2,8},{4,14},{6,12},{8,2},{10,0},{12,6},{14,4},{16,26},{18,... | collective-permute-start | bytes 589832 | tf_op jit(solution)/shard_map/ppermute | solution.py:44
  194.0 16.8 %collective-permute-start.48 = (bf16[96,1024]{1,0:T(8,128)(2,1)S(1)}, bf16[96,1024]{1,0:T(8,128)(2,1)S(1)}, u32[]{:S(2)}, u32[]{:S(2)}) collective-permute-start(bf16[96,1024]{1,0:T(8,128)(2,1)S(1)} %fusion.211), channel_id=1, source_target_pairs={{0,8},{2,10},{4,12},{6,14},{8,0},{10,2},{12,4},{14,6},{16,24},{18,... | collective-permute-start | bytes 589832 | tf_op jit(solution)/shard_map/ppermute | solution.py:44
  194.4 16.4 %collective-permute-start.47 = (bf16[96,1024]{1,0:T(8,128)(2,1)S(1)}, bf16[96,1024]{1,0:T(8,128)(2,1)S(1)}, u32[]{:S(2)}, u32[]{:S(2)}) collective-permute-start(bf16[96,1024]{1,0:T(8,128)(2,1)S(1)} %fusion.211), channel_id=1, source_target_pairs={{0,2},{2,0},{4,6},{6,4},{8,10},{10,8},{12,14},{14,12},{16,18},{18,... | collective-permute-start | bytes 589832 | tf_op jit(solution)/shard_map/ppermute | solution.py:44
  195.6 24.7 %collective-permute-start.66 = (bf16[256,512]{1,0:T(8,128)(2,1)S(1)}, bf16[256,512]{1,0:T(8,128)(2,1)S(1)}, u32[]{:S(2)}, u32[]{:S(2)}) collective-permute-start(bf16[256,512]{1,0:T(8,128)(2,1)S(1)} %convert_add_fusion.1), channel_id=1, source_target_pairs={{0,16},{2,18},{4,20},{6,22},{8,24},{10,26},{12,28},{14,30},{16,0},... | collective-permute-start | bytes 786440 | tf_op jit(solution)/shard_map/ppermute | solution.py:62
  210.1 13.0 %collective-permute-start.65 = (bf16[256,512]{1,0:T(8,128)(2,1)S(1)}, bf16[256,512]{1,0:T(8,128)(2,1)S(1)}, u32[]{:S(2)}, u32[]{:S(2)}) collective-permute-start(bf16[256,512]{1,0:T(8,128)(2,1)S(1)} %fusion.94), channel_id=1, source_target_pairs={{0,4},{2,6},{4,0},{6,2},{8,12},{10,14},{12,8},{14,10},{16,20},{18,... | collective-permute-start | bytes 786440 | tf_op jit(solution)/shard_map/ppermute | solution.py:44
  214.5 19.4 %collective-permute-start.67 = (bf16[256,768]{1,0:T(8,128)(2,1)S(1)}, bf16[256,768]{1,0:T(8,128)(2,1)S(1)}, u32[]{:S(2)}, u32[]{:S(2)}) collective-permute-start(bf16[256,768]{1,0:T(8,128)(2,1)S(1)} %convolution_convert_fusion.2), channel_id=1, source_target_pairs={{0,4},{2,6},{4,0},{6,2},{8,12},{10,14},{12,8},{14,10},{16,20},{18,... | collective-permute-start | bytes 1179656 | tf_op jit(solution)/shard_map/ppermute | solution.py:44
  215.4 42.7 %collective-permute-start.70 = (bf16[256,1536]{1,0:T(8,128)(2,1)S(1)}, bf16[256,1536]{1,0:T(8,128)(2,1)S(1)}, u32[]{:S(2)}, u32[]{:S(2)}) collective-permute-start(bf16[256,1536]{1,0:T(8,128)(2,1)S(1)} %convolution_convert_fusion), channel_id=1, source_target_pairs={{0,4},{2,6},{4,0},{6,2},{8,12},{10,14},{12,8},{14,10},{16,20},{18,... | collective-permute-start | bytes 2359304 | tf_op jit(solution)/shard_map/ppermute | solution.py:44
  231.3 8.6 %collective-permute-start.54 = (bf16[96,1024]{1,0:T(8,128)(2,1)S(1)}, bf16[96,1024]{1,0:T(8,128)(2,1)S(1)}, u32[]{:S(2)}, u32[]{:S(2)}) collective-permute-start(bf16[96,1024]{1,0:T(8,128)(2,1)S(1)} %get-tuple-element.159), channel_id=1, source_target_pairs={{0,8},{2,10},{4,12},{6,14},{8,0},{10,2},{12,4},{14,6},{16,24},{18,... | collective-permute-start | bytes 589832 | tf_op jit(solution)/shard_map/ppermute | solution.py:44
  231.7 10.9 %collective-permute-start.53 = (bf16[96,1024]{1,0:T(8,128)(2,1)S(1)}, bf16[96,1024]{1,0:T(8,128)(2,1)S(1)}, u32[]{:S(2)}, u32[]{:S(2)}) collective-permute-start(bf16[96,1024]{1,0:T(8,128)(2,1)S(1)} %get-tuple-element.159), channel_id=1, source_target_pairs={{0,2},{2,0},{4,6},{6,4},{8,10},{10,8},{12,14},{14,12},{16,18},{18,... | collective-permute-start | bytes 589832 | tf_op jit(solution)/shard_map/ppermute | solution.py:44
  234.4 36.5 %collective-permute-start.69 = (bf16[256,768]{1,0:T(8,128)(2,1)S(1)}, bf16[256,768]{1,0:T(8,128)(2,1)S(1)}, u32[]{:S(2)}, u32[]{:S(2)}) collective-permute-start(bf16[256,768]{1,0:T(8,128)(2,1)S(1)} %convolution_add_fusion.2), channel_id=1, source_target_pairs={{0,16},{2,18},{4,20},{6,22},{8,24},{10,26},{12,28},{14,30},{16,0},... | collective-permute-start | bytes 1179656 | tf_op jit(solution)/shard_map/ppermute | solution.py:62
  239.3 31.5 %collective-permute-start.68 = (bf16[256,768]{1,0:T(8,128)(2,1)S(1)}, bf16[256,768]{1,0:T(8,128)(2,1)S(1)}, u32[]{:S(2)}, u32[]{:S(2)}) collective-permute-start(bf16[256,768]{1,0:T(8,128)(2,1)S(1)} %convolution_convert_fusion.3), channel_id=1, source_target_pairs={{0,4},{2,6},{4,0},{6,2},{8,12},{10,14},{12,8},{14,10},{16,20},{18,... | collective-permute-start | bytes 1179656 | tf_op jit(solution)/shard_map/ppermute | solution.py:44
  245.1 18.1 %collective-permute-start.56 = (bf16[384,512]{1,0:T(8,128)(2,1)S(1)}, bf16[384,512]{1,0:T(8,128)(2,1)S(1)}, u32[]{:S(2)}, u32[]{:S(2)}) collective-permute-start(bf16[384,512]{1,0:T(8,128)(2,1)S(1)} %pad_maximum_fusion.24), channel_id=1, source_target_pairs={{0,1},{1,0},{2,3},{3,2},{4,5},{5,4},{6,7},{7,6},{8,9},{9,8},{10,11... | collective-permute-start | bytes 1179656 | tf_op jit(solution)/shard_map/ppermute | solution.py:39
  259.6 47.4 %collective-permute-start.72 = (bf16[256,1536]{1,0:T(8,128)(2,1)}, bf16[256,1536]{1,0:T(8,128)(2,1)}, u32[]{:S(2)}, u32[]{:S(2)}) collective-permute-start(bf16[256,1536]{1,0:T(8,128)(2,1)} %convolution_add_fusion), channel_id=1, source_target_pairs={{0,16},{2,18},{4,20},{6,22},{8,24},{10,26},{12,28},{14,30},{16,0},... | collective-permute-start | bytes 2359304 | tf_op jit(solution)/shard_map/ppermute | solution.py:62
  262.3 44.7 %collective-permute-start.71 = (bf16[256,1536]{1,0:T(8,128)(2,1)}, bf16[256,1536]{1,0:T(8,128)(2,1)}, u32[]{:S(2)}, u32[]{:S(2)}) collective-permute-start(bf16[256,1536]{1,0:T(8,128)(2,1)} %convolution_convert_fusion.1), channel_id=1, source_target_pairs={{0,4},{2,6},{4,0},{6,2},{8,12},{10,14},{12,8},{14,10},{16,20},{18,... | collective-permute-start | bytes 2359304 | tf_op jit(solution)/shard_map/ppermute | solution.py:44
  266.3 17.3 %collective-permute-start.75 = (bf16[96,1024]{1,0:T(8,128)(2,1)S(1)}, bf16[96,1024]{1,0:T(8,128)(2,1)S(1)}, u32[]{:S(2)}, u32[]{:S(2)}) collective-permute-start(bf16[96,1024]{1,0:T(8,128)(2,1)S(1)} %get-tuple-element.210), channel_id=1, source_target_pairs={{0,10},{2,8},{4,14},{6,12},{8,2},{10,0},{12,6},{14,4},{16,26},{18,... | collective-permute-start | bytes 589832 | tf_op jit(solution)/shard_map/ppermute | solution.py:44
  270.9 17.0 %collective-permute-start.74 = (bf16[96,1024]{1,0:T(8,128)(2,1)S(1)}, bf16[96,1024]{1,0:T(8,128)(2,1)S(1)}, u32[]{:S(2)}, u32[]{:S(2)}) collective-permute-start(bf16[96,1024]{1,0:T(8,128)(2,1)S(1)} %get-tuple-element.211), channel_id=1, source_target_pairs={{0,8},{2,10},{4,12},{6,14},{8,0},{10,2},{12,4},{14,6},{16,24},{18,... | collective-permute-start | bytes 589832 | tf_op jit(solution)/shard_map/ppermute | solution.py:44
  270.9 17.0 %collective-permute-start.73 = (bf16[96,1024]{1,0:T(8,128)(2,1)S(1)}, bf16[96,1024]{1,0:T(8,128)(2,1)S(1)}, u32[]{:S(2)}, u32[]{:S(2)}) collective-permute-start(bf16[96,1024]{1,0:T(8,128)(2,1)S(1)} %get-tuple-element.209), channel_id=1, source_target_pairs={{0,2},{2,0},{4,6},{6,4},{8,10},{10,8},{12,14},{14,12},{16,18},{18,... | collective-permute-start | bytes 589832 | tf_op jit(solution)/shard_map/ppermute | solution.py:44
  283.7 16.0 %collective-permute-start.57 = (bf16[256,1024]{1,0:T(8,128)(2,1)}, bf16[256,1024]{1,0:T(8,128)(2,1)}, u32[]{:S(2)}, u32[]{:S(2)}) collective-permute-start(bf16[256,1024]{1,0:T(8,128)(2,1)} %pad_maximum_fusion.21), channel_id=1, source_target_pairs={{0,4},{2,6},{4,0},{6,2},{8,12},{10,14},{12,8},{14,10},{16,20},{18,... | collective-permute-start | bytes 1572872 | tf_op jit(solution)/shard_map/ppermute | solution.py:44
  290.5 14.6 %all-to-all-start.2 = ((bf16[16,112,64]{1,2,0:T(8,128)(2,1)}), bf16[16,112,64]{1,2,0:T(8,128)(2,1)S(1)}, u32[]{:S(2)}, u32[]{:S(2)}) async-start(bf16[16,112,64]{1,2,0:T(8,128)(2,1)} %bitcast.118), calls=%async_computation.2 | async-start | bytes 524288 | tf_op jit(solution)/shard_map/all_to_all | solution.py:410
  301.6 25.2 %collective-permute-start.59 = (bf16[256,1024]{1,0:T(8,128)(2,1)}, bf16[256,1024]{1,0:T(8,128)(2,1)}, u32[]{:S(2)}, u32[]{:S(2)}) collective-permute-start(bf16[256,1024]{1,0:T(8,128)(2,1)} %maximum_add_fusion.1), channel_id=1, source_target_pairs={{0,16},{2,18},{4,20},{6,22},{8,24},{10,26},{12,28},{14,30},{16,0},... | collective-permute-start | bytes 1572872 | tf_op jit(solution)/shard_map/ppermute | solution.py:62
  303.9 23.0 %collective-permute-start.58 = (bf16[256,1024]{1,0:T(8,128)(2,1)}, bf16[256,1024]{1,0:T(8,128)(2,1)}, u32[]{:S(2)}, u32[]{:S(2)}) collective-permute-start(bf16[256,1024]{1,0:T(8,128)(2,1)} %pad_maximum_fusion.20), channel_id=1, source_target_pairs={{0,4},{2,6},{4,0},{6,2},{8,12},{10,14},{12,8},{14,10},{16,20},{18,... | collective-permute-start | bytes 1572872 | tf_op jit(solution)/shard_map/ppermute | solution.py:44
  305.1 9.4 %collective-permute-start.76 = (bf16[16,112,64]{1,2,0:T(8,128)(2,1)S(1)}, bf16[16,112,64]{1,2,0:T(8,128)(2,1)S(1)}, u32[]{:S(2)}, u32[]{:S(2)}) collective-permute-start(bf16[16,112,64]{1,2,0:T(8,128)(2,1)S(1)} %all-to-all-done.2), channel_id=1, source_target_pairs={{0,1},{1,0},{2,3},{3,2},{4,5},{5,4},{6,7},{7,6},{8,9},{9,8},{10,11... | collective-permute-start | bytes 688136 | tf_op jit(solution)/shard_map/ppermute | solution.py:39
  311.4 30.3 %collective-permute-start.78 = (bf16[64,2816]{1,0:T(8,128)(2,1)}, bf16[64,2816]{1,0:T(8,128)(2,1)}, u32[]{:S(2)}, u32[]{:S(2)}) collective-permute-start(bf16[64,2816]{1,0:T(8,128)(2,1)} %get-tuple-element.181), channel_id=1, source_target_pairs={{0,8},{2,10},{4,12},{6,14},{8,0},{10,2},{12,4},{14,6},{16,24},{18,... | collective-permute-start | bytes 1081352 | tf_op jit(solution)/shard_map/ppermute | solution.py:44
  312.6 29.2 %collective-permute-start.79 = (bf16[64,2816]{1,0:T(8,128)(2,1)}, bf16[64,2816]{1,0:T(8,128)(2,1)}, u32[]{:S(2)}, u32[]{:S(2)}) collective-permute-start(bf16[64,2816]{1,0:T(8,128)(2,1)} %get-tuple-element.180), channel_id=1, source_target_pairs={{0,10},{2,8},{4,14},{6,12},{8,2},{10,0},{12,6},{14,4},{16,26},{18,... | collective-permute-start | bytes 1081352 | tf_op jit(solution)/shard_map/ppermute | solution.py:44
  314.5 27.4 %collective-permute-start.77 = (bf16[64,2816]{1,0:T(8,128)(2,1)}, bf16[64,2816]{1,0:T(8,128)(2,1)}, u32[]{:S(2)}, u32[]{:S(2)}) collective-permute-start(bf16[64,2816]{1,0:T(8,128)(2,1)} %get-tuple-element.179), channel_id=1, source_target_pairs={{0,2},{2,0},{4,6},{6,4},{8,10},{10,8},{12,14},{14,12},{16,18},{18,... | collective-permute-start | bytes 1081352 | tf_op jit(solution)/shard_map/ppermute | solution.py:44
  331.7 20.3 %all-to-all-start.3 = ((f32[32,8,128]{2,1,0:T(8,128)}), f32[32,8,128]{2,1,0:T(8,128)S(1)}, u32[]{:S(2)}, u32[]{:S(2)}) async-start(f32[32,8,128]{2,1,0:T(8,128)} %broadcast_in_dim.92), calls=%async_computation.3 | async-start | bytes 262144 | tf_op jit(solution)/shard_map/all_to_all | solution.py:430
  340.6 9.4 %collective-permute-start.62 = (bf16[64,1024]{1,0:T(8,128)(2,1)S(1)}, bf16[64,1024]{1,0:T(8,128)(2,1)S(1)}, u32[]{:S(2)}, u32[]{:S(2)}) collective-permute-start(bf16[64,1024]{1,0:T(8,128)(2,1)S(1)} %get-tuple-element.240), channel_id=1, source_target_pairs={{0,10},{2,8},{4,14},{6,12},{8,2},{10,0},{12,6},{14,4},{16,26},{18,... | collective-permute-start | bytes 393224 | tf_op jit(solution)/shard_map/ppermute | solution.py:44
  341.8 8.2 %collective-permute-start.60 = (bf16[64,1024]{1,0:T(8,128)(2,1)S(1)}, bf16[64,1024]{1,0:T(8,128)(2,1)S(1)}, u32[]{:S(2)}, u32[]{:S(2)}) collective-permute-start(bf16[64,1024]{1,0:T(8,128)(2,1)S(1)} %get-tuple-element.239), channel_id=1, source_target_pairs={{0,2},{2,0},{4,6},{6,4},{8,10},{10,8},{12,14},{14,12},{16,18},{18,... | collective-permute-start | bytes 393224 | tf_op jit(solution)/shard_map/ppermute | solution.py:44
  344.3 17.3 %collective-permute-start.80 = (bf16[2,64,2816]{2,1,0:T(8,128)(2,1)}, bf16[2,64,2816]{2,1,0:T(8,128)(2,1)}, u32[]{:S(2)}, u32[]{:S(2)}) collective-permute-start(bf16[2,64,2816]{2,1,0:T(8,128)(2,1)} %dynamic-slice_bitcast_fusion), channel_id=1, source_target_pairs={{0,1},{1,0},{2,3},{3,2},{4,5},{5,4},{6,7},{7,6},{8,9},{9,8},{10,11... | collective-permute-start | bytes 2162696 | tf_op jit(solution)/shard_map/ppermute | solution.py:39
  (98 other events, 985.6 us)

commit v4 on v3

--- a/solution.py
+++ b/solution.py
@@ -424,10 +424,10 @@
         + jnp.sum(grad_embed * grad_embed)
         + jnp.sum(gain_mine * gain_mine)
     )
-    tally_lane = lax.broadcasted_iota(jnp.int32, (8, LANE), 1)
+    tally_lane = lax.broadcasted_iota(jnp.int32, (1, LANE), 1)
     tally = jnp.where(tally_lane == 0, squares, jnp.where(tally_lane == 1, loss_local, 0.0))
     ways = chips * lax.axis_size("mp")
-    tally = lax.all_to_all(jnp.broadcast_to(tally[None], (ways, 8, LANE)), ("dp", "mp"), 0, 0)
+    tally = lax.all_to_all(jnp.broadcast_to(tally[None], (ways, 1, LANE)), ("dp", "mp"), 0, 0)
     tally = jnp.sum(tally[:, 0], axis=0)
     grad_norm = jnp.sqrt(tally[0])
     loss = tally[1] / total_count

time: 385 us -> 385 us (level)
  starting transfers between devices: 142 us -> 131 us
  waiting for transfers between devices: 109 us -> 118 us
    ppermute x4, waiting for transfers between devices: 0.01 us -> 5.92 us  [from_h(): lax.ppermute(piece, 'dp', [(chip, (chip - 8 * step) % ways) for chip in r...]
    ppermute x4, starting transfers between devices: 24.4 us -> 18.5 us  [to_h(): lax.ppermute(piece, 'dp', [(chip, (chip + 8 * step) % ways) for chip in r...]
    ppermute x64, starting transfers between devices: 67.1 us -> 62.9 us  [flip(): lax.ppermute(piece, 'dp', [(chip, chip ^ mask) for chip in range(ways)])]
  transfers between devices with their start and end apart: 85 -> 85, of which waited for: 29 -> 32; matrix products, arithmetic and copies ran while one was open for 24% -> 24% of each run, Pallas kernels for 0% -> 0%
where the time goes in v4:
time: 385 us; the launch traced here: 378 us
  starting transfers between devices  131 us (34%)
  waiting for transfers between devices  118 us (31%)
  other arithmetic  49.7 us (13%)
  matrix products  43.1 us (11%)
  local copies, waits for them, and re-layouts  25.2 us (7%)
  between operations  11.5 us (3%)
    ppermute x64, waiting for transfers between devices, flip(): lax.ppermute(piece, 'dp', [(chip, chip ^ mask) for chip in range(ways)])  84 us
    ppermute x64, starting transfers between devices, flip(): lax.ppermute(piece, 'dp', [(chip, chip ^ mask) for chip in range(ways)])  62.9 us
    ppermute x9, starting transfers between devices, core_swap(): return lax.ppermute(piece, 'mp', [(0, 1), (1, 0)])  21.1 us
    dot_general x21, matrix products, t_dot(): lax.dot_general(left, right, (((0,), (0,)), ((), ())), preferred_element_...  20 us
    ppermute x4, starting transfers between devices, to_h(): lax.ppermute(piece, 'dp', [(chip, (chip + 8 * step) % ways) for chip in r...  18.5 us
    sub x7, other arithmetic, adam(): weight * (1.0 - rate * DECAY) - rate * adam_step  17 us
    all_to_all x1, waiting for transfers between devices, shards(): lax.all_to_all(hook(ready, 'looked', looked).reshape(chips, frames, rows)...  15.1 us
    dot_general x7, matrix products, dot(): return jnp.dot(left, right, preferred_element_type=F32)  11.8 us
  transfers between devices with their start and end apart: 85, of which 32 were waited for; matrix products, arithmetic and copies ran while one was open for 24% of the time, Pallas kernels for 0%

profile of v4, /device:TPU:1, one launch (start us, length us, event | category | flops | bytes accessed | tf_op | source)
XLA Modules:
  0.0 378.3 jit_solution(15605092689292446844)
XLA Ops:
  4.9 8.0 %all-to-all-start = ((f32[16,1,672]{2,1,0:T(1,128)}), f32[16,1,672]{2,1,0:T(1,128)S(1)}, u32[]{:S(2)}, u32[]{:S(2)}) async-start(f32[16,1,672]{2,1,0:T(1,128)} %broadcast_in_dim.83), calls=%async_computation | async-start | bytes 98304 | tf_op jit(solution)/shard_map/all_to_all | solution.py:235
  25.8 2.2 fusion.11
  28.0 2.3 collective-permute-start.1
  30.3 2.1 maximum_select_fusion.1
  40.9 4.2 %all-to-all-start.1 = ((bf16[16,96,64]{1,2,0:T(8,128)(2,1)}), bf16[16,96,64]{1,2,0:T(8,128)(2,1)S(1)}, u32[]{:S(2)}, u32[]{:S(2)}) async-start(bf16[16,96,64]{1,2,0:T(8,128)(2,1)} %copy.296), calls=%async_computation.1 | async-start | bytes 524288 | tf_op jit(solution)/shard_map/all_to_all | solution.py:261
  45.1 5.3 %collective-permute-done.22 = bf16[64,1536]{1,0:T(8,128)(2,1)} collective-permute-done((bf16[64,1536]{1,0:T(8,128)(2,1)}, bf16[64,1536]{1,0:T(8,128)(2,1)}, u32[]{:S(2)}, u32[]{:S(2)}) %collective-permute-start.22) | collective-permute-done | bytes 196640 | tf_op jit(solution)/shard_map/ppermute | solution.py:44
  52.6 15.1 %all-to-all-done.1 = bf16[16,96,64]{1,2,0:T(8,128)(2,1)S(1)} async-done(((bf16[16,96,64]{1,2,0:T(8,128)(2,1)}), bf16[16,96,64]{1,2,0:T(8,128)(2,1)S(1)}, u32[]{:S(2)}, u32[]{:S(2)}) %all-to-all-start.1) | async-done | bytes 196640 | tf_op jit(solution)/shard_map/all_to_all | solution.py:261
  68.9 1.6 collective-permute-start.10
  70.6 1.8 collective-permute-start.4
  74.9 5.4 %collective-permute-done.10 = bf16[256,1024]{1,0:T(8,128)(2,1)S(1)} collective-permute-done((bf16[256,1024]{1,0:T(8,128)(2,1)}, bf16[256,1024]{1,0:T(8,128)(2,1)S(1)}, u32[]{:S(2)}, u32[]{:S(2)}) %collective-permute-start.10) | collective-permute-done | bytes 524320 | tf_op jit(solution)/shard_map/ppermute | solution.py:44
  80.2 1.7 collective-permute-start.29
  86.9 12.1 %collective-permute-done.24 = bf16[64,1280]{1,0:T(8,128)(2,1)S(1)} collective-permute-done((bf16[64,1280]{1,0:T(8,128)(2,1)S(1)}, bf16[64,1280]{1,0:T(8,128)(2,1)S(1)}, u32[]{:S(2)}, u32[]{:S(2)}) %collective-permute-start.24) | collective-permute-done | bytes 163872 | tf_op jit(solution)/shard_map/ppermute | solution.py:44
  99.0 4.9 %collective-permute-start.11 = (bf16[384,512]{1,0:T(8,128)(2,1)S(1)}, bf16[384,512]{1,0:T(8,128)(2,1)S(1)}, u32[]{:S(2)}, u32[]{:S(2)}) collective-permute-start(bf16[384,512]{1,0:T(8,128)(2,1)S(1)} %slice.526), channel_id=1, source_target_pairs={{0,1},{1,0},{2,3},{3,2},{4,5},{5,4},{6,7},{7,6},{8,9},{9,8},{10,11... | collective-permute-start | bytes 1179656 | tf_op jit(solution)/shard_map/ppermute | solution.py:39
  107.4 2.4 collective-permute-start.14
  114.5 8.0 %collective-permute-done.13 = bf16[96,1024]{1,0:T(8,128)(2,1)S(1)} collective-permute-done((bf16[96,1024]{1,0:T(8,128)(2,1)S(1)}, bf16[96,1024]{1,0:T(8,128)(2,1)S(1)}, u32[]{:S(2)}, u32[]{:S(2)}) %collective-permute-start.13) | collective-permute-done | bytes 196640 | tf_op jit(solution)/shard_map/ppermute | solution.py:44
  124.0 5.9 %collective-permute-done.26 = bf16[256,768]{1,0:T(8,128)(2,1)} collective-permute-done((bf16[256,768]{1,0:T(8,128)(2,1)}, bf16[256,768]{1,0:T(8,128)(2,1)}, u32[]{:S(2)}, u32[]{:S(2)}) %collective-permute-start.26) | collective-permute-done | bytes 393248 | tf_op jit(solution)/shard_map/ppermute | solution.py:57
  130.0 4.8 %collective-permute-start.15 = (bf16[96,1024]{1,0:T(8,128)(2,1)S(1)}, bf16[96,1024]{1,0:T(8,128)(2,1)S(1)}, u32[]{:S(2)}, u32[]{:S(2)}) collective-permute-start(bf16[96,1024]{1,0:T(8,128)(2,1)S(1)} %multiply_convert_fusion.6), channel_id=1, source_target_pairs={{0,2},{2,0},{4,6},{6,4},{8,10},{10,8},{12,14},{14,12},{16,18},{18,... | collective-permute-start | bytes 589832 | tf_op jit(solution)/shard_map/ppermute | solution.py:44
  135.6 2.2 collective-permute-done.16
  138.7 2.7 collective-permute-done.27
  141.4 3.1 fusion.38
  144.9 4.9 %collective-permute-done.31 = bf16[256,768]{1,0:T(8,128)(2,1)S(1)} collective-permute-done((bf16[256,768]{1,0:T(8,128)(2,1)}, bf16[256,768]{1,0:T(8,128)(2,1)S(1)}, u32[]{:S(2)}, u32[]{:S(2)}) %collective-permute-start.31) | collective-permute-done | bytes 393248 | tf_op jit(solution)/shard_map/ppermute | solution.py:44
  149.8 2.2 fusion.246
  152.2 2.6 collective-permute-start.32
  158.4 4.2 %collective-permute-done.32 = bf16[96,1024]{1,0:T(8,128)(2,1)S(1)} collective-permute-done((bf16[96,1024]{1,0:T(8,128)(2,1)S(1)}, bf16[96,1024]{1,0:T(8,128)(2,1)S(1)}, u32[]{:S(2)}, u32[]{:S(2)}) %collective-permute-start.32) | collective-permute-done | bytes 196640 | tf_op jit(solution)/shard_map/ppermute | solution.py:44
  163.6 2.1 collective-permute-start.35
  166.6 2.1 collective-permute-done.37
  170.0 4.2 %collective-permute-done.35 = bf16[96,1024]{1,0:T(8,128)(2,1)} collective-permute-done((bf16[96,1024]{1,0:T(8,128)(2,1)S(1)}, bf16[96,1024]{1,0:T(8,128)(2,1)}, u32[]{:S(2)}, u32[]{:S(2)}) %collective-permute-start.35) | collective-permute-done | bytes 196640 | tf_op jit(solution)/shard_map/ppermute | solution.py:44
  175.4 1.9 fusion.247
  178.4 2.3 collective-permute-start.41
  183.2 1.8 fusion.248
  188.8 1.8 collective-permute-done.46
  190.6 3.3 collective-permute-done.45
  194.3 1.5 collective-permute-start.49
  198.5 7.7 %collective-permute-start.66 = (bf16[256,512]{1,0:T(8,128)(2,1)S(1)}, bf16[256,512]{1,0:T(8,128)(2,1)S(1)}, u32[]{:S(2)}, u32[]{:S(2)}) collective-permute-start(bf16[256,512]{1,0:T(8,128)(2,1)S(1)} %convert_add_fusion.1), channel_id=1, source_target_pairs={{0,16},{2,18},{4,20},{6,22},{8,24},{10,26},{12,28},{14,30},{16,0},... | collective-permute-start | bytes 786440 | tf_op jit(solution)/shard_map/ppermute | solution.py:62
  207.4 2.3 multiply_convert_fusion.1
  213.8 3.3 fusion.249
  222.6 2.4 collective-permute-done.51
  225.5 1.5 collective-permute-start.55
  228.7 7.2 %collective-permute-start.69 = (bf16[256,768]{1,0:T(8,128)(2,1)S(1)}, bf16[256,768]{1,0:T(8,128)(2,1)S(1)}, u32[]{:S(2)}, u32[]{:S(2)}) collective-permute-start(bf16[256,768]{1,0:T(8,128)(2,1)S(1)} %convolution_add_fusion.2), channel_id=1, source_target_pairs={{0,16},{2,18},{4,20},{6,22},{8,24},{10,26},{12,28},{14,30},{16,0},... | collective-permute-start | bytes 1179656 | tf_op jit(solution)/shard_map/ppermute | solution.py:62
  237.3 4.4 %collective-permute-done.54 = bf16[96,1024]{1,0:T(8,128)(2,1)S(1)} collective-permute-done((bf16[96,1024]{1,0:T(8,128)(2,1)S(1)}, bf16[96,1024]{1,0:T(8,128)(2,1)S(1)}, u32[]{:S(2)}, u32[]{:S(2)}) %collective-permute-start.54) | collective-permute-done | bytes 196640 | tf_op jit(solution)/shard_map/ppermute | solution.py:44
  244.2 9.9 %collective-permute-start.56 = (bf16[384,512]{1,0:T(8,128)(2,1)S(1)}, bf16[384,512]{1,0:T(8,128)(2,1)S(1)}, u32[]{:S(2)}, u32[]{:S(2)}) collective-permute-start(bf16[384,512]{1,0:T(8,128)(2,1)S(1)} %pad_maximum_fusion.24), channel_id=1, source_target_pairs={{0,1},{1,0},{2,3},{3,2},{4,5},{5,4},{6,7},{7,6},{8,9},{9,8},{10,11... | collective-permute-start | bytes 1179656 | tf_op jit(solution)/shard_map/ppermute | solution.py:39
  255.6 1.5 convolution_add_fusion
  259.9 1.5 copy-done.5
  262.7 2.7 collective-permute-start.75
  267.9 1.8 fusion.229
  271.0 8.8 %collective-permute-done.75 = bf16[96,1024]{1,0:T(8,128)(2,1)S(1)} collective-permute-done((bf16[96,1024]{1,0:T(8,128)(2,1)S(1)}, bf16[96,1024]{1,0:T(8,128)(2,1)S(1)}, u32[]{:S(2)}, u32[]{:S(2)}) %collective-permute-start.75) | collective-permute-done | bytes 196640 | tf_op jit(solution)/shard_map/ppermute | solution.py:44
  280.9 3.1 collective-permute-done.74
  286.6 5.8 %all-to-all-start.2 = ((bf16[16,112,64]{1,2,0:T(8,128)(2,1)}), bf16[16,112,64]{1,2,0:T(8,128)(2,1)S(1)}, u32[]{:S(2)}, u32[]{:S(2)}) async-start(bf16[16,112,64]{1,2,0:T(8,128)(2,1)} %bitcast.118), calls=%async_computation.2 | async-start | bytes 524288 | tf_op jit(solution)/shard_map/all_to_all | solution.py:410
  292.5 1.7 convolution_convert_fusion.5
  296.3 2.0 maximum_add_fusion.1
  298.3 2.3 collective-permute-start.59
  301.7 1.7 collective-permute-start.76
  303.6 3.3 fusion.227
  314.0 2.5 multiply_reduce_fusion.13
  316.4 7.1 %collective-permute-done.59 = bf16[256,1024]{1,0:T(8,128)(2,1)} collective-permute-done((bf16[256,1024]{1,0:T(8,128)(2,1)}, bf16[256,1024]{1,0:T(8,128)(2,1)}, u32[]{:S(2)}, u32[]{:S(2)}) %collective-permute-start.59) | collective-permute-done | bytes 524320 | tf_op jit(solution)/shard_map/ppermute | solution.py:62
  323.5 2.2 fusion.67
  328.9 7.4 %all-to-all-start.3 = ((f32[32,1,128]{2,1,0:T(1,128)}), f32[32,1,128]{2,1,0:T(1,128)S(1)}, u32[]{:S(2)}, u32[]{:S(2)}) async-start(f32[32,1,128]{2,1,0:T(1,128)} %broadcast_in_dim.92), calls=%async_computation.3 | async-start | bytes 32768 | tf_op jit(solution)/shard_map/all_to_all | solution.py:430
  339.6 3.3 all-to-all-done.3
  347.6 2.2 multiply_subtract_fusion.4
  351.7 2.7 collective-permute-done.60
  355.4 1.5 collective-permute-start.63
  360.3 1.8 multiply_subtract_fusion.1
  364.9 7.5 %multiply_subtract_fusion = (f32[2,64,2,1408]{3,2,1,0:T(2,128)}, f32[2,64,2,1408]{3,2,1,0:T(2,128)}, f32[2,64,2,1408]{3,2,1,0:T(2,128)}) fusion(f32[2,64,2,1408]{3,2,1,0:T(2,128)S(1)} %copy-done, f32[]{:T(128)S(6)} %min.3, bf16[2,64,1,1408]{3,2,1,0:T(2,128)(2,1)S(1)} %copy.324, bf16[2,64,1,1408]{3,2,1,0:T(2,128)(2,1)S(1)} %copy.323, ...), kind=kLoop, calls=%fused_computation.27 | loop fusion | flops 6848512 | bytes 9371652 | tf_op jit(solution)/shard_map/sub | solution.py:184
  372.4 1.7 multiply_subtract_fusion.2
  (503 shorter events, 121.5 us)
Async XLA Ops:
  3.8 15.5 %collective-permute-start = (bf16[2,64,1024]{2,1,0:T(8,128)(2,1)}, bf16[2,64,1024]{2,1,0:T(8,128)(2,1)}, u32[]{:S(2)}, u32[]{:S(2)}) collective-permute-start(bf16[2,64,1024]{2,1,0:T(8,128)(2,1)} %pad_maximum_fusion.29), channel_id=1, source_target_pairs={{0,1},{1,0},{2,3},{3,2},{4,5},{5,4},{6,7},{7,6},{8,9},{9,8},{10,11... | collective-permute-start | bytes 786440 | tf_op jit(solution)/shard_map/ppermute | solution.py:39
  4.9 14.4 %all-to-all-start = ((f32[16,1,672]{2,1,0:T(1,128)}), f32[16,1,672]{2,1,0:T(1,128)S(1)}, u32[]{:S(2)}, u32[]{:S(2)}) async-start(f32[16,1,672]{2,1,0:T(1,128)} %broadcast_in_dim.83), calls=%async_computation | async-start | bytes 98304 | tf_op jit(solution)/shard_map/all_to_all | solution.py:235
  13.9 14.1 %collective-permute-start.18 = (bf16[2,64,1280]{2,1,0:T(8,128)(2,1)}, bf16[2,64,1280]{2,1,0:T(8,128)(2,1)}, u32[]{:S(2)}, u32[]{:S(2)}) collective-permute-start(bf16[2,64,1280]{2,1,0:T(8,128)(2,1)} %maximum_maximum_fusion), channel_id=1, source_target_pairs={{0,1},{1,0},{2,3},{3,2},{4,5},{5,4},{6,7},{7,6},{8,9},{9,8},{10,11... | collective-permute-start | bytes 983048 | tf_op jit(solution)/shard_map/ppermute | solution.py:39
  16.6 15.8 %collective-permute-start.19 = (bf16[2,64,1536]{2,1,0:T(8,128)(2,1)}, bf16[2,64,1536]{2,1,0:T(8,128)(2,1)}, u32[]{:S(2)}, u32[]{:S(2)}) collective-permute-start(bf16[2,64,1536]{2,1,0:T(8,128)(2,1)} %pad_maximum_fusion.23), channel_id=1, source_target_pairs={{0,1},{1,0},{2,3},{3,2},{4,5},{5,4},{6,7},{7,6},{8,9},{9,8},{10,11... | collective-permute-start | bytes 1179656 | tf_op jit(solution)/shard_map/ppermute | solution.py:39
  21.3 13.5 %collective-permute-start.6 = (bf16[64,1024]{1,0:T(8,128)(2,1)}, bf16[64,1024]{1,0:T(8,128)(2,1)}, u32[]{:S(2)}, u32[]{:S(2)}) collective-permute-start(bf16[64,1024]{1,0:T(8,128)(2,1)} %get-tuple-element.246), channel_id=1, source_target_pairs={{0,8},{2,10},{4,12},{6,14},{8,0},{10,2},{12,4},{14,6},{16,24},{18,... | collective-permute-start | bytes 393224 | tf_op jit(solution)/shard_map/ppermute | solution.py:44
  22.0 14.1 %collective-permute-start.7 = (bf16[64,1024]{1,0:T(8,128)(2,1)}, bf16[64,1024]{1,0:T(8,128)(2,1)}, u32[]{:S(2)}, u32[]{:S(2)}) collective-permute-start(bf16[64,1024]{1,0:T(8,128)(2,1)} %get-tuple-element.245), channel_id=1, source_target_pairs={{0,10},{2,8},{4,14},{6,12},{8,2},{10,0},{12,6},{14,4},{16,26},{18,... | collective-permute-start | bytes 393224 | tf_op jit(solution)/shard_map/ppermute | solution.py:44
  23.2 13.9 %collective-permute-start.5 = (bf16[64,1024]{1,0:T(8,128)(2,1)}, bf16[64,1024]{1,0:T(8,128)(2,1)}, u32[]{:S(2)}, u32[]{:S(2)}) collective-permute-start(bf16[64,1024]{1,0:T(8,128)(2,1)} %get-tuple-element.244), channel_id=1, source_target_pairs={{0,2},{2,0},{4,6},{6,4},{8,10},{10,8},{12,14},{14,12},{16,18},{18,... | collective-permute-start | bytes 393224 | tf_op jit(solution)/shard_map/ppermute | solution.py:44
  28.0 10.8 %collective-permute-start.1 = (bf16[1536,64]{0,1:T(8,128)(2,1)S(1)}, bf16[1536,64]{0,1:T(8,128)(2,1)S(1)}, u32[]{:S(2)}, u32[]{:S(2)}) collective-permute-start(bf16[1536,64]{0,1:T(8,128)(2,1)S(1)} %fusion.11), channel_id=1, source_target_pairs={{0,1},{1,0},{2,3},{3,2},{4,5},{5,4},{6,7},{7,6},{8,9},{9,8},{10,11... | collective-permute-start | bytes 589832 | tf_op jit(solution)/shard_map/ppermute | solution.py:39
  34.5 10.6 %collective-permute-start.21 = (bf16[64,1536]{1,0:T(8,128)(2,1)}, bf16[64,1536]{1,0:T(8,128)(2,1)}, u32[]{:S(2)}, u32[]{:S(2)}) collective-permute-start(bf16[64,1536]{1,0:T(8,128)(2,1)} %get-tuple-element.223), channel_id=1, source_target_pairs={{0,8},{2,10},{4,12},{6,14},{8,0},{10,2},{12,4},{14,6},{16,24},{18,... | collective-permute-start | bytes 589832 | tf_op jit(solution)/shard_map/ppermute | solution.py:44
  34.8 15.6 %collective-permute-start.22 = (bf16[64,1536]{1,0:T(8,128)(2,1)}, bf16[64,1536]{1,0:T(8,128)(2,1)}, u32[]{:S(2)}, u32[]{:S(2)}) collective-permute-start(bf16[64,1536]{1,0:T(8,128)(2,1)} %get-tuple-element.222), channel_id=1, source_target_pairs={{0,10},{2,8},{4,14},{6,12},{8,2},{10,0},{12,6},{14,4},{16,26},{18,... | collective-permute-start | bytes 589832 | tf_op jit(solution)/shard_map/ppermute | solution.py:44
  36.1 14.2 %collective-permute-start.20 = (bf16[64,1536]{1,0:T(8,128)(2,1)}, bf16[64,1536]{1,0:T(8,128)(2,1)}, u32[]{:S(2)}, u32[]{:S(2)}) collective-permute-start(bf16[64,1536]{1,0:T(8,128)(2,1)} %get-tuple-element.221), channel_id=1, source_target_pairs={{0,2},{2,0},{4,6},{6,4},{8,10},{10,8},{12,14},{14,12},{16,18},{18,... | collective-permute-start | bytes 589832 | tf_op jit(solution)/shard_map/ppermute | solution.py:44
  38.3 30.6 %collective-permute-start.8 = (bf16[256,1024]{1,0:T(8,128)(2,1)S(1)}, bf16[256,1024]{1,0:T(8,128)(2,1)}, u32[]{:S(2)}, u32[]{:S(2)}) collective-permute-start(bf16[256,1024]{1,0:T(8,128)(2,1)S(1)} %bitcast.413), channel_id=1, source_target_pairs={{0,16},{2,18},{4,20},{6,22},{8,24},{10,26},{12,28},{14,30},{16,0},... | collective-permute-start | bytes 1572872 | tf_op jit(solution)/shard_map/ppermute | solution.py:57
  38.8 34.6 %collective-permute-start.9 = (bf16[256,1024]{1,0:T(8,128)(2,1)S(1)}, bf16[256,1024]{1,0:T(8,128)(2,1)}, u32[]{:S(2)}, u32[]{:S(2)}) collective-permute-start(bf16[256,1024]{1,0:T(8,128)(2,1)S(1)} %bitcast.414), channel_id=1, source_target_pairs={{0,4},{2,6},{4,0},{6,2},{8,12},{10,14},{12,8},{14,10},{16,20},{18,... | collective-permute-start | bytes 1572872 | tf_op jit(solution)/shard_map/ppermute | solution.py:44
  40.9 26.8 %all-to-all-start.1 = ((bf16[16,96,64]{1,2,0:T(8,128)(2,1)}), bf16[16,96,64]{1,2,0:T(8,128)(2,1)S(1)}, u32[]{:S(2)}, u32[]{:S(2)}) async-start(bf16[16,96,64]{1,2,0:T(8,128)(2,1)} %copy.296), calls=%async_computation.1 | async-start | bytes 524288 | tf_op jit(solution)/shard_map/all_to_all | solution.py:261
  68.9 11.3 %collective-permute-start.10 = (bf16[256,1024]{1,0:T(8,128)(2,1)}, bf16[256,1024]{1,0:T(8,128)(2,1)S(1)}, u32[]{:S(2)}, u32[]{:S(2)}) collective-permute-start(bf16[256,1024]{1,0:T(8,128)(2,1)} %collective-permute-done.8), channel_id=1, source_target_pairs={{0,4},{2,6},{4,0},{6,2},{8,12},{10,14},{12,8},{14,10},{16,20},{18,... | collective-permute-start | bytes 1572872 | tf_op jit(solution)/shard_map/ppermute | solution.py:44
  70.6 12.6 %collective-permute-start.4 = (bf16[96,1024]{1,0:T(8,128)(2,1)S(1)}, bf16[96,1024]{1,0:T(8,128)(2,1)S(1)}, u32[]{:S(2)}, u32[]{:S(2)}) collective-permute-start(bf16[96,1024]{1,0:T(8,128)(2,1)S(1)} %multiply_convert_fusion.7), channel_id=1, source_target_pairs={{0,10},{2,8},{4,14},{6,12},{8,2},{10,0},{12,6},{14,4},{16,26},{18,... | collective-permute-start | bytes 589832 | tf_op jit(solution)/shard_map/ppermute | solution.py:44
  72.4 12.4 %collective-permute-start.3 = (bf16[96,1024]{1,0:T(8,128)(2,1)S(1)}, bf16[96,1024]{1,0:T(8,128)(2,1)S(1)}, u32[]{:S(2)}, u32[]{:S(2)}) collective-permute-start(bf16[96,1024]{1,0:T(8,128)(2,1)S(1)} %multiply_convert_fusion.7), channel_id=1, source_target_pairs={{0,8},{2,10},{4,12},{6,14},{8,0},{10,2},{12,4},{14,6},{16,24},{18,... | collective-permute-start | bytes 589832 | tf_op jit(solution)/shard_map/ppermute | solution.py:44
  72.9 12.7 %collective-permute-start.2 = (bf16[96,1024]{1,0:T(8,128)(2,1)S(1)}, bf16[96,1024]{1,0:T(8,128)(2,1)S(1)}, u32[]{:S(2)}, u32[]{:S(2)}) collective-permute-start(bf16[96,1024]{1,0:T(8,128)(2,1)S(1)} %multiply_convert_fusion.7), channel_id=1, source_target_pairs={{0,2},{2,0},{4,6},{6,4},{8,10},{10,8},{12,14},{14,12},{16,18},{18,... | collective-permute-start | bytes 589832 | tf_op jit(solution)/shard_map/ppermute | solution.py:44
  73.4 38.3 %collective-permute-start.28 = (bf16[256,1536]{1,0:T(8,128)(2,1)}, bf16[256,1536]{1,0:T(8,128)(2,1)}, u32[]{:S(2)}, u32[]{:S(2)}) collective-permute-start(bf16[256,1536]{1,0:T(8,128)(2,1)} %bitcast.84), channel_id=1, source_target_pairs={{0,16},{2,18},{4,20},{6,22},{8,24},{10,26},{12,28},{14,30},{16,0},... | collective-permute-start | bytes 2359304 | tf_op jit(solution)/shard_map/ppermute | solution.py:57
  80.2 61.2 %collective-permute-start.29 = (bf16[256,1536]{1,0:T(8,128)(2,1)}, bf16[256,1536]{1,0:T(8,128)(2,1)}, u32[]{:S(2)}, u32[]{:S(2)}) collective-permute-start(bf16[256,1536]{1,0:T(8,128)(2,1)} %bitcast.84), channel_id=1, source_target_pairs={{0,4},{2,6},{4,0},{6,2},{8,12},{10,14},{12,8},{14,10},{16,20},{18,... | collective-permute-start | bytes 2359304 | tf_op jit(solution)/shard_map/ppermute | solution.py:44
  83.3 15.7 %collective-permute-start.24 = (bf16[64,1280]{1,0:T(8,128)(2,1)S(1)}, bf16[64,1280]{1,0:T(8,128)(2,1)S(1)}, u32[]{:S(2)}, u32[]{:S(2)}) collective-permute-start(bf16[64,1280]{1,0:T(8,128)(2,1)S(1)} %get-tuple-element.238), channel_id=1, source_target_pairs={{0,8},{2,10},{4,12},{6,14},{8,0},{10,2},{12,4},{14,6},{16,24},{18,... | collective-permute-start | bytes 491528 | tf_op jit(solution)/shard_map/ppermute | solution.py:44
  84.8 19.1 %collective-permute-start.25 = (bf16[64,1280]{1,0:T(8,128)(2,1)S(1)}, bf16[64,1280]{1,0:T(8,128)(2,1)S(1)}, u32[]{:S(2)}, u32[]{:S(2)}) collective-permute-start(bf16[64,1280]{1,0:T(8,128)(2,1)S(1)} %get-tuple-element.237), channel_id=1, source_target_pairs={{0,10},{2,8},{4,14},{6,12},{8,2},{10,0},{12,6},{14,4},{16,26},{18,... | collective-permute-start | bytes 491528 | tf_op jit(solution)/shard_map/ppermute | solution.py:44
  85.6 18.4 %collective-permute-start.23 = (bf16[64,1280]{1,0:T(8,128)(2,1)S(1)}, bf16[64,1280]{1,0:T(8,128)(2,1)S(1)}, u32[]{:S(2)}, u32[]{:S(2)}) collective-permute-start(bf16[64,1280]{1,0:T(8,128)(2,1)S(1)} %get-tuple-element.236), channel_id=1, source_target_pairs={{0,2},{2,0},{4,6},{6,4},{8,10},{10,8},{12,14},{14,12},{16,18},{18,... | collective-permute-start | bytes 491528 | tf_op jit(solution)/shard_map/ppermute | solution.py:44
  109.8 12.7 %collective-permute-start.13 = (bf16[96,1024]{1,0:T(8,128)(2,1)S(1)}, bf16[96,1024]{1,0:T(8,128)(2,1)S(1)}, u32[]{:S(2)}, u32[]{:S(2)}) collective-permute-start(bf16[96,1024]{1,0:T(8,128)(2,1)S(1)} %get-tuple-element.226), channel_id=1, source_target_pairs={{0,8},{2,10},{4,12},{6,14},{8,0},{10,2},{12,4},{14,6},{16,24},{18,... | collective-permute-start | bytes 589832 | tf_op jit(solution)/shard_map/ppermute | solution.py:44
  109.8 12.7 %collective-permute-start.12 = (bf16[96,1024]{1,0:T(8,128)(2,1)S(1)}, bf16[96,1024]{1,0:T(8,128)(2,1)S(1)}, u32[]{:S(2)}, u32[]{:S(2)}) collective-permute-start(bf16[96,1024]{1,0:T(8,128)(2,1)S(1)} %get-tuple-element.224), channel_id=1, source_target_pairs={{0,2},{2,0},{4,6},{6,4},{8,10},{10,8},{12,14},{14,12},{16,18},{18,... | collective-permute-start | bytes 589832 | tf_op jit(solution)/shard_map/ppermute | solution.py:44
  111.7 18.2 %collective-permute-start.26 = (bf16[256,768]{1,0:T(8,128)(2,1)}, bf16[256,768]{1,0:T(8,128)(2,1)}, u32[]{:S(2)}, u32[]{:S(2)}) collective-permute-start(bf16[256,768]{1,0:T(8,128)(2,1)} %bitcast.83), channel_id=1, source_target_pairs={{0,16},{2,18},{4,20},{6,22},{8,24},{10,26},{12,28},{14,30},{16,0},... | collective-permute-start | bytes 1179656 | tf_op jit(solution)/shard_map/ppermute | solution.py:57
  114.2 27.2 %collective-permute-start.30 = (bf16[256,1536]{1,0:T(8,128)(2,1)}, bf16[256,1536]{1,0:T(8,128)(2,1)}, u32[]{:S(2)}, u32[]{:S(2)}) collective-permute-start(bf16[256,1536]{1,0:T(8,128)(2,1)} %collective-permute-done.28), channel_id=1, source_target_pairs={{0,4},{2,6},{4,0},{6,2},{8,12},{10,14},{12,8},{14,10},{16,20},{18,... | collective-permute-start | bytes 2359304 | tf_op jit(solution)/shard_map/ppermute | solution.py:44
  129.9 11.5 %collective-permute-start.27 = (bf16[256,768]{1,0:T(8,128)(2,1)}, bf16[256,768]{1,0:T(8,128)(2,1)}, u32[]{:S(2)}, u32[]{:S(2)}) collective-permute-start(bf16[256,768]{1,0:T(8,128)(2,1)} %collective-permute-done.26), channel_id=1, source_target_pairs={{0,4},{2,6},{4,0},{6,2},{8,12},{10,14},{12,8},{14,10},{16,20},{18,... | collective-permute-start | bytes 1179656 | tf_op jit(solution)/shard_map/ppermute | solution.py:44
  137.7 12.1 %collective-permute-start.31 = (bf16[256,768]{1,0:T(8,128)(2,1)}, bf16[256,768]{1,0:T(8,128)(2,1)S(1)}, u32[]{:S(2)}, u32[]{:S(2)}) collective-permute-start(bf16[256,768]{1,0:T(8,128)(2,1)} %bitcast.83), channel_id=1, source_target_pairs={{0,4},{2,6},{4,0},{6,2},{8,12},{10,14},{12,8},{14,10},{16,20},{18,... | collective-permute-start | bytes 1179656 | tf_op jit(solution)/shard_map/ppermute | solution.py:44
  138.6 16.4 %collective-permute-start.38 = (bf16[256,512]{1,0:T(8,128)(2,1)}, bf16[256,512]{1,0:T(8,128)(2,1)}, u32[]{:S(2)}, u32[]{:S(2)}) collective-permute-start(bf16[256,512]{1,0:T(8,128)(2,1)} %bitcast.86), channel_id=1, source_target_pairs={{0,16},{2,18},{4,20},{6,22},{8,24},{10,26},{12,28},{14,30},{16,0},... | collective-permute-start | bytes 786440 | tf_op jit(solution)/shard_map/ppermute | solution.py:57
  152.2 10.4 %collective-permute-start.32 = (bf16[96,1024]{1,0:T(8,128)(2,1)S(1)}, bf16[96,1024]{1,0:T(8,128)(2,1)S(1)}, u32[]{:S(2)}, u32[]{:S(2)}) collective-permute-start(bf16[96,1024]{1,0:T(8,128)(2,1)S(1)} %get-tuple-element.218), channel_id=1, source_target_pairs={{0,2},{2,0},{4,6},{6,4},{8,10},{10,8},{12,14},{14,12},{16,18},{18,... | collective-permute-start | bytes 589832 | tf_op jit(solution)/shard_map/ppermute | solution.py:44
  154.9 20.5 %collective-permute-start.39 = (bf16[256,512]{1,0:T(8,128)(2,1)}, bf16[256,512]{1,0:T(8,128)(2,1)}, u32[]{:S(2)}, u32[]{:S(2)}) collective-permute-start(bf16[256,512]{1,0:T(8,128)(2,1)} %bitcast.86), channel_id=1, source_target_pairs={{0,4},{2,6},{4,0},{6,2},{8,12},{10,14},{12,8},{14,10},{16,20},{18,... | collective-permute-start | bytes 786440 | tf_op jit(solution)/shard_map/ppermute | solution.py:44
  155.0 20.4 %collective-permute-start.40 = (bf16[256,512]{1,0:T(8,128)(2,1)}, bf16[256,512]{1,0:T(8,128)(2,1)}, u32[]{:S(2)}, u32[]{:S(2)}) collective-permute-start(bf16[256,512]{1,0:T(8,128)(2,1)} %collective-permute-done.38), channel_id=1, source_target_pairs={{0,4},{2,6},{4,0},{6,2},{8,12},{10,14},{12,8},{14,10},{16,20},{18,... | collective-permute-start | bytes 786440 | tf_op jit(solution)/shard_map/ppermute | solution.py:44
  163.6 10.6 %collective-permute-start.35 = (bf16[96,1024]{1,0:T(8,128)(2,1)S(1)}, bf16[96,1024]{1,0:T(8,128)(2,1)}, u32[]{:S(2)}, u32[]{:S(2)}) collective-permute-start(bf16[96,1024]{1,0:T(8,128)(2,1)S(1)} %multiply_convert_fusion.5), channel_id=1, source_target_pairs={{0,2},{2,0},{4,6},{6,4},{8,10},{10,8},{12,14},{14,12},{16,18},{18,... | collective-permute-start | bytes 589832 | tf_op jit(solution)/shard_map/ppermute | solution.py:44
  188.1 10.3 %collective-permute-start.64 = (bf16[256,512]{1,0:T(8,128)(2,1)S(1)}, bf16[256,512]{1,0:T(8,128)(2,1)S(1)}, u32[]{:S(2)}, u32[]{:S(2)}) collective-permute-start(bf16[256,512]{1,0:T(8,128)(2,1)S(1)} %fusion.92), channel_id=1, source_target_pairs={{0,4},{2,6},{4,0},{6,2},{8,12},{10,14},{12,8},{14,10},{16,20},{18,... | collective-permute-start | bytes 786440 | tf_op jit(solution)/shard_map/ppermute | solution.py:44
  194.3 13.1 %collective-permute-start.49 = (bf16[96,1024]{1,0:T(8,128)(2,1)S(1)}, bf16[96,1024]{1,0:T(8,128)(2,1)S(1)}, u32[]{:S(2)}, u32[]{:S(2)}) collective-permute-start(bf16[96,1024]{1,0:T(8,128)(2,1)S(1)} %fusion.211), channel_id=1, source_target_pairs={{0,10},{2,8},{4,14},{6,12},{8,2},{10,0},{12,6},{14,4},{16,26},{18,... | collective-permute-start | bytes 589832 | tf_op jit(solution)/shard_map/ppermute | solution.py:44
  195.8 11.6 %collective-permute-start.48 = (bf16[96,1024]{1,0:T(8,128)(2,1)S(1)}, bf16[96,1024]{1,0:T(8,128)(2,1)S(1)}, u32[]{:S(2)}, u32[]{:S(2)}) collective-permute-start(bf16[96,1024]{1,0:T(8,128)(2,1)S(1)} %fusion.211), channel_id=1, source_target_pairs={{0,8},{2,10},{4,12},{6,14},{8,0},{10,2},{12,4},{14,6},{16,24},{18,... | collective-permute-start | bytes 589832 | tf_op jit(solution)/shard_map/ppermute | solution.py:44
  197.3 10.1 %collective-permute-start.47 = (bf16[96,1024]{1,0:T(8,128)(2,1)S(1)}, bf16[96,1024]{1,0:T(8,128)(2,1)S(1)}, u32[]{:S(2)}, u32[]{:S(2)}) collective-permute-start(bf16[96,1024]{1,0:T(8,128)(2,1)S(1)} %fusion.211), channel_id=1, source_target_pairs={{0,2},{2,0},{4,6},{6,4},{8,10},{10,8},{12,14},{14,12},{16,18},{18,... | collective-permute-start | bytes 589832 | tf_op jit(solution)/shard_map/ppermute | solution.py:44
  198.5 20.3 %collective-permute-start.66 = (bf16[256,512]{1,0:T(8,128)(2,1)S(1)}, bf16[256,512]{1,0:T(8,128)(2,1)S(1)}, u32[]{:S(2)}, u32[]{:S(2)}) collective-permute-start(bf16[256,512]{1,0:T(8,128)(2,1)S(1)} %convert_add_fusion.1), channel_id=1, source_target_pairs={{0,16},{2,18},{4,20},{6,22},{8,24},{10,26},{12,28},{14,30},{16,0},... | collective-permute-start | bytes 786440 | tf_op jit(solution)/shard_map/ppermute | solution.py:62
  206.2 13.8 %collective-permute-start.65 = (bf16[256,512]{1,0:T(8,128)(2,1)S(1)}, bf16[256,512]{1,0:T(8,128)(2,1)S(1)}, u32[]{:S(2)}, u32[]{:S(2)}) collective-permute-start(bf16[256,512]{1,0:T(8,128)(2,1)S(1)} %fusion.94), channel_id=1, source_target_pairs={{0,4},{2,6},{4,0},{6,2},{8,12},{10,14},{12,8},{14,10},{16,20},{18,... | collective-permute-start | bytes 786440 | tf_op jit(solution)/shard_map/ppermute | solution.py:44
  212.3 16.0 %collective-permute-start.67 = (bf16[256,768]{1,0:T(8,128)(2,1)S(1)}, bf16[256,768]{1,0:T(8,128)(2,1)S(1)}, u32[]{:S(2)}, u32[]{:S(2)}) collective-permute-start(bf16[256,768]{1,0:T(8,128)(2,1)S(1)} %convolution_convert_fusion.2), channel_id=1, source_target_pairs={{0,4},{2,6},{4,0},{6,2},{8,12},{10,14},{12,8},{14,10},{16,20},{18,... | collective-permute-start | bytes 1179656 | tf_op jit(solution)/shard_map/ppermute | solution.py:44
  212.7 42.9 %collective-permute-start.70 = (bf16[256,1536]{1,0:T(8,128)(2,1)S(1)}, bf16[256,1536]{1,0:T(8,128)(2,1)S(1)}, u32[]{:S(2)}, u32[]{:S(2)}) collective-permute-start(bf16[256,1536]{1,0:T(8,128)(2,1)S(1)} %convolution_convert_fusion), channel_id=1, source_target_pairs={{0,4},{2,6},{4,0},{6,2},{8,12},{10,14},{12,8},{14,10},{16,20},{18,... | collective-permute-start | bytes 2359304 | tf_op jit(solution)/shard_map/ppermute | solution.py:44
  225.5 10.4 %collective-permute-start.55 = (bf16[96,1024]{1,0:T(8,128)(2,1)S(1)}, bf16[96,1024]{1,0:T(8,128)(2,1)S(1)}, u32[]{:S(2)}, u32[]{:S(2)}) collective-permute-start(bf16[96,1024]{1,0:T(8,128)(2,1)S(1)} %get-tuple-element.159), channel_id=1, source_target_pairs={{0,10},{2,8},{4,14},{6,12},{8,2},{10,0},{12,6},{14,4},{16,26},{18,... | collective-permute-start | bytes 589832 | tf_op jit(solution)/shard_map/ppermute | solution.py:44
  227.1 14.7 %collective-permute-start.54 = (bf16[96,1024]{1,0:T(8,128)(2,1)S(1)}, bf16[96,1024]{1,0:T(8,128)(2,1)S(1)}, u32[]{:S(2)}, u32[]{:S(2)}) collective-permute-start(bf16[96,1024]{1,0:T(8,128)(2,1)S(1)} %get-tuple-element.159), channel_id=1, source_target_pairs={{0,8},{2,10},{4,12},{6,14},{8,0},{10,2},{12,4},{14,6},{16,24},{18,... | collective-permute-start | bytes 589832 | tf_op jit(solution)/shard_map/ppermute | solution.py:44
  228.0 13.8 %collective-permute-start.53 = (bf16[96,1024]{1,0:T(8,128)(2,1)S(1)}, bf16[96,1024]{1,0:T(8,128)(2,1)S(1)}, u32[]{:S(2)}, u32[]{:S(2)}) collective-permute-start(bf16[96,1024]{1,0:T(8,128)(2,1)S(1)} %get-tuple-element.159), channel_id=1, source_target_pairs={{0,2},{2,0},{4,6},{6,4},{8,10},{10,8},{12,14},{14,12},{16,18},{18,... | collective-permute-start | bytes 589832 | tf_op jit(solution)/shard_map/ppermute | solution.py:44
  228.7 38.8 %collective-permute-start.69 = (bf16[256,768]{1,0:T(8,128)(2,1)S(1)}, bf16[256,768]{1,0:T(8,128)(2,1)S(1)}, u32[]{:S(2)}, u32[]{:S(2)}) collective-permute-start(bf16[256,768]{1,0:T(8,128)(2,1)S(1)} %convolution_add_fusion.2), channel_id=1, source_target_pairs={{0,16},{2,18},{4,20},{6,22},{8,24},{10,26},{12,28},{14,30},{16,0},... | collective-permute-start | bytes 1179656 | tf_op jit(solution)/shard_map/ppermute | solution.py:62
  235.9 31.6 %collective-permute-start.68 = (bf16[256,768]{1,0:T(8,128)(2,1)S(1)}, bf16[256,768]{1,0:T(8,128)(2,1)S(1)}, u32[]{:S(2)}, u32[]{:S(2)}) collective-permute-start(bf16[256,768]{1,0:T(8,128)(2,1)S(1)} %convolution_convert_fusion.3), channel_id=1, source_target_pairs={{0,4},{2,6},{4,0},{6,2},{8,12},{10,14},{12,8},{14,10},{16,20},{18,... | collective-permute-start | bytes 1179656 | tf_op jit(solution)/shard_map/ppermute | solution.py:44
  244.2 15.3 %collective-permute-start.56 = (bf16[384,512]{1,0:T(8,128)(2,1)S(1)}, bf16[384,512]{1,0:T(8,128)(2,1)S(1)}, u32[]{:S(2)}, u32[]{:S(2)}) collective-permute-start(bf16[384,512]{1,0:T(8,128)(2,1)S(1)} %pad_maximum_fusion.24), channel_id=1, source_target_pairs={{0,1},{1,0},{2,3},{3,2},{4,5},{5,4},{6,7},{7,6},{8,9},{9,8},{10,11... | collective-permute-start | bytes 1179656 | tf_op jit(solution)/shard_map/ppermute | solution.py:39
  257.1 46.5 %collective-permute-start.72 = (bf16[256,1536]{1,0:T(8,128)(2,1)}, bf16[256,1536]{1,0:T(8,128)(2,1)}, u32[]{:S(2)}, u32[]{:S(2)}) collective-permute-start(bf16[256,1536]{1,0:T(8,128)(2,1)} %convolution_add_fusion), channel_id=1, source_target_pairs={{0,16},{2,18},{4,20},{6,22},{8,24},{10,26},{12,28},{14,30},{16,0},... | collective-permute-start | bytes 2359304 | tf_op jit(solution)/shard_map/ppermute | solution.py:62
  258.4 45.3 %collective-permute-start.71 = (bf16[256,1536]{1,0:T(8,128)(2,1)}, bf16[256,1536]{1,0:T(8,128)(2,1)}, u32[]{:S(2)}, u32[]{:S(2)}) collective-permute-start(bf16[256,1536]{1,0:T(8,128)(2,1)} %convolution_convert_fusion.1), channel_id=1, source_target_pairs={{0,4},{2,6},{4,0},{6,2},{8,12},{10,14},{12,8},{14,10},{16,20},{18,... | collective-permute-start | bytes 2359304 | tf_op jit(solution)/shard_map/ppermute | solution.py:44
  262.7 17.1 %collective-permute-start.75 = (bf16[96,1024]{1,0:T(8,128)(2,1)S(1)}, bf16[96,1024]{1,0:T(8,128)(2,1)S(1)}, u32[]{:S(2)}, u32[]{:S(2)}) collective-permute-start(bf16[96,1024]{1,0:T(8,128)(2,1)S(1)} %get-tuple-element.210), channel_id=1, source_target_pairs={{0,10},{2,8},{4,14},{6,12},{8,2},{10,0},{12,6},{14,4},{16,26},{18,... | collective-permute-start | bytes 589832 | tf_op jit(solution)/shard_map/ppermute | solution.py:44
  267.5 16.5 %collective-permute-start.74 = (bf16[96,1024]{1,0:T(8,128)(2,1)S(1)}, bf16[96,1024]{1,0:T(8,128)(2,1)S(1)}, u32[]{:S(2)}, u32[]{:S(2)}) collective-permute-start(bf16[96,1024]{1,0:T(8,128)(2,1)S(1)} %get-tuple-element.211), channel_id=1, source_target_pairs={{0,8},{2,10},{4,12},{6,14},{8,0},{10,2},{12,4},{14,6},{16,24},{18,... | collective-permute-start | bytes 589832 | tf_op jit(solution)/shard_map/ppermute | solution.py:44
  267.5 16.5 %collective-permute-start.73 = (bf16[96,1024]{1,0:T(8,128)(2,1)S(1)}, bf16[96,1024]{1,0:T(8,128)(2,1)S(1)}, u32[]{:S(2)}, u32[]{:S(2)}) collective-permute-start(bf16[96,1024]{1,0:T(8,128)(2,1)S(1)} %get-tuple-element.209), channel_id=1, source_target_pairs={{0,2},{2,0},{4,6},{6,4},{8,10},{10,8},{12,14},{14,12},{16,18},{18,... | collective-permute-start | bytes 589832 | tf_op jit(solution)/shard_map/ppermute | solution.py:44
  279.8 16.5 %collective-permute-start.57 = (bf16[256,1024]{1,0:T(8,128)(2,1)}, bf16[256,1024]{1,0:T(8,128)(2,1)}, u32[]{:S(2)}, u32[]{:S(2)}) collective-permute-start(bf16[256,1024]{1,0:T(8,128)(2,1)} %pad_maximum_fusion.21), channel_id=1, source_target_pairs={{0,4},{2,6},{4,0},{6,2},{8,12},{10,14},{12,8},{14,10},{16,20},{18,... | collective-permute-start | bytes 1572872 | tf_op jit(solution)/shard_map/ppermute | solution.py:44
  286.6 15.1 %all-to-all-start.2 = ((bf16[16,112,64]{1,2,0:T(8,128)(2,1)}), bf16[16,112,64]{1,2,0:T(8,128)(2,1)S(1)}, u32[]{:S(2)}, u32[]{:S(2)}) async-start(bf16[16,112,64]{1,2,0:T(8,128)(2,1)} %bitcast.118), calls=%async_computation.2 | async-start | bytes 524288 | tf_op jit(solution)/shard_map/all_to_all | solution.py:410
  298.3 25.2 %collective-permute-start.59 = (bf16[256,1024]{1,0:T(8,128)(2,1)}, bf16[256,1024]{1,0:T(8,128)(2,1)}, u32[]{:S(2)}, u32[]{:S(2)}) collective-permute-start(bf16[256,1024]{1,0:T(8,128)(2,1)} %maximum_add_fusion.1), channel_id=1, source_target_pairs={{0,16},{2,18},{4,20},{6,22},{8,24},{10,26},{12,28},{14,30},{16,0},... | collective-permute-start | bytes 1572872 | tf_op jit(solution)/shard_map/ppermute | solution.py:62
  300.5 23.0 %collective-permute-start.58 = (bf16[256,1024]{1,0:T(8,128)(2,1)}, bf16[256,1024]{1,0:T(8,128)(2,1)}, u32[]{:S(2)}, u32[]{:S(2)}) collective-permute-start(bf16[256,1024]{1,0:T(8,128)(2,1)} %pad_maximum_fusion.20), channel_id=1, source_target_pairs={{0,4},{2,6},{4,0},{6,2},{8,12},{10,14},{12,8},{14,10},{16,20},{18,... | collective-permute-start | bytes 1572872 | tf_op jit(solution)/shard_map/ppermute | solution.py:44
  301.7 9.4 %collective-permute-start.76 = (bf16[16,112,64]{1,2,0:T(8,128)(2,1)S(1)}, bf16[16,112,64]{1,2,0:T(8,128)(2,1)S(1)}, u32[]{:S(2)}, u32[]{:S(2)}) collective-permute-start(bf16[16,112,64]{1,2,0:T(8,128)(2,1)S(1)} %all-to-all-done.2), channel_id=1, source_target_pairs={{0,1},{1,0},{2,3},{3,2},{4,5},{5,4},{6,7},{7,6},{8,9},{9,8},{10,11... | collective-permute-start | bytes 688136 | tf_op jit(solution)/shard_map/ppermute | solution.py:39
  308.1 41.7 %collective-permute-start.78 = (bf16[64,2816]{1,0:T(8,128)(2,1)}, bf16[64,2816]{1,0:T(8,128)(2,1)}, u32[]{:S(2)}, u32[]{:S(2)}) collective-permute-start(bf16[64,2816]{1,0:T(8,128)(2,1)} %get-tuple-element.181), channel_id=1, source_target_pairs={{0,8},{2,10},{4,12},{6,14},{8,0},{10,2},{12,4},{14,6},{16,24},{18,... | collective-permute-start | bytes 1081352 | tf_op jit(solution)/shard_map/ppermute | solution.py:44
  309.3 40.9 %collective-permute-start.79 = (bf16[64,2816]{1,0:T(8,128)(2,1)}, bf16[64,2816]{1,0:T(8,128)(2,1)}, u32[]{:S(2)}, u32[]{:S(2)}) collective-permute-start(bf16[64,2816]{1,0:T(8,128)(2,1)} %get-tuple-element.180), channel_id=1, source_target_pairs={{0,10},{2,8},{4,14},{6,12},{8,2},{10,0},{12,6},{14,4},{16,26},{18,... | collective-permute-start | bytes 1081352 | tf_op jit(solution)/shard_map/ppermute | solution.py:44
  311.1 39.0 %collective-permute-start.77 = (bf16[64,2816]{1,0:T(8,128)(2,1)}, bf16[64,2816]{1,0:T(8,128)(2,1)}, u32[]{:S(2)}, u32[]{:S(2)}) collective-permute-start(bf16[64,2816]{1,0:T(8,128)(2,1)} %get-tuple-element.179), channel_id=1, source_target_pairs={{0,2},{2,0},{4,6},{6,4},{8,10},{10,8},{12,14},{14,12},{16,18},{18,... | collective-permute-start | bytes 1081352 | tf_op jit(solution)/shard_map/ppermute | solution.py:44
  328.9 14.1 %all-to-all-start.3 = ((f32[32,1,128]{2,1,0:T(1,128)}), f32[32,1,128]{2,1,0:T(1,128)S(1)}, u32[]{:S(2)}, u32[]{:S(2)}) async-start(f32[32,1,128]{2,1,0:T(1,128)} %broadcast_in_dim.92), calls=%async_computation.3 | async-start | bytes 32768 | tf_op jit(solution)/shard_map/all_to_all | solution.py:430
  337.1 14.6 %collective-permute-start.61 = (bf16[64,1024]{1,0:T(8,128)(2,1)}, bf16[64,1024]{1,0:T(8,128)(2,1)S(1)}, u32[]{:S(2)}, u32[]{:S(2)}) collective-permute-start(bf16[64,1024]{1,0:T(8,128)(2,1)} %get-tuple-element.241), channel_id=1, source_target_pairs={{0,8},{2,10},{4,12},{6,14},{8,0},{10,2},{12,4},{14,6},{16,24},{18,... | collective-permute-start | bytes 393224 | tf_op jit(solution)/shard_map/ppermute | solution.py:44
  338.5 13.2 %collective-permute-start.62 = (bf16[64,1024]{1,0:T(8,128)(2,1)}, bf16[64,1024]{1,0:T(8,128)(2,1)}, u32[]{:S(2)}, u32[]{:S(2)}) collective-permute-start(bf16[64,1024]{1,0:T(8,128)(2,1)} %get-tuple-element.240), channel_id=1, source_target_pairs={{0,10},{2,8},{4,14},{6,12},{8,2},{10,0},{12,6},{14,4},{16,26},{18,... | collective-permute-start | bytes 393224 | tf_op jit(solution)/shard_map/ppermute | solution.py:44
  (98 other events, 998.4 us)
